TPU v7x, 32 devices: a whole 2x2x4 slice. The times are simulated.
32 devices in a mesh: row: 4 (over z), col: 8 (over y, x, core).
Axes of the slice: x: 2, y: 2, z: 4, core: 2. Of those that a mesh axis runs over, the one named last changes fastest.
Arguments:
- gate_pre: bfloat16 [1024, 16384], P('row', 'col'), may hold values from -8 to 8
- up_pre: bfloat16 [1024, 16384], P('row', 'col'), may hold values from -6 to 6
- down_t: bfloat16 [4096, 16384], P('row', 'col'), may hold values from -0.09375 to 0.09375
- grad_out: bfloat16 [1024, 4096], P('row', 'col'), may hold values from -6 to 6
Outputs:
- gate_grad: bfloat16 [1024, 16384], P('row', 'col')
- up_grad: bfloat16 [1024, 16384], P('row', 'col')
- weight_grad: bfloat16 [4096, 16384], P('row', 'col')
All inputs are finite; a program needn't handle non-finite values.
Results may differ from a plain program's by a relative error of at most 0.0049.
Values may be sent and summed in bfloat16 or wider, within the bound.
No kernel may reach another device: no remote copies, remote signals or barrier semaphores. Data moves between devices by JAX's collectives and lax.ppermute only.
A program may use at most 128 MiB of HBM per device.

v0:
```python
import jax
import jax.numpy as jnp
from jax import lax
from jax.experimental import pallas as pl
from jax.experimental.pallas import tpu as pltpu
from jax.sharding import PartitionSpec as P


def after(value, first):
    return lax.optimization_barrier((value, first))[0]


def lay_strips(near, far):
    chips = len(near)
    rows, strip, width = near[0].shape

    def kernel(*refs):
        row, col = lax.axis_index("row"), lax.axis_index("col")
        out_ref = refs[-1]
        for at, ref in enumerate(refs[:-1]):
            core, chip = at // chips, at % chips
            lane = pl.multiple_of(((col & 1) ^ core) * width, width)
            for group in range(rows):
                slot = lax.rem((row ^ group) + rows - row, rows)
                start = (slot * chips + (col // 2 ^ chip)) * strip
                out_ref[pl.ds(pl.multiple_of(start, strip), strip), pl.ds(lane, width)] = ref[group]

    return pl.pallas_call(
        kernel,
        out_shape=jax.ShapeDtypeStruct((rows * chips * strip, 2 * width), near[0].dtype),
        in_specs=[pl.BlockSpec(memory_space=pltpu.VMEM)] * 2 * chips,
        out_specs=pl.BlockSpec(memory_space=pltpu.VMEM),
        compiler_params=pltpu.CompilerParams(vmem_limit_bytes=32 * 2**20),
        name="lay_strips",
    )(*near, *far)


def goes_ahead(way):
    return (lax.axis_index("col") & 1) == way


def ring(value, way):
    rows, cols = lax.axis_size("row"), lax.axis_size("col")
    pairs = []
    for row in range(rows):
        for col in range(cols):
            to = row + 1 if col & 1 == way else row - 1
            if 0 <= to < rows:
                pairs.append((row * cols + col, to * cols + col))
    return lax.ppermute(value, ("row", "col"), pairs)


def add_share(got, cot, down_t, way, step, first, tok_rows):
    span, width = got.shape
    tile = 512 if width % 512 == 0 else width

    def kernel(got_ref, cot_ref, down_ref, out_ref):
        rows, row, ahead = lax.axis_size("row"), lax.axis_index("row"), goes_ahead(way)
        is_sum = step > jnp.where(ahead, row + 1, rows - row)
        start = jnp.where(ahead, rows + 1 - step, step - 1) * tok_rows + first

        @pl.when(is_sum)
        def _():
            tokens = cot_ref[pl.ds(pl.multiple_of(start, 16), span), :]
            for at in range(0, width, tile):
                cut = slice(at, at + tile)
                share = jnp.dot(tokens, down_ref[:, cut], preferred_element_type=jnp.float32)
                out_ref[:, cut] = (got_ref[:, cut].astype(jnp.float32) + share).astype(out_ref.dtype)

        @pl.when(jnp.logical_not(is_sum))
        def _():
            out_ref[...] = got_ref[...]

    whole = pl.BlockSpec(memory_space=pltpu.VMEM)
    return pl.pallas_call(
        kernel,
        out_shape=jax.ShapeDtypeStruct(got.shape, got.dtype),
        in_specs=[whole] * 3,
        out_specs=whole,
        compiler_params=pltpu.CompilerParams(vmem_limit_bytes=32 * 2**20),
        cost_estimate=pl.CostEstimate(
            flops=2 * span * down_t.size, bytes_accessed=4 * span * width, transcendentals=0
        ),
        name="add_share",
    )(got, cot, down_t)


def weight_product(cot, own, ways, scale):
    rows = len(ways[0]) + 1
    tok_rows, width = own.shape
    tile = 512 if width % 512 == 0 else width
    flat = [piece for steps in ways for pieces in steps for piece in pieces]

    def kernel(cot_ref, own_ref, *refs):
        ends, (out_ref, hidden_ref) = iter(refs[: len(flat)]), refs[len(flat) :]
        way_refs = [[[next(ends) for _ in pieces] for pieces in steps] for steps in ways]
        row = lax.axis_index("row")

        def place(pieces, start, cut):
            for piece in pieces:
                hidden_ref[start : start + piece.shape[0], :] = piece[:, cut].astype(hidden_ref.dtype)
                start += piece.shape[0]

        @pl.loop(0, width // tile)
        def _(at):
            cut = pl.ds(pl.multiple_of(at * tile, tile), tile)
            place([own_ref], 0, cut)
            for slot in range(1, rows):
                for way, refs_of in enumerate(way_refs):
                    ahead, from_next = goes_ahead(way), row + slot < rows
                    for here, step in (
                        (jnp.logical_and(from_next, jnp.logical_not(ahead)), slot),
                        (jnp.logical_and(jnp.logical_not(from_next), ahead), rows - slot),
                    ):
                        pieces = refs_of[step - 1]
                        pl.when(here)(lambda pieces=pieces, slot=slot: place(pieces, slot * tok_rows, cut))
            total = lax.dot_general(
                cot_ref[...],
                hidden_ref[...],
                (((0,), (0,)), ((), ())),
                preferred_element_type=jnp.float32,
            )
            out_ref[:, cut] = (total * scale).astype(out_ref.dtype)

    whole = pl.BlockSpec(memory_space=pltpu.VMEM)
    return pl.pallas_call(
        kernel,
        out_shape=jax.ShapeDtypeStruct((cot.shape[1], width), jnp.bfloat16),
        in_specs=[whole] * (2 + len(flat)),
        out_specs=whole,
        scratch_shapes=[pltpu.VMEM((cot.shape[0], tile), jnp.bfloat16)],
        compiler_params=pltpu.CompilerParams(vmem_limit_bytes=32 * 2**20),
        cost_estimate=pl.CostEstimate(
            flops=2 * cot.size * width, bytes_accessed=4 * cot.shape[0] * width, transcendentals=0
        ),
        name="weight_product",
    )(cot, own, *flat)


def finish(gate_pre, up_pre, share, fore, back, start, grads):
    span, width = fore.shape
    tile = 512 if width % 512 == 0 else width
    old = () if grads is None else tuple(grads)

    def kernel(*refs):
        gate_ref, up_ref, share_ref, fore_ref, back_ref = refs[:5]
        outs, parts, sems = refs[5 + len(old) : 7 + len(old)], refs[-3:-1], refs[-1]
        here = slice(start, start + span)
        copies = []
        for at in range(0, width, tile):
            cut = slice(at, at + tile)
            grad = share_ref[here, cut] + fore_ref[:, cut].astype(jnp.float32) + back_ref[:, cut].astype(jnp.float32)
            gate = gate_ref[here, cut].astype(jnp.float32)
            sigmoid = jax.nn.sigmoid(gate)
            slope = sigmoid * (1.0 + gate * (1.0 - sigmoid))
            parts[0][:, cut] = (grad * up_ref[here, cut].astype(jnp.float32) * slope).astype(jnp.bfloat16)
            parts[1][:, cut] = (grad * (gate * sigmoid)).astype(jnp.bfloat16)
            for which, (part, out) in enumerate(zip(parts, outs)):
                copy = pltpu.make_async_copy(part.at[:, cut], out.at[here, cut], sems.at[which, at // tile])
                copy.start()
                copies.append(copy)
        for copy in copies:
            copy.wait()

    whole, anywhere = pl.BlockSpec(memory_space=pltpu.VMEM), pl.BlockSpec(memory_space=pl.ANY)
    return pl.pallas_call(
        kernel,
        out_shape=[jax.ShapeDtypeStruct(gate_pre.shape, jnp.bfloat16)] * 2,
        in_specs=[whole] * 5 + [anywhere] * len(old),
        out_specs=[anywhere] * 2,
        scratch_shapes=[pltpu.VMEM((span, width), jnp.bfloat16)] * 2
        + [pltpu.SemaphoreType.DMA((2, width // tile))],
        input_output_aliases={5 + at: at for at in range(len(old))},
        compiler_params=pltpu.CompilerParams(vmem_limit_bytes=32 * 2**20),
        cost_estimate=pl.CostEstimate(flops=20 * span * width, bytes_accessed=8 * span * width, transcendentals=span * width),
        name="finish",
    )(gate_pre, up_pre, share, fore, back, *old)


def swap(value, bits):
    return lax.ppermute(value, "col", [(at, at ^ bits) for at in range(lax.axis_size("col"))])


def spread_cotangent(grad_out, hidden, first, second):
    rows, cols = lax.axis_size("row"), lax.axis_size("col")
    row = lax.axis_index("row")
    tok_rows, width = grad_out.shape
    per_row = cols // rows
    if (rows, cols) != (4, 8):
        pairs = [
            (src * cols + per_row * dst + part, dst * cols + per_row * ((src - dst) % rows) + part)
            for src in range(rows)
            for dst in range(rows)
            for part in range(per_row)
        ]
        moved = lax.ppermute(grad_out, ("row", "col"), pairs)
        blocks = lax.all_gather(moved, "col", axis=0)
        blocks = blocks.reshape(rows, per_row, tok_rows, width)
        return blocks.transpose(0, 2, 1, 3).reshape(rows * tok_rows, per_row * width)
    strip = tok_rows * 2 // cols
    chip = lax.axis_index("col") // 2

    def quarter(bits):
        piece = lax.dynamic_slice_in_dim(grad_out, (chip ^ bits) * strip, strip, 0)
        return swap(piece, 2 * bits) if bits else piece

    wide = after([quarter(bits) for bits in range(cols // 2)], hidden[0])

    def across(bits):
        piece = lax.dynamic_index_in_dim(jnp.stack(wide), chip ^ row ^ bits, 0, keepdims=False)
        return lax.ppermute(piece, "row", [(at, at ^ bits) for at in range(rows)]) if bits else piece

    tall = [across(bits) for bits in range(rows - 1, -1, -1)]
    tall = jnp.stack(tall[::-1])
    near = [tall, swap(tall, 2), swap(tall, 4), swap(tall, 6)]
    near[3] = after(near[3], first)
    far = [swap(block, 1) for block in near]
    far = after(far, second[0])
    return lay_strips(near, far)


def per_device(gate_pre, up_pre, down_t, grad_out):
    rows = lax.axis_size("row")
    tok_rows, width = gate_pre.shape
    norm_scale = (tok_rows * rows) ** (-0.5)
    wire = jnp.bfloat16 if rows <= 4 else jnp.float32
    lead = tok_rows * 8 // 16
    chains = ((0, lead), (lead, tok_rows - lead))

    hidden, ways = [], ([[]], [[]])
    for start, count in chains:
        gate_cut = gate_pre[start : start + count].astype(jnp.float32)
        up_cut = up_pre[start : start + count].astype(jnp.float32)
        hidden.append((gate_cut * jax.nn.sigmoid(gate_cut) * up_cut).astype(jnp.bfloat16))
        for way, steps in enumerate(ways):
            steps[0].append(ring(hidden[-1].astype(wire), way))

    cot = spread_cotangent(grad_out, hidden, [steps[0][0] for steps in ways], [steps[0][1] for steps in ways])
    turn = hidden[0]
    for step in range(2, rows + 1):
        for steps in ways:
            steps.append([])
        for at, (first, _) in enumerate(chains):
            for way, steps in enumerate(ways):
                got = after(steps[-2][at], turn)
                turn = add_share(got, cot, down_t, way, step, first, tok_rows)
                steps[-1].append(ring(turn, way))
        late = turn

    weight_grad = weight_product(cot, jnp.concatenate(hidden), [steps[:-1] for steps in ways], norm_scale)

    own_share = jnp.dot(after(cot[:tok_rows], late), down_t, preferred_element_type=jnp.float32)
    own_share, gate_again, up_again = after((own_share, gate_pre, up_pre), turn)
    grads = None
    for at, (first, _) in enumerate(chains):
        grads = finish(gate_again, up_again, own_share, ways[0][-1][at], ways[1][-1][at], first, grads)
    return *grads, weight_grad


def solution(mesh):
    specs = (P("row", "col"),) * 4
    return jax.shard_map(
        per_device, mesh=mesh, in_specs=specs, out_specs=specs[:3], check_vma=False
    )
```

profile of v0, /device:TPU:0, one launch (start us, length us, event | category | flops | bytes accessed | tf_op | source)
XLA Modules:
  0.0 115.3 jit_solution(6587469654595531553)
XLA Ops:
  1.6 3.0 %collective-permute-start = (bf16[64,512]{1,0:T(8,128)(2,1)S(1)}, bf16[64,512]{1,0:T(8,128)(2,1)S(1)}, u32[]{:S(2)}, u32[]{:S(2)}) collective-permute-start(bf16[64,512]{1,0:T(8,128)(2,1)S(1)} %get-tuple-element.68), channel_id=1, source_target_pairs={{0,2},{1,3},{2,0},{3,1},{4,6},{5,7},{6,4},{7,5},{8,10},{9,11},{10,... | collective-permute-start | bytes 196616 | tf_op jit(solution)/shard_map/ppermute | solution.py:181
  4.6 1.5 %collective-permute-start.1 = (bf16[64,512]{1,0:T(8,128)(2,1)S(1)}, bf16[64,512]{1,0:T(8,128)(2,1)S(1)}, u32[]{:S(2)}, u32[]{:S(2)}) collective-permute-start(bf16[64,512]{1,0:T(8,128)(2,1)S(1)} %get-tuple-element.70), channel_id=1, source_target_pairs={{0,4},{1,5},{2,6},{3,7},{4,0},{5,1},{6,2},{7,3},{8,12},{9,13},{10,... | collective-permute-start | bytes 196616 | tf_op jit(solution)/shard_map/ppermute | solution.py:181
  6.2 2.2 %fusion.8 = (bf16[128,2048]{1,0:T(8,128)(2,1)S(1)}, bf16[128,2048]{1,0:T(8,128)(2,1)S(1)}) fusion(bf16[256,2048]{1,0:T(8,128)(2,1)} %refs_1_.1, bf16[256,2048]{1,0:T(8,128)(2,1)} %refs_0_.1), kind=kLoop, calls=%fused_computation.13 | loop fusion | flops 4194304 | bytes 3145728 | tf_op jit(solution)/shard_map/convert_element_type | solution.py:234
  8.9 2.4 %collective-permute-done.2 = bf16[64,512]{1,0:T(8,128)(2,1)S(1)} collective-permute-done((bf16[64,512]{1,0:T(8,128)(2,1)S(1)}, bf16[64,512]{1,0:T(8,128)(2,1)S(1)}, u32[]{:S(2)}, u32[]{:S(2)}) %collective-permute-start.2) | collective-permute-done | bytes 65568 | tf_op jit(solution)/shard_map/ppermute | solution.py:181
  11.4 1.6 %collective-permute-start.3 = (bf16[64,512]{1,0:T(8,128)(2,1)S(1)}, bf16[64,512]{1,0:T(8,128)(2,1)S(1)}, u32[]{:S(2)}, u32[]{:S(2)}) collective-permute-start(bf16[64,512]{1,0:T(8,128)(2,1)S(1)} %get-tuple-element.66), channel_id=1, source_target_pairs={{0,8},{8,0},{16,24},{24,16},{1,9},{9,1},{17,25},{25,17},{2,10},{10... | collective-permute-start | bytes 196616 | tf_op jit(solution)/shard_map/ppermute | solution.py:211
  13.0 2.6 %collective-permute-start.4 = (bf16[64,512]{1,0:T(8,128)(2,1)S(1)}, bf16[64,512]{1,0:T(8,128)(2,1)S(1)}, u32[]{:S(2)}, u32[]{:S(2)}) collective-permute-start(bf16[64,512]{1,0:T(8,128)(2,1)S(1)} %get-tuple-element.65), channel_id=1, source_target_pairs={{0,16},{8,24},{16,0},{24,8},{1,17},{9,25},{17,1},{25,9},{2,18},{10... | collective-permute-start | bytes 196616 | tf_op jit(solution)/shard_map/ppermute | solution.py:211
  17.1 4.6 %collective-permute-start.9 = (bf16[128,2048]{1,0:T(8,128)(2,1)S(1)}, bf16[128,2048]{1,0:T(8,128)(2,1)S(1)}, u32[]{:S(2)}, u32[]{:S(2)}) collective-permute-start(bf16[128,2048]{1,0:T(8,128)(2,1)S(1)} %get-tuple-element.62), channel_id=1, source_target_pairs={{0,8},{2,10},{4,12},{6,14},{8,16},{9,1},{10,18},{11,3},{12,20},{13... | collective-permute-start | bytes 1572872 | tf_op jit(solution)/shard_map/ppermute | solution.py:50
  23.9 1.5 %collective-permute-start.7 = (bf16[4,64,512]{2,1,0:T(8,128)(2,1)S(1)}, bf16[4,64,512]{2,1,0:T(8,128)(2,1)S(1)}, u32[]{:S(2)}, u32[]{:S(2)}) collective-permute-start(bf16[4,64,512]{2,1,0:T(8,128)(2,1)S(1)} %pad_maximum_fusion.2.refs_0_), channel_id=1, source_target_pairs={{0,4},{1,5},{2,6},{3,7},{4,0},{5,1},{6,2},{7,3},{8,12},{9,13},{10,... | collective-permute-start | bytes 786440 | tf_op jit(solution)/shard_map/ppermute | solution.py:181
  25.4 5.5 %collective-permute-done.8.refs_3_ = bf16[4,64,512]{2,1,0:T(8,128)(2,1)S(1)} collective-permute-done((bf16[4,64,512]{2,1,0:T(8,128)(2,1)S(1)}, bf16[4,64,512]{2,1,0:T(8,128)(2,1)S(1)}, u32[]{:S(2)}, u32[]{:S(2)}) %collective-permute-start.8) | collective-permute-done | bytes 262176 | tf_op jit(solution)/shard_map/ppermute | solution.py:181
  30.9 2.6 %collective-permute-start.15 = (bf16[128,2048]{1,0:T(8,128)(2,1)S(1)}, bf16[128,2048]{1,0:T(8,128)(2,1)S(1)}, u32[]{:S(2)}, u32[]{:S(2)}) collective-permute-start(bf16[128,2048]{1,0:T(8,128)(2,1)S(1)} %get-tuple-element.61), channel_id=1, source_target_pairs={{0,8},{2,10},{4,12},{6,14},{8,16},{9,1},{10,18},{11,3},{12,20},{13... | collective-permute-start | bytes 1572872 | tf_op jit(solution)/shard_map/ppermute | solution.py:50
  34.9 3.2 %collective-permute-start.12 = (bf16[4,64,512]{2,1,0:T(8,128)(2,1)S(1)}, bf16[4,64,512]{2,1,0:T(8,128)(2,1)S(1)}, u32[]{:S(2)}, u32[]{:S(2)}) collective-permute-start(bf16[4,64,512]{2,1,0:T(8,128)(2,1)S(1)} %collective-permute-done.6.refs_1_), channel_id=1, source_target_pairs={{0,1},{1,0},{2,3},{3,2},{4,5},{5,4},{6,7},{7,6},{8,9},{9,8},{10,11... | collective-permute-start | bytes 786440 | tf_op jit(solution)/shard_map/ppermute | solution.py:181
  38.6 3.3 %collective-permute-done.15.got_ref.refs_1_ = bf16[128,2048]{1,0:T(8,128)(2,1)S(1)} collective-permute-done((bf16[128,2048]{1,0:T(8,128)(2,1)S(1)}, bf16[128,2048]{1,0:T(8,128)(2,1)S(1)}, u32[]{:S(2)}, u32[]{:S(2)}) %collective-permute-start.15) | collective-permute-done | bytes 524320 | tf_op jit(solution)/shard_map/ppermute | solution.py:50
  42.9 4.3 %collective-permute-start.20 = (bf16[128,2048]{1,0:T(8,128)(2,1)S(1)}, bf16[128,2048]{1,0:T(8,128)(2,1)S(1)}, u32[]{:S(2)}, u32[]{:S(2)}) collective-permute-start(bf16[128,2048]{1,0:T(8,128)(2,1)S(1)} %add_share.12), channel_id=1, source_target_pairs={{0,8},{2,10},{4,12},{6,14},{8,16},{9,1},{10,18},{11,3},{12,20},{13... | collective-permute-start | bytes 1572872 | tf_op jit(solution)/shard_map/ppermute | solution.py:50
  49.3 4.6 %collective-permute-start.18 = (bf16[128,2048]{1,0:T(8,128)(2,1)S(1)}, bf16[128,2048]{1,0:T(8,128)(2,1)S(1)}, u32[]{:S(2)}, u32[]{:S(2)}) collective-permute-start(bf16[128,2048]{1,0:T(8,128)(2,1)S(1)} %add_share.14), channel_id=1, source_target_pairs={{0,8},{2,10},{4,12},{6,14},{8,16},{9,1},{10,18},{11,3},{12,20},{13... | collective-permute-start | bytes 1572872 | tf_op jit(solution)/shard_map/ppermute | solution.py:50
  55.3 4.2 %collective-permute-done.20.got_ref.refs_2_ = bf16[128,2048]{1,0:T(8,128)(2,1)S(1)} collective-permute-done((bf16[128,2048]{1,0:T(8,128)(2,1)S(1)}, bf16[128,2048]{1,0:T(8,128)(2,1)S(1)}, u32[]{:S(2)}, u32[]{:S(2)}) %collective-permute-start.20) | collective-permute-done | bytes 524320 | tf_op jit(solution)/shard_map/ppermute | solution.py:50
  60.2 4.7 %collective-permute-start.24 = (bf16[128,2048]{1,0:T(8,128)(2,1)S(1)}, bf16[128,2048]{1,0:T(8,128)(2,1)S(1)}, u32[]{:S(2)}, u32[]{:S(2)}) collective-permute-start(bf16[128,2048]{1,0:T(8,128)(2,1)S(1)} %add_share.16), channel_id=1, source_target_pairs={{0,8},{2,10},{4,12},{6,14},{8,16},{9,1},{10,18},{11,3},{12,20},{13... | collective-permute-start | bytes 1572872 | tf_op jit(solution)/shard_map/ppermute | solution.py:50
  66.4 4.4 %collective-permute-done.18.got_ref.refs_3_ = bf16[128,2048]{1,0:T(8,128)(2,1)S(1)} collective-permute-done((bf16[128,2048]{1,0:T(8,128)(2,1)S(1)}, bf16[128,2048]{1,0:T(8,128)(2,1)S(1)}, u32[]{:S(2)}, u32[]{:S(2)}) %collective-permute-start.18) | collective-permute-done | bytes 524320 | tf_op jit(solution)/shard_map/ppermute | solution.py:50
  71.5 4.7 %collective-permute-start.22 = (bf16[128,2048]{1,0:T(8,128)(2,1)S(1)}, bf16[128,2048]{1,0:T(8,128)(2,1)S(1)}, u32[]{:S(2)}, u32[]{:S(2)}) collective-permute-start(bf16[128,2048]{1,0:T(8,128)(2,1)S(1)} %add_share.18), channel_id=1, source_target_pairs={{0,8},{2,10},{4,12},{6,14},{8,16},{9,1},{10,18},{11,3},{12,20},{13... | collective-permute-start | bytes 1572872 | tf_op jit(solution)/shard_map/ppermute | solution.py:50
  77.7 4.3 %collective-permute-done.24.got_ref.refs_4_ = bf16[128,2048]{1,0:T(8,128)(2,1)S(1)} collective-permute-done((bf16[128,2048]{1,0:T(8,128)(2,1)S(1)}, bf16[128,2048]{1,0:T(8,128)(2,1)S(1)}, u32[]{:S(2)}, u32[]{:S(2)}) %collective-permute-start.24) | collective-permute-done | bytes 524320 | tf_op jit(solution)/shard_map/ppermute | solution.py:50
  82.7 4.7 %collective-permute-start.27 = (bf16[128,2048]{1,0:T(8,128)(2,1)S(1)}, bf16[128,2048]{1,0:T(8,128)(2,1)S(1)}, u32[]{:S(2)}, u32[]{:S(2)}) collective-permute-start(bf16[128,2048]{1,0:T(8,128)(2,1)S(1)} %add_share.20), channel_id=1, source_target_pairs={{0,8},{2,10},{4,12},{6,14},{8,16},{9,1},{10,18},{11,3},{12,20},{13... | collective-permute-start | bytes 1572872 | tf_op jit(solution)/shard_map/ppermute | solution.py:50
  88.8 4.4 %collective-permute-done.22.got_ref.refs_5_ = bf16[128,2048]{1,0:T(8,128)(2,1)S(1)} collective-permute-done((bf16[128,2048]{1,0:T(8,128)(2,1)S(1)}, bf16[128,2048]{1,0:T(8,128)(2,1)S(1)}, u32[]{:S(2)}, u32[]{:S(2)}) %collective-permute-start.22) | collective-permute-done | bytes 524320 | tf_op jit(solution)/shard_map/ppermute | solution.py:50
  93.9 4.7 %collective-permute-start.25 = (bf16[128,2048]{1,0:T(8,128)(2,1)S(1)}, bf16[128,2048]{1,0:T(8,128)(2,1)S(1)}, u32[]{:S(2)}, u32[]{:S(2)}) collective-permute-start(bf16[128,2048]{1,0:T(8,128)(2,1)S(1)} %add_share.22), channel_id=1, source_target_pairs={{0,8},{2,10},{4,12},{6,14},{8,16},{9,1},{10,18},{11,3},{12,20},{13... | collective-permute-start | bytes 1572872 | tf_op jit(solution)/shard_map/ppermute | solution.py:50
  101.5 7.6 %weight_product.1 = bf16[1024,2048]{1,0:T(8,128)(2,1)} custom-call(bf16[1024,1024]{1,0:T(8,128)(2,1)S(1)} %lay_strips.1.cot_ref, bf16[256,2048]{1,0:T(8,128)(2,1)S(1)} %pad_maximum_fusion.own_ref, bf16[128,2048]{1,0:T(8,128)(2,1)S(1)} %collective-permute-done.9.got_ref.refs_0_, bf16[128,2048]{1,0:T(8,128)(2,1)S(1)} %collective-permute-done.15.got_ref.refs_1_, ...), custom_call_target="tpu_custom_call" | custom-call | flops 4294967296 | bytes 8388608 | tf_op jit(solution)/shard_map/weight_product/pallas_call | solution.py:126
  110.5 2.0 %collective-permute-done.26.refs_4_ = bf16[128,2048]{1,0:T(8,128)(2,1)S(1)} collective-permute-done((bf16[128,2048]{1,0:T(8,128)(2,1)S(1)}, bf16[128,2048]{1,0:T(8,128)(2,1)S(1)}, u32[]{:S(2)}, u32[]{:S(2)}) %collective-permute-start.26) | collective-permute-done | bytes 524320 | tf_op jit(solution)/shard_map/ppermute | solution.py:50
  (64 shorter events, 25.3 us)
Async XLA Ops:
  1.6 6.8 %collective-permute-start = (bf16[64,512]{1,0:T(8,128)(2,1)S(1)}, bf16[64,512]{1,0:T(8,128)(2,1)S(1)}, u32[]{:S(2)}, u32[]{:S(2)}) collective-permute-start(bf16[64,512]{1,0:T(8,128)(2,1)S(1)} %get-tuple-element.68), channel_id=1, source_target_pairs={{0,2},{1,3},{2,0},{3,1},{4,6},{5,7},{6,4},{7,5},{8,10},{9,11},{10,... | collective-permute-start | bytes 196616 | tf_op jit(solution)/shard_map/ppermute | solution.py:181
  11.4 10.3 %collective-permute-start.3 = (bf16[64,512]{1,0:T(8,128)(2,1)S(1)}, bf16[64,512]{1,0:T(8,128)(2,1)S(1)}, u32[]{:S(2)}, u32[]{:S(2)}) collective-permute-start(bf16[64,512]{1,0:T(8,128)(2,1)S(1)} %get-tuple-element.66), channel_id=1, source_target_pairs={{0,8},{8,0},{16,24},{24,16},{1,9},{9,1},{17,25},{25,17},{2,10},{10... | collective-permute-start | bytes 196616 | tf_op jit(solution)/shard_map/ppermute | solution.py:211
  13.0 8.7 %collective-permute-start.4 = (bf16[64,512]{1,0:T(8,128)(2,1)S(1)}, bf16[64,512]{1,0:T(8,128)(2,1)S(1)}, u32[]{:S(2)}, u32[]{:S(2)}) collective-permute-start(bf16[64,512]{1,0:T(8,128)(2,1)S(1)} %get-tuple-element.65), channel_id=1, source_target_pairs={{0,16},{8,24},{16,0},{24,8},{1,17},{9,25},{17,1},{25,9},{2,18},{10... | collective-permute-start | bytes 196616 | tf_op jit(solution)/shard_map/ppermute | solution.py:211
  15.6 6.2 %collective-permute-start.5 = (bf16[64,512]{1,0:T(8,128)(2,1)S(1)}, bf16[64,512]{1,0:T(8,128)(2,1)S(1)}, u32[]{:S(2)}, u32[]{:S(2)}) collective-permute-start(bf16[64,512]{1,0:T(8,128)(2,1)S(1)} %get-tuple-element.64), channel_id=1, source_target_pairs={{0,24},{8,16},{16,8},{24,0},{1,25},{9,17},{17,9},{25,1},{2,26},{10... | collective-permute-start | bytes 196616 | tf_op jit(solution)/shard_map/ppermute | solution.py:211
  15.9 19.1 %collective-permute-start.10 = (bf16[128,2048]{1,0:T(8,128)(2,1)S(1)}, bf16[128,2048]{1,0:T(8,128)(2,1)S(1)}, u32[]{:S(2)}, u32[]{:S(2)}) collective-permute-start(bf16[128,2048]{1,0:T(8,128)(2,1)S(1)} %get-tuple-element.62), channel_id=1, source_target_pairs={{1,9},{3,11},{5,13},{7,15},{8,0},{9,17},{10,2},{11,19},{12,4},{13,... | collective-permute-start | bytes 1572872 | tf_op jit(solution)/shard_map/ppermute | solution.py:50
  17.1 21.0 %collective-permute-start.9 = (bf16[128,2048]{1,0:T(8,128)(2,1)S(1)}, bf16[128,2048]{1,0:T(8,128)(2,1)S(1)}, u32[]{:S(2)}, u32[]{:S(2)}) collective-permute-start(bf16[128,2048]{1,0:T(8,128)(2,1)S(1)} %get-tuple-element.62), channel_id=1, source_target_pairs={{0,8},{2,10},{4,12},{6,14},{8,16},{9,1},{10,18},{11,3},{12,20},{13... | collective-permute-start | bytes 1572872 | tf_op jit(solution)/shard_map/ppermute | solution.py:50
  21.8 9.1 %collective-permute-start.8 = (bf16[4,64,512]{2,1,0:T(8,128)(2,1)S(1)}, bf16[4,64,512]{2,1,0:T(8,128)(2,1)S(1)}, u32[]{:S(2)}, u32[]{:S(2)}) collective-permute-start(bf16[4,64,512]{2,1,0:T(8,128)(2,1)S(1)} %pad_maximum_fusion.2.refs_0_), channel_id=1, source_target_pairs={{0,6},{1,7},{2,4},{3,5},{4,2},{5,3},{6,0},{7,1},{8,14},{9,15},{10,... | collective-permute-start | bytes 786440 | tf_op jit(solution)/shard_map/ppermute | solution.py:181
  22.4 11.2 %collective-permute-start.6 = (bf16[4,64,512]{2,1,0:T(8,128)(2,1)S(1)}, bf16[4,64,512]{2,1,0:T(8,128)(2,1)S(1)}, u32[]{:S(2)}, u32[]{:S(2)}) collective-permute-start(bf16[4,64,512]{2,1,0:T(8,128)(2,1)S(1)} %pad_maximum_fusion.2.refs_0_), channel_id=1, source_target_pairs={{0,2},{1,3},{2,0},{3,1},{4,6},{5,7},{6,4},{7,5},{8,10},{9,11},{10,... | collective-permute-start | bytes 786440 | tf_op jit(solution)/shard_map/ppermute | solution.py:181
  23.9 9.8 %collective-permute-start.7 = (bf16[4,64,512]{2,1,0:T(8,128)(2,1)S(1)}, bf16[4,64,512]{2,1,0:T(8,128)(2,1)S(1)}, u32[]{:S(2)}, u32[]{:S(2)}) collective-permute-start(bf16[4,64,512]{2,1,0:T(8,128)(2,1)S(1)} %pad_maximum_fusion.2.refs_0_), channel_id=1, source_target_pairs={{0,4},{1,5},{2,6},{3,7},{4,0},{5,1},{6,2},{7,3},{8,12},{9,13},{10,... | collective-permute-start | bytes 786440 | tf_op jit(solution)/shard_map/ppermute | solution.py:181
  30.9 11.0 %collective-permute-start.15 = (bf16[128,2048]{1,0:T(8,128)(2,1)S(1)}, bf16[128,2048]{1,0:T(8,128)(2,1)S(1)}, u32[]{:S(2)}, u32[]{:S(2)}) collective-permute-start(bf16[128,2048]{1,0:T(8,128)(2,1)S(1)} %get-tuple-element.61), channel_id=1, source_target_pairs={{0,8},{2,10},{4,12},{6,14},{8,16},{9,1},{10,18},{11,3},{12,20},{13... | collective-permute-start | bytes 1572872 | tf_op jit(solution)/shard_map/ppermute | solution.py:50
  33.6 20.3 %collective-permute-start.16 = (bf16[128,2048]{1,0:T(8,128)(2,1)S(1)}, bf16[128,2048]{1,0:T(8,128)(2,1)S(1)}, u32[]{:S(2)}, u32[]{:S(2)}) collective-permute-start(bf16[128,2048]{1,0:T(8,128)(2,1)S(1)} %get-tuple-element.61), channel_id=1, source_target_pairs={{1,9},{3,11},{5,13},{7,15},{8,0},{9,17},{10,2},{11,19},{12,4},{13,... | collective-permute-start | bytes 1572872 | tf_op jit(solution)/shard_map/ppermute | solution.py:50
  34.9 7.0 %collective-permute-start.12 = (bf16[4,64,512]{2,1,0:T(8,128)(2,1)S(1)}, bf16[4,64,512]{2,1,0:T(8,128)(2,1)S(1)}, u32[]{:S(2)}, u32[]{:S(2)}) collective-permute-start(bf16[4,64,512]{2,1,0:T(8,128)(2,1)S(1)} %collective-permute-done.6.refs_1_), channel_id=1, source_target_pairs={{0,1},{1,0},{2,3},{3,2},{4,5},{5,4},{6,7},{7,6},{8,9},{9,8},{10,11... | collective-permute-start | bytes 786440 | tf_op jit(solution)/shard_map/ppermute | solution.py:181
  42.9 16.6 %collective-permute-start.20 = (bf16[128,2048]{1,0:T(8,128)(2,1)S(1)}, bf16[128,2048]{1,0:T(8,128)(2,1)S(1)}, u32[]{:S(2)}, u32[]{:S(2)}) collective-permute-start(bf16[128,2048]{1,0:T(8,128)(2,1)S(1)} %add_share.12), channel_id=1, source_target_pairs={{0,8},{2,10},{4,12},{6,14},{8,16},{9,1},{10,18},{11,3},{12,20},{13... | collective-permute-start | bytes 1572872 | tf_op jit(solution)/shard_map/ppermute | solution.py:50
  47.2 17.8 %collective-permute-start.19 = (bf16[128,2048]{1,0:T(8,128)(2,1)S(1)}, bf16[128,2048]{1,0:T(8,128)(2,1)S(1)}, u32[]{:S(2)}, u32[]{:S(2)}) collective-permute-start(bf16[128,2048]{1,0:T(8,128)(2,1)S(1)} %add_share.13), channel_id=1, source_target_pairs={{1,9},{3,11},{5,13},{7,15},{8,0},{9,17},{10,2},{11,19},{12,4},{13,... | collective-permute-start | bytes 1572872 | tf_op jit(solution)/shard_map/ppermute | solution.py:50
  49.3 21.5 %collective-permute-start.18 = (bf16[128,2048]{1,0:T(8,128)(2,1)S(1)}, bf16[128,2048]{1,0:T(8,128)(2,1)S(1)}, u32[]{:S(2)}, u32[]{:S(2)}) collective-permute-start(bf16[128,2048]{1,0:T(8,128)(2,1)S(1)} %add_share.14), channel_id=1, source_target_pairs={{0,8},{2,10},{4,12},{6,14},{8,16},{9,1},{10,18},{11,3},{12,20},{13... | collective-permute-start | bytes 1572872 | tf_op jit(solution)/shard_map/ppermute | solution.py:50
  54.0 22.2 %collective-permute-start.17 = (bf16[128,2048]{1,0:T(8,128)(2,1)S(1)}, bf16[128,2048]{1,0:T(8,128)(2,1)S(1)}, u32[]{:S(2)}, u32[]{:S(2)}) collective-permute-start(bf16[128,2048]{1,0:T(8,128)(2,1)S(1)} %add_share.15), channel_id=1, source_target_pairs={{1,9},{3,11},{5,13},{7,15},{8,0},{9,17},{10,2},{11,19},{12,4},{13,... | collective-permute-start | bytes 1572872 | tf_op jit(solution)/shard_map/ppermute | solution.py:50
  60.2 21.7 %collective-permute-start.24 = (bf16[128,2048]{1,0:T(8,128)(2,1)S(1)}, bf16[128,2048]{1,0:T(8,128)(2,1)S(1)}, u32[]{:S(2)}, u32[]{:S(2)}) collective-permute-start(bf16[128,2048]{1,0:T(8,128)(2,1)S(1)} %add_share.16), channel_id=1, source_target_pairs={{0,8},{2,10},{4,12},{6,14},{8,16},{9,1},{10,18},{11,3},{12,20},{13... | collective-permute-start | bytes 1572872 | tf_op jit(solution)/shard_map/ppermute | solution.py:50
  65.1 22.4 %collective-permute-start.23 = (bf16[128,2048]{1,0:T(8,128)(2,1)S(1)}, bf16[128,2048]{1,0:T(8,128)(2,1)S(1)}, u32[]{:S(2)}, u32[]{:S(2)}) collective-permute-start(bf16[128,2048]{1,0:T(8,128)(2,1)S(1)} %add_share.17), channel_id=1, source_target_pairs={{1,9},{3,11},{5,13},{7,15},{8,0},{9,17},{10,2},{11,19},{12,4},{13,... | collective-permute-start | bytes 1572872 | tf_op jit(solution)/shard_map/ppermute | solution.py:50
  71.5 21.7 %collective-permute-start.22 = (bf16[128,2048]{1,0:T(8,128)(2,1)S(1)}, bf16[128,2048]{1,0:T(8,128)(2,1)S(1)}, u32[]{:S(2)}, u32[]{:S(2)}) collective-permute-start(bf16[128,2048]{1,0:T(8,128)(2,1)S(1)} %add_share.18), channel_id=1, source_target_pairs={{0,8},{2,10},{4,12},{6,14},{8,16},{9,1},{10,18},{11,3},{12,20},{13... | collective-permute-start | bytes 1572872 | tf_op jit(solution)/shard_map/ppermute | solution.py:50
  76.3 22.4 %collective-permute-start.21 = (bf16[128,2048]{1,0:T(8,128)(2,1)S(1)}, bf16[128,2048]{1,0:T(8,128)(2,1)S(1)}, u32[]{:S(2)}, u32[]{:S(2)}) collective-permute-start(bf16[128,2048]{1,0:T(8,128)(2,1)S(1)} %add_share.19), channel_id=1, source_target_pairs={{1,9},{3,11},{5,13},{7,15},{8,0},{9,17},{10,2},{11,19},{12,4},{13,... | collective-permute-start | bytes 1572872 | tf_op jit(solution)/shard_map/ppermute | solution.py:50
  82.7 26.4 %collective-permute-start.27 = (bf16[128,2048]{1,0:T(8,128)(2,1)S(1)}, bf16[128,2048]{1,0:T(8,128)(2,1)S(1)}, u32[]{:S(2)}, u32[]{:S(2)}) collective-permute-start(bf16[128,2048]{1,0:T(8,128)(2,1)S(1)} %add_share.20), channel_id=1, source_target_pairs={{0,8},{2,10},{4,12},{6,14},{8,16},{9,1},{10,18},{11,3},{12,20},{13... | collective-permute-start | bytes 1572872 | tf_op jit(solution)/shard_map/ppermute | solution.py:50
  87.5 21.6 %collective-permute-start.28 = (bf16[128,2048]{1,0:T(8,128)(2,1)S(1)}, bf16[128,2048]{1,0:T(8,128)(2,1)S(1)}, u32[]{:S(2)}, u32[]{:S(2)}) collective-permute-start(bf16[128,2048]{1,0:T(8,128)(2,1)S(1)} %add_share.21), channel_id=1, source_target_pairs={{1,9},{3,11},{5,13},{7,15},{8,0},{9,17},{10,2},{11,19},{12,4},{13,... | collective-permute-start | bytes 1572872 | tf_op jit(solution)/shard_map/ppermute | solution.py:50
  93.9 19.9 %collective-permute-start.25 = (bf16[128,2048]{1,0:T(8,128)(2,1)S(1)}, bf16[128,2048]{1,0:T(8,128)(2,1)S(1)}, u32[]{:S(2)}, u32[]{:S(2)}) collective-permute-start(bf16[128,2048]{1,0:T(8,128)(2,1)S(1)} %add_share.22), channel_id=1, source_target_pairs={{0,8},{2,10},{4,12},{6,14},{8,16},{9,1},{10,18},{11,3},{12,20},{13... | collective-permute-start | bytes 1572872 | tf_op jit(solution)/shard_map/ppermute | solution.py:50
  98.9 13.6 %collective-permute-start.26 = (bf16[128,2048]{1,0:T(8,128)(2,1)S(1)}, bf16[128,2048]{1,0:T(8,128)(2,1)S(1)}, u32[]{:S(2)}, u32[]{:S(2)}) collective-permute-start(bf16[128,2048]{1,0:T(8,128)(2,1)S(1)} %add_share.23), channel_id=1, source_target_pairs={{1,9},{3,11},{5,13},{7,15},{8,0},{9,17},{10,2},{11,19},{12,4},{13,... | collective-permute-start | bytes 1572872 | tf_op jit(solution)/shard_map/ppermute | solution.py:50
  (8 other events, 48.1 us)
where the time goes:
time: 116 us; the launch traced here: 115 us
  starting transfers between devices  61.6 us (53%)
  waiting for transfers between devices  32.4 us (28%)
  Pallas kernels  15.4 us (13%)
  other arithmetic  2.33 us (2%)
  between operations  1.29 us (1%)
  matrix products  1.25 us (1%)
    ppermute x16, starting transfers between devices, ring(): return lax.ppermute(value, ('row', 'col'), pairs)  45.3 us
    ppermute x16, waiting for transfers between devices, ring(): return lax.ppermute(value, ('row', 'col'), pairs)  23.9 us
    ppermute x10, starting transfers between devices, swap(): lax.ppermute(value, 'col', [(at, at ^ bits) for at in range(lax.axis_size...  11.8 us
    ppermute x10, waiting for transfers between devices, swap(): lax.ppermute(value, 'col', [(at, at ^ bits) for at in range(lax.axis_size...  8.45 us
    pallas_call x1, Pallas kernels, weight_product(): pl.pallas_call(kernel, out_shape=jax.ShapeDtypeStruct((cot.shape[1], widt...  7.6 us
    pallas_call x12, Pallas kernels, add_share(): pl.pallas_call(kernel, out_shape=jax.ShapeDtypeStruct(got.shape, got.dtyp...  4.88 us
    ppermute x3, starting transfers between devices, across(): lax.ppermute(piece, 'row', [(at, at ^ bits) for at in range(rows)])  4.45 us
    pallas_call x2, Pallas kernels, finish(): pl.pallas_call(kernel, out_shape=[jax.ShapeDtypeStruct(gate_pre.shape, jn...  2.77 us
  transfers between devices with their start and end apart: 29, of which 11 were waited for; matrix products, arithmetic and copies ran while one was open for 3% of the time, Pallas kernels for 12%

commit v1 on v0

--- a/solution.py
+++ b/solution.py
@@ -10,24 +10,24 @@
     return lax.optimization_barrier((value, first))[0]
 
 
-def lay_strips(near, far):
+def lay_strips(near, far, groups):
     chips = len(near)
-    rows, strip, width = near[0].shape
+    _, strip, width = near[0].shape
 
     def kernel(*refs):
-        row, col = lax.axis_index("row"), lax.axis_index("col")
+        rows, row, col = lax.axis_size("row"), lax.axis_index("row"), lax.axis_index("col")
         out_ref = refs[-1]
         for at, ref in enumerate(refs[:-1]):
             core, chip = at // chips, at % chips
             lane = pl.multiple_of(((col & 1) ^ core) * width, width)
-            for group in range(rows):
-                slot = lax.rem((row ^ group) + rows - row, rows)
+            for at_group, group in enumerate(groups):
+                slot = lax.rem((row ^ group) + rows - row, rows) - groups[0]
                 start = (slot * chips + (col // 2 ^ chip)) * strip
-                out_ref[pl.ds(pl.multiple_of(start, strip), strip), pl.ds(lane, width)] = ref[group]
-
-    return pl.pallas_call(
-        kernel,
-        out_shape=jax.ShapeDtypeStruct((rows * chips * strip, 2 * width), near[0].dtype),
+                out_ref[pl.ds(pl.multiple_of(start, strip), strip), pl.ds(lane, width)] = ref[at_group]
+
+    return pl.pallas_call(
+        kernel,
+        out_shape=jax.ShapeDtypeStruct((len(groups) * chips * strip, 2 * width), near[0].dtype),
         in_specs=[pl.BlockSpec(memory_space=pltpu.VMEM)] * 2 * chips,
         out_specs=pl.BlockSpec(memory_space=pltpu.VMEM),
         compiler_params=pltpu.CompilerParams(vmem_limit_bytes=32 * 2**20),
@@ -57,7 +57,7 @@
     def kernel(got_ref, cot_ref, down_ref, out_ref):
         rows, row, ahead = lax.axis_size("row"), lax.axis_index("row"), goes_ahead(way)
         is_sum = step > jnp.where(ahead, row + 1, rows - row)
-        start = jnp.where(ahead, rows + 1 - step, step - 1) * tok_rows + first
+        start = jnp.where(ahead, rows - step, step - 2) * tok_rows + first
 
         @pl.when(is_sum)
         def _():
@@ -85,13 +85,13 @@
     )(got, cot, down_t)
 
 
-def weight_product(cot, own, ways, scale):
+def weight_product(own_cot, cot, own, ways, scale):
     rows = len(ways[0]) + 1
     tok_rows, width = own.shape
     tile = 512 if width % 512 == 0 else width
     flat = [piece for steps in ways for pieces in steps for piece in pieces]
 
-    def kernel(cot_ref, own_ref, *refs):
+    def kernel(own_cot_ref, cot_ref, own_ref, *refs):
         ends, (out_ref, hidden_ref) = iter(refs[: len(flat)]), refs[len(flat) :]
         way_refs = [[[next(ends) for _ in pieces] for pieces in steps] for steps in ways]
         row = lax.axis_index("row")
@@ -114,11 +114,14 @@
                     ):
                         pieces = refs_of[step - 1]
                         pl.when(here)(lambda pieces=pieces, slot=slot: place(pieces, slot * tok_rows, cut))
-            total = lax.dot_general(
-                cot_ref[...],
-                hidden_ref[...],
-                (((0,), (0,)), ((), ())),
-                preferred_element_type=jnp.float32,
+            total = sum(
+                lax.dot_general(
+                    tokens[...], blocks, (((0,), (0,)), ((), ())), preferred_element_type=jnp.float32
+                )
+                for tokens, blocks in (
+                    (own_cot_ref, hidden_ref[:tok_rows, :]),
+                    (cot_ref, hidden_ref[tok_rows:, :]),
+                )
             )
             out_ref[:, cut] = (total * scale).astype(out_ref.dtype)
 
@@ -126,15 +129,15 @@
     return pl.pallas_call(
         kernel,
         out_shape=jax.ShapeDtypeStruct((cot.shape[1], width), jnp.bfloat16),
-        in_specs=[whole] * (2 + len(flat)),
+        in_specs=[whole] * (3 + len(flat)),
         out_specs=whole,
-        scratch_shapes=[pltpu.VMEM((cot.shape[0], tile), jnp.bfloat16)],
+        scratch_shapes=[pltpu.VMEM((rows * tok_rows, tile), jnp.bfloat16)],
         compiler_params=pltpu.CompilerParams(vmem_limit_bytes=32 * 2**20),
         cost_estimate=pl.CostEstimate(
-            flops=2 * cot.size * width, bytes_accessed=4 * cot.shape[0] * width, transcendentals=0
+            flops=2 * rows * own_cot.size * width, bytes_accessed=4 * rows * tok_rows * width, transcendentals=0
         ),
         name="weight_product",
-    )(cot, own, *flat)
+    )(own_cot, cot, own, *flat)
 
 
 def finish(gate_pre, up_pre, share, fore, back, start, grads):
@@ -196,7 +199,8 @@
         moved = lax.ppermute(grad_out, ("row", "col"), pairs)
         blocks = lax.all_gather(moved, "col", axis=0)
         blocks = blocks.reshape(rows, per_row, tok_rows, width)
-        return blocks.transpose(0, 2, 1, 3).reshape(rows * tok_rows, per_row * width)
+        cot = blocks.transpose(0, 2, 1, 3).reshape(rows * tok_rows, per_row * width)
+        return cot[tok_rows:], lambda stage, value, first: cot[:tok_rows]
     strip = tok_rows * 2 // cols
     chip = lax.axis_index("col") // 2
 
@@ -211,12 +215,23 @@
         return lax.ppermute(piece, "row", [(at, at ^ bits) for at in range(rows)]) if bits else piece
 
     tall = [across(bits) for bits in range(rows - 1, -1, -1)]
-    tall = jnp.stack(tall[::-1])
+    own, tall = tall[-1], jnp.stack(tall[-2::-1])
     near = [tall, swap(tall, 2), swap(tall, 4), swap(tall, 6)]
     near[3] = after(near[3], first)
     far = [swap(block, 1) for block in near]
     far = after(far, second[0])
-    return lay_strips(near, far)
+
+    own = own[None]
+
+    def own_group(stage, value, first):
+        if stage < 2:
+            value = after(own if stage == 0 else value, first)
+            return jnp.concatenate([value, swap(value, (2, 4)[stage])])
+        near = after(value, first)
+        far = swap(near, 1)
+        return lay_strips(*([block[None] for block in blocks] for blocks in (near, far)), range(1))
+
+    return lay_strips(near, far, range(1, rows)), own_group
 
 
 def per_device(gate_pre, up_pre, down_t, grad_out):
@@ -235,8 +250,9 @@
         for way, steps in enumerate(ways):
             steps[0].append(ring(hidden[-1].astype(wire), way))
 
-    cot = spread_cotangent(grad_out, hidden, [steps[0][0] for steps in ways], [steps[0][1] for steps in ways])
+    cot, own_group = spread_cotangent(grad_out, hidden, [steps[0][0] for steps in ways], [steps[0][1] for steps in ways])
     turn = hidden[0]
+    own_cot, stage = None, 0
     for step in range(2, rows + 1):
         for steps in ways:
             steps.append([])
@@ -245,11 +261,13 @@
                 got = after(steps[-2][at], turn)
                 turn = add_share(got, cot, down_t, way, step, first, tok_rows)
                 steps[-1].append(ring(turn, way))
+                if (step, at, way) in ((2, 1, 1), (3, 0, 1), (3, 1, 1)):
+                    own_cot, stage = own_group(stage, own_cot, turn), stage + 1
         late = turn
 
-    weight_grad = weight_product(cot, jnp.concatenate(hidden), [steps[:-1] for steps in ways], norm_scale)
-
-    own_share = jnp.dot(after(cot[:tok_rows], late), down_t, preferred_element_type=jnp.float32)
+    weight_grad = weight_product(own_cot, cot, jnp.concatenate(hidden), [steps[:-1] for steps in ways], norm_scale)
+
+    own_share = jnp.dot(after(own_cot, late), down_t, preferred_element_type=jnp.float32)
     own_share, gate_again, up_again = after((own_share, gate_pre, up_pre), turn)
     grads = None
     for at, (first, _) in enumerate(chains):

time: 116 us -> 114 us (0.983)
  waiting for transfers between devices: 32.4 us -> 28.7 us
  starting transfers between devices: 61.6 us -> 62.9 us
    ppermute x16, waiting for transfers between devices: 23.9 us -> 18 us  [ring(): return lax.ppermute(value, ('row', 'col'), pairs)]
    ppermute x10 -> x13, waiting for transfers between devices: 8.45 us -> 10.7 us  [swap(): lax.ppermute(value, 'col', [(at, at ^ bits) for at in range(lax.axis_size...]
    ppermute x10 -> x13, starting transfers between devices: 11.8 us -> 12.9 us  [swap(): lax.ppermute(value, 'col', [(at, at ^ bits) for at in range(lax.axis_size...]
  transfers between devices with their start and end apart: 29 -> 32, of which waited for: 11 -> 15; matrix products, arithmetic and copies ran while one was open for 3% -> 3% of each run, Pallas kernels for 12% -> 12%
where the time goes in v1:
time: 114 us; the launch traced here: 113 us
  starting transfers between devices  62.9 us (55%)
  waiting for transfers between devices  28.7 us (25%)
  Pallas kernels  15.5 us (14%)
  other arithmetic  2.36 us (2%)
  between operations  1.32 us (1%)
  matrix products  1.25 us (1%)
    ppermute x16, starting transfers between devices, ring(): return lax.ppermute(value, ('row', 'col'), pairs)  45.6 us
    ppermute x16, waiting for transfers between devices, ring(): return lax.ppermute(value, ('row', 'col'), pairs)  18 us
    ppermute x13, starting transfers between devices, swap(): lax.ppermute(value, 'col', [(at, at ^ bits) for at in range(lax.axis_size...  12.9 us
    ppermute x13, waiting for transfers between devices, swap(): lax.ppermute(value, 'col', [(at, at ^ bits) for at in range(lax.axis_size...  10.7 us
    pallas_call x1, Pallas kernels, weight_product(): pl.pallas_call(kernel, out_shape=jax.ShapeDtypeStruct((cot.shape[1], widt...  7.6 us
    pallas_call x12, Pallas kernels, add_share(): pl.pallas_call(kernel, out_shape=jax.ShapeDtypeStruct(got.shape, got.dtyp...  4.89 us
    ppermute x3, starting transfers between devices, across(): lax.ppermute(piece, 'row', [(at, at ^ bits) for at in range(rows)])  4.45 us
    pallas_call x2, Pallas kernels, finish(): pl.pallas_call(kernel, out_shape=[jax.ShapeDtypeStruct(gate_pre.shape, jn...  2.77 us
  transfers between devices with their start and end apart: 32, of which 15 were waited for; matrix products, arithmetic and copies ran while one was open for 3% of the time, Pallas kernels for 12%

profile of v1, /device:TPU:0, one launch (start us, length us, event | category | flops | bytes accessed | tf_op | source)
XLA Modules:
  0.0 113.1 jit_solution(14668011010527942489)
XLA Ops:
  1.6 3.0 %collective-permute-start = (bf16[64,512]{1,0:T(8,128)(2,1)S(1)}, bf16[64,512]{1,0:T(8,128)(2,1)S(1)}, u32[]{:S(2)}, u32[]{:S(2)}) collective-permute-start(bf16[64,512]{1,0:T(8,128)(2,1)S(1)} %get-tuple-element.82), channel_id=1, source_target_pairs={{0,2},{1,3},{2,0},{3,1},{4,6},{5,7},{6,4},{7,5},{8,10},{9,11},{10,... | collective-permute-start | bytes 196616 | tf_op jit(solution)/shard_map/ppermute | solution.py:184
  6.2 2.2 %fusion.8 = (bf16[128,2048]{1,0:T(8,128)(2,1)S(1)}, bf16[128,2048]{1,0:T(8,128)(2,1)S(1)}) fusion(bf16[256,2048]{1,0:T(8,128)(2,1)} %refs_1_.1, bf16[256,2048]{1,0:T(8,128)(2,1)} %refs_0_.1), kind=kLoop, calls=%fused_computation.13 | loop fusion | flops 4194304 | bytes 3145728 | tf_op jit(solution)/shard_map/convert_element_type | solution.py:249
  8.9 2.4 %collective-permute-done.2 = bf16[64,512]{1,0:T(8,128)(2,1)S(1)} collective-permute-done((bf16[64,512]{1,0:T(8,128)(2,1)S(1)}, bf16[64,512]{1,0:T(8,128)(2,1)S(1)}, u32[]{:S(2)}, u32[]{:S(2)}) %collective-permute-start.2) | collective-permute-done | bytes 65568 | tf_op jit(solution)/shard_map/ppermute | solution.py:184
  11.4 1.6 %collective-permute-start.7 = (bf16[64,512]{1,0:T(8,128)(2,1)S(1)}, bf16[64,512]{1,0:T(8,128)(2,1)S(1)}, u32[]{:S(2)}, u32[]{:S(2)}) collective-permute-start(bf16[64,512]{1,0:T(8,128)(2,1)S(1)} %get-tuple-element.77), channel_id=1, source_target_pairs={{0,8},{8,0},{16,24},{24,16},{1,9},{9,1},{17,25},{25,17},{2,10},{10... | collective-permute-start | bytes 196616 | tf_op jit(solution)/shard_map/ppermute | solution.py:215
  13.0 2.6 %collective-permute-start.8 = (bf16[64,512]{1,0:T(8,128)(2,1)S(1)}, bf16[64,512]{1,0:T(8,128)(2,1)S(1)}, u32[]{:S(2)}, u32[]{:S(2)}) collective-permute-start(bf16[64,512]{1,0:T(8,128)(2,1)S(1)} %get-tuple-element.79), channel_id=1, source_target_pairs={{0,16},{8,24},{16,0},{24,8},{1,17},{9,25},{17,1},{25,9},{2,18},{10... | collective-permute-start | bytes 196616 | tf_op jit(solution)/shard_map/ppermute | solution.py:215
  17.1 4.6 %collective-permute-start.6 = (bf16[128,2048]{1,0:T(8,128)(2,1)S(1)}, bf16[128,2048]{1,0:T(8,128)(2,1)S(1)}, u32[]{:S(2)}, u32[]{:S(2)}) collective-permute-start(bf16[128,2048]{1,0:T(8,128)(2,1)S(1)} %get-tuple-element.68), channel_id=1, source_target_pairs={{0,8},{2,10},{4,12},{6,14},{8,16},{9,1},{10,18},{11,3},{12,20},{13... | collective-permute-start | bytes 1572872 | tf_op jit(solution)/shard_map/ppermute | solution.py:50
  23.9 1.5 %collective-permute-start.11 = (bf16[3,64,512]{2,1,0:T(8,128)(2,1)S(1)}, bf16[3,64,512]{2,1,0:T(8,128)(2,1)S(1)}, u32[]{:S(2)}, u32[]{:S(2)}) collective-permute-start(bf16[3,64,512]{2,1,0:T(8,128)(2,1)S(1)} %pad_maximum_fusion.3.refs_0_), channel_id=1, source_target_pairs={{0,4},{1,5},{2,6},{3,7},{4,0},{5,1},{6,2},{7,3},{8,12},{9,13},{10,... | collective-permute-start | bytes 589832 | tf_op jit(solution)/shard_map/ppermute | solution.py:184
  25.4 3.4 %collective-permute-done.12.refs_3_ = bf16[3,64,512]{2,1,0:T(8,128)(2,1)S(1)} collective-permute-done((bf16[3,64,512]{2,1,0:T(8,128)(2,1)S(1)}, bf16[3,64,512]{2,1,0:T(8,128)(2,1)S(1)}, u32[]{:S(2)}, u32[]{:S(2)}) %collective-permute-start.12) | collective-permute-done | bytes 196640 | tf_op jit(solution)/shard_map/ppermute | solution.py:184
  28.8 2.3 %collective-permute-start.4 = (bf16[128,2048]{1,0:T(8,128)(2,1)S(1)}, bf16[128,2048]{1,0:T(8,128)(2,1)S(1)}, u32[]{:S(2)}, u32[]{:S(2)}) collective-permute-start(bf16[128,2048]{1,0:T(8,128)(2,1)S(1)} %get-tuple-element.67), channel_id=1, source_target_pairs={{0,8},{2,10},{4,12},{6,14},{8,16},{9,1},{10,18},{11,3},{12,20},{13... | collective-permute-start | bytes 1572872 | tf_op jit(solution)/shard_map/ppermute | solution.py:50
  33.1 2.6 %collective-permute-start.14 = (bf16[3,64,512]{2,1,0:T(8,128)(2,1)S(1)}, bf16[3,64,512]{2,1,0:T(8,128)(2,1)S(1)}, u32[]{:S(2)}, u32[]{:S(2)}) collective-permute-start(bf16[3,64,512]{2,1,0:T(8,128)(2,1)S(1)} %collective-permute-done.10.refs_1_), channel_id=1, source_target_pairs={{0,1},{1,0},{2,3},{3,2},{4,5},{5,4},{6,7},{7,6},{8,9},{9,8},{10,11... | collective-permute-start | bytes 589832 | tf_op jit(solution)/shard_map/ppermute | solution.py:184
  37.1 2.4 %collective-permute-done.4.got_ref.refs_1_ = bf16[128,2048]{1,0:T(8,128)(2,1)S(1)} collective-permute-done((bf16[128,2048]{1,0:T(8,128)(2,1)S(1)}, bf16[128,2048]{1,0:T(8,128)(2,1)S(1)}, u32[]{:S(2)}, u32[]{:S(2)}) %collective-permute-start.4) | collective-permute-done | bytes 524320 | tf_op jit(solution)/shard_map/ppermute | solution.py:50
  40.4 4.1 %collective-permute-start.19 = (bf16[128,2048]{1,0:T(8,128)(2,1)S(1)}, bf16[128,2048]{1,0:T(8,128)(2,1)S(1)}, u32[]{:S(2)}, u32[]{:S(2)}) collective-permute-start(bf16[128,2048]{1,0:T(8,128)(2,1)S(1)} %add_share.12), channel_id=1, source_target_pairs={{0,8},{2,10},{4,12},{6,14},{8,16},{9,1},{10,18},{11,3},{12,20},{13... | collective-permute-start | bytes 1572872 | tf_op jit(solution)/shard_map/ppermute | solution.py:50
  46.6 5.1 %collective-permute-start.22 = (bf16[128,2048]{1,0:T(8,128)(2,1)S(1)}, bf16[128,2048]{1,0:T(8,128)(2,1)S(1)}, u32[]{:S(2)}, u32[]{:S(2)}) collective-permute-start(bf16[128,2048]{1,0:T(8,128)(2,1)S(1)} %add_share.14), channel_id=1, source_target_pairs={{0,8},{2,10},{4,12},{6,14},{8,16},{9,1},{10,18},{11,3},{12,20},{13... | collective-permute-start | bytes 1572872 | tf_op jit(solution)/shard_map/ppermute | solution.py:50
  54.0 3.4 %collective-permute-done.17 = bf16[1,64,512]{2,1,0:T(8,128)(2,1)S(1)} collective-permute-done((bf16[1,64,512]{2,1,0:T(8,128)(2,1)S(1)}, bf16[1,64,512]{2,1,0:T(8,128)(2,1)S(1)}, u32[]{:S(2)}, u32[]{:S(2)}) %collective-permute-start.17) | collective-permute-done | bytes 65568 | tf_op jit(solution)/shard_map/ppermute | solution.py:184
  58.2 1.8 %collective-permute-done.18.got_ref.refs_8_ = bf16[128,2048]{1,0:T(8,128)(2,1)S(1)} collective-permute-done((bf16[128,2048]{1,0:T(8,128)(2,1)S(1)}, bf16[128,2048]{1,0:T(8,128)(2,1)S(1)}, u32[]{:S(2)}, u32[]{:S(2)}) %collective-permute-start.18) | collective-permute-done | bytes 524320 | tf_op jit(solution)/shard_map/ppermute | solution.py:50
  61.9 4.6 %collective-permute-start.27 = (bf16[128,2048]{1,0:T(8,128)(2,1)S(1)}, bf16[128,2048]{1,0:T(8,128)(2,1)S(1)}, u32[]{:S(2)}, u32[]{:S(2)}) collective-permute-start(bf16[128,2048]{1,0:T(8,128)(2,1)S(1)} %add_share.16), channel_id=1, source_target_pairs={{0,8},{2,10},{4,12},{6,14},{8,16},{9,1},{10,18},{11,3},{12,20},{13... | collective-permute-start | bytes 1572872 | tf_op jit(solution)/shard_map/ppermute | solution.py:50
  66.5 1.6 %collective-permute-done.22.got_ref.refs_3_ = bf16[128,2048]{1,0:T(8,128)(2,1)S(1)} collective-permute-done((bf16[128,2048]{1,0:T(8,128)(2,1)S(1)}, bf16[128,2048]{1,0:T(8,128)(2,1)S(1)}, u32[]{:S(2)}, u32[]{:S(2)}) %collective-permute-start.22) | collective-permute-done | bytes 524320 | tf_op jit(solution)/shard_map/ppermute | solution.py:50
  70.4 5.8 %collective-permute-start.25 = (bf16[128,2048]{1,0:T(8,128)(2,1)S(1)}, bf16[128,2048]{1,0:T(8,128)(2,1)S(1)}, u32[]{:S(2)}, u32[]{:S(2)}) collective-permute-start(bf16[128,2048]{1,0:T(8,128)(2,1)S(1)} %add_share.18), channel_id=1, source_target_pairs={{0,8},{2,10},{4,12},{6,14},{8,16},{9,1},{10,18},{11,3},{12,20},{13... | collective-permute-start | bytes 1572872 | tf_op jit(solution)/shard_map/ppermute | solution.py:50
  76.3 3.0 %collective-permute-done.27.got_ref.refs_4_ = bf16[128,2048]{1,0:T(8,128)(2,1)S(1)} collective-permute-done((bf16[128,2048]{1,0:T(8,128)(2,1)S(1)}, bf16[128,2048]{1,0:T(8,128)(2,1)S(1)}, u32[]{:S(2)}, u32[]{:S(2)}) %collective-permute-start.27) | collective-permute-done | bytes 524320 | tf_op jit(solution)/shard_map/ppermute | solution.py:50
  80.0 4.4 %collective-permute-start.30 = (bf16[128,2048]{1,0:T(8,128)(2,1)S(1)}, bf16[128,2048]{1,0:T(8,128)(2,1)S(1)}, u32[]{:S(2)}, u32[]{:S(2)}) collective-permute-start(bf16[128,2048]{1,0:T(8,128)(2,1)S(1)} %add_share.20), channel_id=1, source_target_pairs={{0,8},{2,10},{4,12},{6,14},{8,16},{9,1},{10,18},{11,3},{12,20},{13... | collective-permute-start | bytes 1572872 | tf_op jit(solution)/shard_map/ppermute | solution.py:50
  85.8 4.7 %collective-permute-done.25.got_ref.refs_5_ = bf16[128,2048]{1,0:T(8,128)(2,1)S(1)} collective-permute-done((bf16[128,2048]{1,0:T(8,128)(2,1)S(1)}, bf16[128,2048]{1,0:T(8,128)(2,1)S(1)}, u32[]{:S(2)}, u32[]{:S(2)}) %collective-permute-start.25) | collective-permute-done | bytes 524320 | tf_op jit(solution)/shard_map/ppermute | solution.py:50
  91.3 4.4 %collective-permute-start.28 = (bf16[128,2048]{1,0:T(8,128)(2,1)S(1)}, bf16[128,2048]{1,0:T(8,128)(2,1)S(1)}, u32[]{:S(2)}, u32[]{:S(2)}) collective-permute-start(bf16[128,2048]{1,0:T(8,128)(2,1)S(1)} %add_share.22), channel_id=1, source_target_pairs={{0,8},{2,10},{4,12},{6,14},{8,16},{9,1},{10,18},{11,3},{12,20},{13... | collective-permute-start | bytes 1572872 | tf_op jit(solution)/shard_map/ppermute | solution.py:50
  98.5 7.6 %weight_product.1 = bf16[1024,2048]{1,0:T(8,128)(2,1)} custom-call(bf16[256,1024]{1,0:T(8,128)(2,1)S(1)} %lay_strips.3.own_cot_ref, bf16[768,1024]{1,0:T(8,128)(2,1)S(1)} %lay_strips.2.cot_ref, bf16[256,2048]{1,0:T(8,128)(2,1)S(1)} %pad_maximum_fusion.own_ref, bf16[128,2048]{1,0:T(8,128)(2,1)S(1)} %collective-permute-done.6.got_ref.refs_0_, ...), custom_call_target="tpu_custom_call" | custom-call | flops 4294967296 | bytes 8388608 | tf_op jit(solution)/shard_map/weight_product/pallas_call | solution.py:129
  107.5 3.0 %collective-permute-done.29.refs_4_ = bf16[128,2048]{1,0:T(8,128)(2,1)S(1)} collective-permute-done((bf16[128,2048]{1,0:T(8,128)(2,1)S(1)}, bf16[128,2048]{1,0:T(8,128)(2,1)S(1)}, u32[]{:S(2)}, u32[]{:S(2)}) %collective-permute-start.29) | collective-permute-done | bytes 524320 | tf_op jit(solution)/shard_map/ppermute | solution.py:50
  (74 shorter events, 29.7 us)
Async XLA Ops:
  1.6 6.8 %collective-permute-start = (bf16[64,512]{1,0:T(8,128)(2,1)S(1)}, bf16[64,512]{1,0:T(8,128)(2,1)S(1)}, u32[]{:S(2)}, u32[]{:S(2)}) collective-permute-start(bf16[64,512]{1,0:T(8,128)(2,1)S(1)} %get-tuple-element.82), channel_id=1, source_target_pairs={{0,2},{1,3},{2,0},{3,1},{4,6},{5,7},{6,4},{7,5},{8,10},{9,11},{10,... | collective-permute-start | bytes 196616 | tf_op jit(solution)/shard_map/ppermute | solution.py:184
  11.4 10.3 %collective-permute-start.7 = (bf16[64,512]{1,0:T(8,128)(2,1)S(1)}, bf16[64,512]{1,0:T(8,128)(2,1)S(1)}, u32[]{:S(2)}, u32[]{:S(2)}) collective-permute-start(bf16[64,512]{1,0:T(8,128)(2,1)S(1)} %get-tuple-element.77), channel_id=1, source_target_pairs={{0,8},{8,0},{16,24},{24,16},{1,9},{9,1},{17,25},{25,17},{2,10},{10... | collective-permute-start | bytes 196616 | tf_op jit(solution)/shard_map/ppermute | solution.py:215
  13.0 8.7 %collective-permute-start.8 = (bf16[64,512]{1,0:T(8,128)(2,1)S(1)}, bf16[64,512]{1,0:T(8,128)(2,1)S(1)}, u32[]{:S(2)}, u32[]{:S(2)}) collective-permute-start(bf16[64,512]{1,0:T(8,128)(2,1)S(1)} %get-tuple-element.79), channel_id=1, source_target_pairs={{0,16},{8,24},{16,0},{24,8},{1,17},{9,25},{17,1},{25,9},{2,18},{10... | collective-permute-start | bytes 196616 | tf_op jit(solution)/shard_map/ppermute | solution.py:215
  15.9 17.2 %collective-permute-start.5 = (bf16[128,2048]{1,0:T(8,128)(2,1)S(1)}, bf16[128,2048]{1,0:T(8,128)(2,1)S(1)}, u32[]{:S(2)}, u32[]{:S(2)}) collective-permute-start(bf16[128,2048]{1,0:T(8,128)(2,1)S(1)} %get-tuple-element.68), channel_id=1, source_target_pairs={{1,9},{3,11},{5,13},{7,15},{8,0},{9,17},{10,2},{11,19},{12,4},{13,... | collective-permute-start | bytes 1572872 | tf_op jit(solution)/shard_map/ppermute | solution.py:50
  17.1 18.6 %collective-permute-start.6 = (bf16[128,2048]{1,0:T(8,128)(2,1)S(1)}, bf16[128,2048]{1,0:T(8,128)(2,1)S(1)}, u32[]{:S(2)}, u32[]{:S(2)}) collective-permute-start(bf16[128,2048]{1,0:T(8,128)(2,1)S(1)} %get-tuple-element.68), channel_id=1, source_target_pairs={{0,8},{2,10},{4,12},{6,14},{8,16},{9,1},{10,18},{11,3},{12,20},{13... | collective-permute-start | bytes 1572872 | tf_op jit(solution)/shard_map/ppermute | solution.py:50
  21.8 6.9 %collective-permute-start.12 = (bf16[3,64,512]{2,1,0:T(8,128)(2,1)S(1)}, bf16[3,64,512]{2,1,0:T(8,128)(2,1)S(1)}, u32[]{:S(2)}, u32[]{:S(2)}) collective-permute-start(bf16[3,64,512]{2,1,0:T(8,128)(2,1)S(1)} %pad_maximum_fusion.3.refs_0_), channel_id=1, source_target_pairs={{0,6},{1,7},{2,4},{3,5},{4,2},{5,3},{6,0},{7,1},{8,14},{9,15},{10,... | collective-permute-start | bytes 589832 | tf_op jit(solution)/shard_map/ppermute | solution.py:184
  22.4 8.7 %collective-permute-start.10 = (bf16[3,64,512]{2,1,0:T(8,128)(2,1)S(1)}, bf16[3,64,512]{2,1,0:T(8,128)(2,1)S(1)}, u32[]{:S(2)}, u32[]{:S(2)}) collective-permute-start(bf16[3,64,512]{2,1,0:T(8,128)(2,1)S(1)} %pad_maximum_fusion.3.refs_0_), channel_id=1, source_target_pairs={{0,2},{1,3},{2,0},{3,1},{4,6},{5,7},{6,4},{7,5},{8,10},{9,11},{10,... | collective-permute-start | bytes 589832 | tf_op jit(solution)/shard_map/ppermute | solution.py:184
  23.9 7.3 %collective-permute-start.11 = (bf16[3,64,512]{2,1,0:T(8,128)(2,1)S(1)}, bf16[3,64,512]{2,1,0:T(8,128)(2,1)S(1)}, u32[]{:S(2)}, u32[]{:S(2)}) collective-permute-start(bf16[3,64,512]{2,1,0:T(8,128)(2,1)S(1)} %pad_maximum_fusion.3.refs_0_), channel_id=1, source_target_pairs={{0,4},{1,5},{2,6},{3,7},{4,0},{5,1},{6,2},{7,3},{8,12},{9,13},{10,... | collective-permute-start | bytes 589832 | tf_op jit(solution)/shard_map/ppermute | solution.py:184
  28.8 10.7 %collective-permute-start.4 = (bf16[128,2048]{1,0:T(8,128)(2,1)S(1)}, bf16[128,2048]{1,0:T(8,128)(2,1)S(1)}, u32[]{:S(2)}, u32[]{:S(2)}) collective-permute-start(bf16[128,2048]{1,0:T(8,128)(2,1)S(1)} %get-tuple-element.67), channel_id=1, source_target_pairs={{0,8},{2,10},{4,12},{6,14},{8,16},{9,1},{10,18},{11,3},{12,20},{13... | collective-permute-start | bytes 1572872 | tf_op jit(solution)/shard_map/ppermute | solution.py:50
  31.2 20.5 %collective-permute-start.3 = (bf16[128,2048]{1,0:T(8,128)(2,1)S(1)}, bf16[128,2048]{1,0:T(8,128)(2,1)S(1)}, u32[]{:S(2)}, u32[]{:S(2)}) collective-permute-start(bf16[128,2048]{1,0:T(8,128)(2,1)S(1)} %get-tuple-element.67), channel_id=1, source_target_pairs={{1,9},{3,11},{5,13},{7,15},{8,0},{9,17},{10,2},{11,19},{12,4},{13,... | collective-permute-start | bytes 1572872 | tf_op jit(solution)/shard_map/ppermute | solution.py:50
  40.4 17.0 %collective-permute-start.19 = (bf16[128,2048]{1,0:T(8,128)(2,1)S(1)}, bf16[128,2048]{1,0:T(8,128)(2,1)S(1)}, u32[]{:S(2)}, u32[]{:S(2)}) collective-permute-start(bf16[128,2048]{1,0:T(8,128)(2,1)S(1)} %add_share.12), channel_id=1, source_target_pairs={{0,8},{2,10},{4,12},{6,14},{8,16},{9,1},{10,18},{11,3},{12,20},{13... | collective-permute-start | bytes 1572872 | tf_op jit(solution)/shard_map/ppermute | solution.py:50
  44.6 15.4 %collective-permute-start.18 = (bf16[128,2048]{1,0:T(8,128)(2,1)S(1)}, bf16[128,2048]{1,0:T(8,128)(2,1)S(1)}, u32[]{:S(2)}, u32[]{:S(2)}) collective-permute-start(bf16[128,2048]{1,0:T(8,128)(2,1)S(1)} %add_share.13), channel_id=1, source_target_pairs={{1,9},{3,11},{5,13},{7,15},{8,0},{9,17},{10,2},{11,19},{12,4},{13,... | collective-permute-start | bytes 1572872 | tf_op jit(solution)/shard_map/ppermute | solution.py:50
  46.6 21.4 %collective-permute-start.22 = (bf16[128,2048]{1,0:T(8,128)(2,1)S(1)}, bf16[128,2048]{1,0:T(8,128)(2,1)S(1)}, u32[]{:S(2)}, u32[]{:S(2)}) collective-permute-start(bf16[128,2048]{1,0:T(8,128)(2,1)S(1)} %add_share.14), channel_id=1, source_target_pairs={{0,8},{2,10},{4,12},{6,14},{8,16},{9,1},{10,18},{11,3},{12,20},{13... | collective-permute-start | bytes 1572872 | tf_op jit(solution)/shard_map/ppermute | solution.py:50
  51.8 17.0 %collective-permute-start.21 = (bf16[128,2048]{1,0:T(8,128)(2,1)S(1)}, bf16[128,2048]{1,0:T(8,128)(2,1)S(1)}, u32[]{:S(2)}, u32[]{:S(2)}) collective-permute-start(bf16[128,2048]{1,0:T(8,128)(2,1)S(1)} %add_share.15), channel_id=1, source_target_pairs={{1,9},{3,11},{5,13},{7,15},{8,0},{9,17},{10,2},{11,19},{12,4},{13,... | collective-permute-start | bytes 1572872 | tf_op jit(solution)/shard_map/ppermute | solution.py:50
  60.0 8.9 %collective-permute-start.20 = (bf16[2,64,512]{2,1,0:T(8,128)(2,1)S(1)}, bf16[2,64,512]{2,1,0:T(8,128)(2,1)S(1)}, u32[]{:S(2)}, u32[]{:S(2)}) collective-permute-start(bf16[2,64,512]{2,1,0:T(8,128)(2,1)S(1)} %pad_maximum_fusion.4), channel_id=1, source_target_pairs={{0,4},{1,5},{2,6},{3,7},{4,0},{5,1},{6,2},{7,3},{8,12},{9,13},{10,... | collective-permute-start | bytes 393224 | tf_op jit(solution)/shard_map/ppermute | solution.py:184
  60.6 23.8 %collective-permute-start.26 = (bf16[128,2048]{1,0:T(8,128)(2,1)S(1)}, bf16[128,2048]{1,0:T(8,128)(2,1)S(1)}, u32[]{:S(2)}, u32[]{:S(2)}) collective-permute-start(bf16[128,2048]{1,0:T(8,128)(2,1)S(1)} %add_share.17), channel_id=1, source_target_pairs={{1,9},{3,11},{5,13},{7,15},{8,0},{9,17},{10,2},{11,19},{12,4},{13,... | collective-permute-start | bytes 1572872 | tf_op jit(solution)/shard_map/ppermute | solution.py:50
  61.9 17.4 %collective-permute-start.27 = (bf16[128,2048]{1,0:T(8,128)(2,1)S(1)}, bf16[128,2048]{1,0:T(8,128)(2,1)S(1)}, u32[]{:S(2)}, u32[]{:S(2)}) collective-permute-start(bf16[128,2048]{1,0:T(8,128)(2,1)S(1)} %add_share.16), channel_id=1, source_target_pairs={{0,8},{2,10},{4,12},{6,14},{8,16},{9,1},{10,18},{11,3},{12,20},{13... | collective-permute-start | bytes 1572872 | tf_op jit(solution)/shard_map/ppermute | solution.py:50
  68.9 7.3 %collective-permute-start.23 = (bf16[4,64,512]{2,1,0:T(8,128)(2,1)S(1)}, bf16[4,64,512]{2,1,0:T(8,128)(2,1)S(1)}, u32[]{:S(2)}, u32[]{:S(2)}) collective-permute-start(bf16[4,64,512]{2,1,0:T(8,128)(2,1)S(1)} %pad_maximum_fusion.2), channel_id=1, source_target_pairs={{0,1},{1,0},{2,3},{3,2},{4,5},{5,4},{6,7},{7,6},{8,9},{9,8},{10,11... | collective-permute-start | bytes 786440 | tf_op jit(solution)/shard_map/ppermute | solution.py:184
  69.1 26.6 %collective-permute-start.24 = (bf16[128,2048]{1,0:T(8,128)(2,1)S(1)}, bf16[128,2048]{1,0:T(8,128)(2,1)S(1)}, u32[]{:S(2)}, u32[]{:S(2)}) collective-permute-start(bf16[128,2048]{1,0:T(8,128)(2,1)S(1)} %add_share.19), channel_id=1, source_target_pairs={{1,9},{3,11},{5,13},{7,15},{8,0},{9,17},{10,2},{11,19},{12,4},{13,... | collective-permute-start | bytes 1572872 | tf_op jit(solution)/shard_map/ppermute | solution.py:50
  70.4 20.2 %collective-permute-start.25 = (bf16[128,2048]{1,0:T(8,128)(2,1)S(1)}, bf16[128,2048]{1,0:T(8,128)(2,1)S(1)}, u32[]{:S(2)}, u32[]{:S(2)}) collective-permute-start(bf16[128,2048]{1,0:T(8,128)(2,1)S(1)} %add_share.18), channel_id=1, source_target_pairs={{0,8},{2,10},{4,12},{6,14},{8,16},{9,1},{10,18},{11,3},{12,20},{13... | collective-permute-start | bytes 1572872 | tf_op jit(solution)/shard_map/ppermute | solution.py:50
  80.0 26.1 %collective-permute-start.30 = (bf16[128,2048]{1,0:T(8,128)(2,1)S(1)}, bf16[128,2048]{1,0:T(8,128)(2,1)S(1)}, u32[]{:S(2)}, u32[]{:S(2)}) collective-permute-start(bf16[128,2048]{1,0:T(8,128)(2,1)S(1)} %add_share.20), channel_id=1, source_target_pairs={{0,8},{2,10},{4,12},{6,14},{8,16},{9,1},{10,18},{11,3},{12,20},{13... | collective-permute-start | bytes 1572872 | tf_op jit(solution)/shard_map/ppermute | solution.py:50
  84.5 21.6 %collective-permute-start.31 = (bf16[128,2048]{1,0:T(8,128)(2,1)S(1)}, bf16[128,2048]{1,0:T(8,128)(2,1)S(1)}, u32[]{:S(2)}, u32[]{:S(2)}) collective-permute-start(bf16[128,2048]{1,0:T(8,128)(2,1)S(1)} %add_share.21), channel_id=1, source_target_pairs={{1,9},{3,11},{5,13},{7,15},{8,0},{9,17},{10,2},{11,19},{12,4},{13,... | collective-permute-start | bytes 1572872 | tf_op jit(solution)/shard_map/ppermute | solution.py:50
  91.3 20.3 %collective-permute-start.28 = (bf16[128,2048]{1,0:T(8,128)(2,1)S(1)}, bf16[128,2048]{1,0:T(8,128)(2,1)S(1)}, u32[]{:S(2)}, u32[]{:S(2)}) collective-permute-start(bf16[128,2048]{1,0:T(8,128)(2,1)S(1)} %add_share.22), channel_id=1, source_target_pairs={{0,8},{2,10},{4,12},{6,14},{8,16},{9,1},{10,18},{11,3},{12,20},{13... | collective-permute-start | bytes 1572872 | tf_op jit(solution)/shard_map/ppermute | solution.py:50
  95.9 14.6 %collective-permute-start.29 = (bf16[128,2048]{1,0:T(8,128)(2,1)S(1)}, bf16[128,2048]{1,0:T(8,128)(2,1)S(1)}, u32[]{:S(2)}, u32[]{:S(2)}) collective-permute-start(bf16[128,2048]{1,0:T(8,128)(2,1)S(1)} %add_share.23), channel_id=1, source_target_pairs={{1,9},{3,11},{5,13},{7,15},{8,0},{9,17},{10,2},{11,19},{12,4},{13,... | collective-permute-start | bytes 1572872 | tf_op jit(solution)/shard_map/ppermute | solution.py:50
  (11 other events, 77.1 us)

commit v2 on v1

--- a/solution.py
+++ b/solution.py
@@ -140,25 +140,28 @@
     )(own_cot, cot, own, *flat)
 
 
-def finish(gate_pre, up_pre, share, fore, back, start, grads):
+def factors_of(gate_value, up_value):
+    gate_value, up_value = gate_value.astype(jnp.float32), up_value.astype(jnp.float32)
+    gate_sigmoid = jax.nn.sigmoid(gate_value)
+    return up_value * (gate_sigmoid * (1.0 + gate_value * (1.0 - gate_sigmoid))), gate_value * gate_sigmoid
+
+
+def finish(sources, ready, share, fore, back, start, grads):
     span, width = fore.shape
     tile = 512 if width % 512 == 0 else width
     old = () if grads is None else tuple(grads)
 
     def kernel(*refs):
-        gate_ref, up_ref, share_ref, fore_ref, back_ref = refs[:5]
+        source_refs, (share_ref, fore_ref, back_ref) = refs[:2], refs[2:5]
         outs, parts, sems = refs[5 + len(old) : 7 + len(old)], refs[-3:-1], refs[-1]
         here = slice(start, start + span)
         copies = []
         for at in range(0, width, tile):
             cut = slice(at, at + tile)
             grad = share_ref[here, cut] + fore_ref[:, cut].astype(jnp.float32) + back_ref[:, cut].astype(jnp.float32)
-            gate = gate_ref[here, cut].astype(jnp.float32)
-            sigmoid = jax.nn.sigmoid(gate)
-            slope = sigmoid * (1.0 + gate * (1.0 - sigmoid))
-            parts[0][:, cut] = (grad * up_ref[here, cut].astype(jnp.float32) * slope).astype(jnp.bfloat16)
-            parts[1][:, cut] = (grad * (gate * sigmoid)).astype(jnp.bfloat16)
-            for which, (part, out) in enumerate(zip(parts, outs)):
+            factors = [ref[:, cut] for ref in source_refs] if ready else factors_of(*(ref[here, cut] for ref in source_refs))
+            for which, (factor, part, out) in enumerate(zip(factors, parts, outs)):
+                part[:, cut] = (grad * factor).astype(jnp.bfloat16)
                 copy = pltpu.make_async_copy(part.at[:, cut], out.at[here, cut], sems.at[which, at // tile])
                 copy.start()
                 copies.append(copy)
@@ -168,7 +171,7 @@
     whole, anywhere = pl.BlockSpec(memory_space=pltpu.VMEM), pl.BlockSpec(memory_space=pl.ANY)
     return pl.pallas_call(
         kernel,
-        out_shape=[jax.ShapeDtypeStruct(gate_pre.shape, jnp.bfloat16)] * 2,
+        out_shape=[jax.ShapeDtypeStruct(share.shape, jnp.bfloat16)] * 2,
         in_specs=[whole] * 5 + [anywhere] * len(old),
         out_specs=[anywhere] * 2,
         scratch_shapes=[pltpu.VMEM((span, width), jnp.bfloat16)] * 2
@@ -177,7 +180,7 @@
         compiler_params=pltpu.CompilerParams(vmem_limit_bytes=32 * 2**20),
         cost_estimate=pl.CostEstimate(flops=20 * span * width, bytes_accessed=8 * span * width, transcendentals=span * width),
         name="finish",
-    )(gate_pre, up_pre, share, fore, back, *old)
+    )(*sources, share, fore, back, *old)
 
 
 def swap(value, bits):
@@ -217,9 +220,10 @@
     tall = [across(bits) for bits in range(rows - 1, -1, -1)]
     own, tall = tall[-1], jnp.stack(tall[-2::-1])
     near = [tall, swap(tall, 2), swap(tall, 4), swap(tall, 6)]
-    near[3] = after(near[3], first)
+    near[0] = after(near[0], [first[0]])
+    near[1] = after(near[1], [first[1]])
     far = [swap(block, 1) for block in near]
-    far = after(far, second[0])
+    far[3] = after(far[3], [second[0]])
 
     own = own[None]
 
@@ -268,10 +272,14 @@
     weight_grad = weight_product(own_cot, cot, jnp.concatenate(hidden), [steps[:-1] for steps in ways], norm_scale)
 
     own_share = jnp.dot(after(own_cot, late), down_t, preferred_element_type=jnp.float32)
+    last, count = chains[-1]
+    factors = factors_of(*(value[last : last + count] for value in after((gate_pre, up_pre), late)))
     own_share, gate_again, up_again = after((own_share, gate_pre, up_pre), turn)
     grads = None
     for at, (first, _) in enumerate(chains):
-        grads = finish(gate_again, up_again, own_share, ways[0][-1][at], ways[1][-1][at], first, grads)
+        ready = first == last
+        sources = factors if ready else (gate_again, up_again)
+        grads = finish(sources, ready, own_share, ways[0][-1][at], ways[1][-1][at], first, grads)
     return *grads, weight_grad
 
 

time: 114 us -> 115 us (level)
  waiting for transfers between devices: 28.7 us -> 35.1 us
  starting transfers between devices: 62.9 us -> 58.2 us
    ppermute x3, waiting for transfers between devices: 0.06 us -> 4.58 us  [across(): lax.ppermute(piece, 'row', [(at, at ^ bits) for at in range(rows)])]
    ppermute x16, waiting for transfers between devices: 18 us -> 22.3 us  [ring(): return lax.ppermute(value, ('row', 'col'), pairs)]
    ppermute x16, starting transfers between devices: 45.6 us -> 41.8 us  [ring(): return lax.ppermute(value, ('row', 'col'), pairs)]
    ppermute x13, waiting for transfers between devices: 10.7 us -> 8.22 us  [swap(): lax.ppermute(value, 'col', [(at, at ^ bits) for at in range(lax.axis_size...]
  transfers between devices with their start and end apart: 32 -> 32, of which waited for: 15 -> 14; matrix products, arithmetic and copies ran while one was open for 3% -> 4% of each run, Pallas kernels for 12% -> 12%
where the time goes in v2:
time: 115 us
  starting transfers between devices  58.2 us (51%)
  waiting for transfers between devices  35.1 us (31%)
  Pallas kernels  15.2 us (13%)
  other arithmetic  2.82 us (2%)
  between operations  1.33 us (1%)
  matrix products  1.25 us (1%)
    ppermute x16, starting transfers between devices, ring(): return lax.ppermute(value, ('row', 'col'), pairs)  41.8 us
    ppermute x16, waiting for transfers between devices, ring(): return lax.ppermute(value, ('row', 'col'), pairs)  22.3 us
    ppermute x13, starting transfers between devices, swap(): lax.ppermute(value, 'col', [(at, at ^ bits) for at in range(lax.axis_size...  11.9 us
    ppermute x13, waiting for transfers between devices, swap(): lax.ppermute(value, 'col', [(at, at ^ bits) for at in range(lax.axis_size...  8.22 us
    pallas_call x1, Pallas kernels, weight_product(): pl.pallas_call(kernel, out_shape=jax.ShapeDtypeStruct((cot.shape[1], widt...  7.6 us
    pallas_call x12, Pallas kernels, add_share(): pl.pallas_call(kernel, out_shape=jax.ShapeDtypeStruct(got.shape, got.dtyp...  4.86 us
    ppermute x3, waiting for transfers between devices, across(): lax.ppermute(piece, 'row', [(at, at ^ bits) for at in range(rows)])  4.58 us
    ppermute x3, starting transfers between devices, across(): lax.ppermute(piece, 'row', [(at, at ^ bits) for at in range(rows)])  4.45 us
  transfers between devices with their start and end apart: 32, of which 14 were waited for; matrix products, arithmetic and copies ran while one was open for 4% of the time, Pallas kernels for 12%

profile of v2, /device:TPU:0, one launch (start us, length us, event | category | flops | bytes accessed | tf_op | source)
XLA Modules:
  0.0 114.9 jit_solution(11605376777962293255)
XLA Ops:
  1.6 3.0 %collective-permute-start.4 = (bf16[64,512]{1,0:T(8,128)(2,1)S(1)}, bf16[64,512]{1,0:T(8,128)(2,1)S(1)}, u32[]{:S(2)}, u32[]{:S(2)}) collective-permute-start(bf16[64,512]{1,0:T(8,128)(2,1)S(1)} %get-tuple-element.84), channel_id=1, source_target_pairs={{0,2},{1,3},{2,0},{3,1},{4,6},{5,7},{6,4},{7,5},{8,10},{9,11},{10,... | collective-permute-start | bytes 196616 | tf_op jit(solution)/shard_map/ppermute | solution.py:187
  6.2 2.2 %fusion.14 = (bf16[128,2048]{1,0:T(8,128)(2,1)S(1)}, bf16[128,2048]{1,0:T(8,128)(2,1)S(1)}) fusion(bf16[256,2048]{1,0:T(8,128)(2,1)} %refs_1_, bf16[256,2048]{1,0:T(8,128)(2,1)} %refs_0_), kind=kLoop, calls=%fused_computation.22 | loop fusion | flops 4194304 | bytes 3145728 | tf_op jit(solution)/shard_map/convert_element_type | solution.py:253
  8.9 2.4 %collective-permute-done.6 = bf16[64,512]{1,0:T(8,128)(2,1)S(1)} collective-permute-done((bf16[64,512]{1,0:T(8,128)(2,1)S(1)}, bf16[64,512]{1,0:T(8,128)(2,1)S(1)}, u32[]{:S(2)}, u32[]{:S(2)}) %collective-permute-start.6) | collective-permute-done | bytes 65568 | tf_op jit(solution)/shard_map/ppermute | solution.py:187
  11.4 1.6 %collective-permute-start.7 = (bf16[64,512]{1,0:T(8,128)(2,1)S(1)}, bf16[64,512]{1,0:T(8,128)(2,1)S(1)}, u32[]{:S(2)}, u32[]{:S(2)}) collective-permute-start(bf16[64,512]{1,0:T(8,128)(2,1)S(1)} %get-tuple-element.82), channel_id=1, source_target_pairs={{0,8},{8,0},{16,24},{24,16},{1,9},{9,1},{17,25},{25,17},{2,10},{10... | collective-permute-start | bytes 196616 | tf_op jit(solution)/shard_map/ppermute | solution.py:218
  13.0 2.6 %collective-permute-start.8 = (bf16[64,512]{1,0:T(8,128)(2,1)S(1)}, bf16[64,512]{1,0:T(8,128)(2,1)S(1)}, u32[]{:S(2)}, u32[]{:S(2)}) collective-permute-start(bf16[64,512]{1,0:T(8,128)(2,1)S(1)} %get-tuple-element.81), channel_id=1, source_target_pairs={{0,16},{8,24},{16,0},{24,8},{1,17},{9,25},{17,1},{25,9},{2,18},{10... | collective-permute-start | bytes 196616 | tf_op jit(solution)/shard_map/ppermute | solution.py:218
  17.2 2.5 %collective-permute-done.8 = bf16[64,512]{1,0:T(8,128)(2,1)S(1)} collective-permute-done((bf16[64,512]{1,0:T(8,128)(2,1)S(1)}, bf16[64,512]{1,0:T(8,128)(2,1)S(1)}, u32[]{:S(2)}, u32[]{:S(2)}) %collective-permute-start.8) | collective-permute-done | bytes 65568 | tf_op jit(solution)/shard_map/ppermute | solution.py:218
  19.6 2.1 %collective-permute-done.9 = bf16[64,512]{1,0:T(8,128)(2,1)S(1)} collective-permute-done((bf16[64,512]{1,0:T(8,128)(2,1)S(1)}, bf16[64,512]{1,0:T(8,128)(2,1)S(1)}, u32[]{:S(2)}, u32[]{:S(2)}) %collective-permute-start.9) | collective-permute-done | bytes 65568 | tf_op jit(solution)/shard_map/ppermute | solution.py:218
  22.3 1.7 %collective-permute-start.3 = (bf16[128,2048]{1,0:T(8,128)(2,1)S(1)}, bf16[128,2048]{1,0:T(8,128)(2,1)S(1)}, u32[]{:S(2)}, u32[]{:S(2)}) collective-permute-start(bf16[128,2048]{1,0:T(8,128)(2,1)S(1)} %get-tuple-element.67), channel_id=1, source_target_pairs={{0,8},{2,10},{4,12},{6,14},{8,16},{9,1},{10,18},{11,3},{12,20},{13... | collective-permute-start | bytes 1572872 | tf_op jit(solution)/shard_map/ppermute | solution.py:50
  26.7 2.0 %collective-permute-done.12.refs_3_ = bf16[3,64,512]{2,1,0:T(8,128)(2,1)S(1)} collective-permute-done((bf16[3,64,512]{2,1,0:T(8,128)(2,1)S(1)}, bf16[3,64,512]{2,1,0:T(8,128)(2,1)S(1)}, u32[]{:S(2)}, u32[]{:S(2)}) %collective-permute-start.12) | collective-permute-done | bytes 196640 | tf_op jit(solution)/shard_map/ppermute | solution.py:187
  28.7 2.5 %collective-permute-start.1 = (bf16[128,2048]{1,0:T(8,128)(2,1)S(1)}, bf16[128,2048]{1,0:T(8,128)(2,1)S(1)}, u32[]{:S(2)}, u32[]{:S(2)}) collective-permute-start(bf16[128,2048]{1,0:T(8,128)(2,1)S(1)} %get-tuple-element.68), channel_id=1, source_target_pairs={{0,8},{2,10},{4,12},{6,14},{8,16},{9,1},{10,18},{11,3},{12,20},{13... | collective-permute-start | bytes 1572872 | tf_op jit(solution)/shard_map/ppermute | solution.py:50
  32.5 2.2 %collective-permute-start.15 = (bf16[3,64,512]{2,1,0:T(8,128)(2,1)S(1)}, bf16[3,64,512]{2,1,0:T(8,128)(2,1)S(1)}, u32[]{:S(2)}, u32[]{:S(2)}) collective-permute-start(bf16[3,64,512]{2,1,0:T(8,128)(2,1)S(1)} %collective-permute-done.11.refs_2_), channel_id=1, source_target_pairs={{0,1},{1,0},{2,3},{3,2},{4,5},{5,4},{6,7},{7,6},{8,9},{9,8},{10,11... | collective-permute-start | bytes 589832 | tf_op jit(solution)/shard_map/ppermute | solution.py:187
  35.2 5.3 %collective-permute-done.1.got_ref.refs_1_ = bf16[128,2048]{1,0:T(8,128)(2,1)S(1)} collective-permute-done((bf16[128,2048]{1,0:T(8,128)(2,1)S(1)}, bf16[128,2048]{1,0:T(8,128)(2,1)S(1)}, u32[]{:S(2)}, u32[]{:S(2)}) %collective-permute-start.1) | collective-permute-done | bytes 524320 | tf_op jit(solution)/shard_map/ppermute | solution.py:50
  41.5 3.7 %collective-permute-start.20 = (bf16[128,2048]{1,0:T(8,128)(2,1)S(1)}, bf16[128,2048]{1,0:T(8,128)(2,1)S(1)}, u32[]{:S(2)}, u32[]{:S(2)}) collective-permute-start(bf16[128,2048]{1,0:T(8,128)(2,1)S(1)} %add_share.12), channel_id=1, source_target_pairs={{0,8},{2,10},{4,12},{6,14},{8,16},{9,1},{10,18},{11,3},{12,20},{13... | collective-permute-start | bytes 1572872 | tf_op jit(solution)/shard_map/ppermute | solution.py:50
  47.3 3.9 %collective-permute-start.18 = (bf16[128,2048]{1,0:T(8,128)(2,1)S(1)}, bf16[128,2048]{1,0:T(8,128)(2,1)S(1)}, u32[]{:S(2)}, u32[]{:S(2)}) collective-permute-start(bf16[128,2048]{1,0:T(8,128)(2,1)S(1)} %add_share.14), channel_id=1, source_target_pairs={{0,8},{2,10},{4,12},{6,14},{8,16},{9,1},{10,18},{11,3},{12,20},{13... | collective-permute-start | bytes 1572872 | tf_op jit(solution)/shard_map/ppermute | solution.py:50
  53.6 3.3 %collective-permute-done.25 = bf16[1,64,512]{2,1,0:T(8,128)(2,1)S(1)} collective-permute-done((bf16[1,64,512]{2,1,0:T(8,128)(2,1)S(1)}, bf16[1,64,512]{2,1,0:T(8,128)(2,1)S(1)}, u32[]{:S(2)}, u32[]{:S(2)}) %collective-permute-start.25) | collective-permute-done | bytes 65568 | tf_op jit(solution)/shard_map/ppermute | solution.py:187
  58.1 3.9 %collective-permute-done.19.got_ref.refs_8_ = bf16[128,2048]{1,0:T(8,128)(2,1)S(1)} collective-permute-done((bf16[128,2048]{1,0:T(8,128)(2,1)S(1)}, bf16[128,2048]{1,0:T(8,128)(2,1)S(1)}, u32[]{:S(2)}, u32[]{:S(2)}) %collective-permute-start.19) | collective-permute-done | bytes 524320 | tf_op jit(solution)/shard_map/ppermute | solution.py:50
  63.4 4.6 %collective-permute-start.24 = (bf16[128,2048]{1,0:T(8,128)(2,1)S(1)}, bf16[128,2048]{1,0:T(8,128)(2,1)S(1)}, u32[]{:S(2)}, u32[]{:S(2)}) collective-permute-start(bf16[128,2048]{1,0:T(8,128)(2,1)S(1)} %add_share.16), channel_id=1, source_target_pairs={{0,8},{2,10},{4,12},{6,14},{8,16},{9,1},{10,18},{11,3},{12,20},{13... | collective-permute-start | bytes 1572872 | tf_op jit(solution)/shard_map/ppermute | solution.py:50
  71.1 5.0 %collective-permute-start.22 = (bf16[128,2048]{1,0:T(8,128)(2,1)S(1)}, bf16[128,2048]{1,0:T(8,128)(2,1)S(1)}, u32[]{:S(2)}, u32[]{:S(2)}) collective-permute-start(bf16[128,2048]{1,0:T(8,128)(2,1)S(1)} %add_share.18), channel_id=1, source_target_pairs={{0,8},{2,10},{4,12},{6,14},{8,16},{9,1},{10,18},{11,3},{12,20},{13... | collective-permute-start | bytes 1572872 | tf_op jit(solution)/shard_map/ppermute | solution.py:50
  76.2 4.1 %collective-permute-done.24.got_ref.refs_4_ = bf16[128,2048]{1,0:T(8,128)(2,1)S(1)} collective-permute-done((bf16[128,2048]{1,0:T(8,128)(2,1)S(1)}, bf16[128,2048]{1,0:T(8,128)(2,1)S(1)}, u32[]{:S(2)}, u32[]{:S(2)}) %collective-permute-start.24) | collective-permute-done | bytes 524320 | tf_op jit(solution)/shard_map/ppermute | solution.py:50
  81.0 4.4 %collective-permute-start.30 = (bf16[128,2048]{1,0:T(8,128)(2,1)S(1)}, bf16[128,2048]{1,0:T(8,128)(2,1)S(1)}, u32[]{:S(2)}, u32[]{:S(2)}) collective-permute-start(bf16[128,2048]{1,0:T(8,128)(2,1)S(1)} %add_share.20), channel_id=1, source_target_pairs={{0,8},{2,10},{4,12},{6,14},{8,16},{9,1},{10,18},{11,3},{12,20},{13... | collective-permute-start | bytes 1572872 | tf_op jit(solution)/shard_map/ppermute | solution.py:50
  86.8 4.7 %collective-permute-done.22.got_ref.refs_5_ = bf16[128,2048]{1,0:T(8,128)(2,1)S(1)} collective-permute-done((bf16[128,2048]{1,0:T(8,128)(2,1)S(1)}, bf16[128,2048]{1,0:T(8,128)(2,1)S(1)}, u32[]{:S(2)}, u32[]{:S(2)}) %collective-permute-start.22) | collective-permute-done | bytes 524320 | tf_op jit(solution)/shard_map/ppermute | solution.py:50
  93.8 5.7 %collective-permute-start.28 = (bf16[128,2048]{1,0:T(8,128)(2,1)S(1)}, bf16[128,2048]{1,0:T(8,128)(2,1)S(1)}, u32[]{:S(2)}, u32[]{:S(2)}) collective-permute-start(bf16[128,2048]{1,0:T(8,128)(2,1)S(1)} %add_share.22), channel_id=1, source_target_pairs={{0,8},{2,10},{4,12},{6,14},{8,16},{9,1},{10,18},{11,3},{12,20},{13... | collective-permute-start | bytes 1572872 | tf_op jit(solution)/shard_map/ppermute | solution.py:50
  100.8 7.6 %weight_product.1 = bf16[1024,2048]{1,0:T(8,128)(2,1)} custom-call(bf16[256,1024]{1,0:T(8,128)(2,1)S(1)} %lay_strips.3.own_cot_ref, bf16[768,1024]{1,0:T(8,128)(2,1)S(1)} %lay_strips.2.cot_ref, bf16[256,2048]{1,0:T(8,128)(2,1)S(1)} %pad_maximum_fusion.own_ref, bf16[128,2048]{1,0:T(8,128)(2,1)S(1)} %collective-permute-done.3.got_ref.refs_0_, ...), custom_call_target="tpu_custom_call" | custom-call | flops 4294967296 | bytes 8388608 | tf_op jit(solution)/shard_map/weight_product/pallas_call | solution.py:129
  110.3 2.2 %collective-permute-done.29.refs_4_ = bf16[128,2048]{1,0:T(8,128)(2,1)S(1)} collective-permute-done((bf16[128,2048]{1,0:T(8,128)(2,1)S(1)}, bf16[128,2048]{1,0:T(8,128)(2,1)S(1)}, u32[]{:S(2)}, u32[]{:S(2)}) %collective-permute-start.29) | collective-permute-done | bytes 524320 | tf_op jit(solution)/shard_map/ppermute | solution.py:50
  (75 shorter events, 30.5 us)
Async XLA Ops:
  1.6 6.8 %collective-permute-start.4 = (bf16[64,512]{1,0:T(8,128)(2,1)S(1)}, bf16[64,512]{1,0:T(8,128)(2,1)S(1)}, u32[]{:S(2)}, u32[]{:S(2)}) collective-permute-start(bf16[64,512]{1,0:T(8,128)(2,1)S(1)} %get-tuple-element.84), channel_id=1, source_target_pairs={{0,2},{1,3},{2,0},{3,1},{4,6},{5,7},{6,4},{7,5},{8,10},{9,11},{10,... | collective-permute-start | bytes 196616 | tf_op jit(solution)/shard_map/ppermute | solution.py:187
  13.0 6.6 %collective-permute-start.8 = (bf16[64,512]{1,0:T(8,128)(2,1)S(1)}, bf16[64,512]{1,0:T(8,128)(2,1)S(1)}, u32[]{:S(2)}, u32[]{:S(2)}) collective-permute-start(bf16[64,512]{1,0:T(8,128)(2,1)S(1)} %get-tuple-element.81), channel_id=1, source_target_pairs={{0,16},{8,24},{16,0},{24,8},{1,17},{9,25},{17,1},{25,9},{2,18},{10... | collective-permute-start | bytes 196616 | tf_op jit(solution)/shard_map/ppermute | solution.py:218
  15.6 6.1 %collective-permute-start.9 = (bf16[64,512]{1,0:T(8,128)(2,1)S(1)}, bf16[64,512]{1,0:T(8,128)(2,1)S(1)}, u32[]{:S(2)}, u32[]{:S(2)}) collective-permute-start(bf16[64,512]{1,0:T(8,128)(2,1)S(1)} %get-tuple-element.80), channel_id=1, source_target_pairs={{0,24},{8,16},{16,8},{24,0},{1,25},{9,17},{17,9},{25,1},{2,26},{10... | collective-permute-start | bytes 196616 | tf_op jit(solution)/shard_map/ppermute | solution.py:218
  15.9 16.7 %collective-permute-start.2 = (bf16[128,2048]{1,0:T(8,128)(2,1)S(1)}, bf16[128,2048]{1,0:T(8,128)(2,1)S(1)}, u32[]{:S(2)}, u32[]{:S(2)}) collective-permute-start(bf16[128,2048]{1,0:T(8,128)(2,1)S(1)} %get-tuple-element.67), channel_id=1, source_target_pairs={{1,9},{3,11},{5,13},{7,15},{8,0},{9,17},{10,2},{11,19},{12,4},{13,... | collective-permute-start | bytes 1572872 | tf_op jit(solution)/shard_map/ppermute | solution.py:50
  21.8 6.9 %collective-permute-start.12 = (bf16[3,64,512]{2,1,0:T(8,128)(2,1)S(1)}, bf16[3,64,512]{2,1,0:T(8,128)(2,1)S(1)}, u32[]{:S(2)}, u32[]{:S(2)}) collective-permute-start(bf16[3,64,512]{2,1,0:T(8,128)(2,1)S(1)} %pad_maximum_fusion.3.refs_0_), channel_id=1, source_target_pairs={{0,6},{1,7},{2,4},{3,5},{4,2},{5,3},{6,0},{7,1},{8,14},{9,15},{10,... | collective-permute-start | bytes 589832 | tf_op jit(solution)/shard_map/ppermute | solution.py:187
  22.3 12.4 %collective-permute-start.3 = (bf16[128,2048]{1,0:T(8,128)(2,1)S(1)}, bf16[128,2048]{1,0:T(8,128)(2,1)S(1)}, u32[]{:S(2)}, u32[]{:S(2)}) collective-permute-start(bf16[128,2048]{1,0:T(8,128)(2,1)S(1)} %get-tuple-element.67), channel_id=1, source_target_pairs={{0,8},{2,10},{4,12},{6,14},{8,16},{9,1},{10,18},{11,3},{12,20},{13... | collective-permute-start | bytes 1572872 | tf_op jit(solution)/shard_map/ppermute | solution.py:50
  24.0 7.1 %collective-permute-start.10 = (bf16[3,64,512]{2,1,0:T(8,128)(2,1)S(1)}, bf16[3,64,512]{2,1,0:T(8,128)(2,1)S(1)}, u32[]{:S(2)}, u32[]{:S(2)}) collective-permute-start(bf16[3,64,512]{2,1,0:T(8,128)(2,1)S(1)} %pad_maximum_fusion.3.refs_0_), channel_id=1, source_target_pairs={{0,2},{1,3},{2,0},{3,1},{4,6},{5,7},{6,4},{7,5},{8,10},{9,11},{10,... | collective-permute-start | bytes 589832 | tf_op jit(solution)/shard_map/ppermute | solution.py:187
  28.7 11.9 %collective-permute-start.1 = (bf16[128,2048]{1,0:T(8,128)(2,1)S(1)}, bf16[128,2048]{1,0:T(8,128)(2,1)S(1)}, u32[]{:S(2)}, u32[]{:S(2)}) collective-permute-start(bf16[128,2048]{1,0:T(8,128)(2,1)S(1)} %get-tuple-element.68), channel_id=1, source_target_pairs={{0,8},{2,10},{4,12},{6,14},{8,16},{9,1},{10,18},{11,3},{12,20},{13... | collective-permute-start | bytes 1572872 | tf_op jit(solution)/shard_map/ppermute | solution.py:50
  31.2 20.0 %collective-permute-start = (bf16[128,2048]{1,0:T(8,128)(2,1)S(1)}, bf16[128,2048]{1,0:T(8,128)(2,1)S(1)}, u32[]{:S(2)}, u32[]{:S(2)}) collective-permute-start(bf16[128,2048]{1,0:T(8,128)(2,1)S(1)} %get-tuple-element.68), channel_id=1, source_target_pairs={{1,9},{3,11},{5,13},{7,15},{8,0},{9,17},{10,2},{11,19},{12,4},{13,... | collective-permute-start | bytes 1572872 | tf_op jit(solution)/shard_map/ppermute | solution.py:50
  32.5 8.0 %collective-permute-start.15 = (bf16[3,64,512]{2,1,0:T(8,128)(2,1)S(1)}, bf16[3,64,512]{2,1,0:T(8,128)(2,1)S(1)}, u32[]{:S(2)}, u32[]{:S(2)}) collective-permute-start(bf16[3,64,512]{2,1,0:T(8,128)(2,1)S(1)} %collective-permute-done.11.refs_2_), channel_id=1, source_target_pairs={{0,1},{1,0},{2,3},{3,2},{4,5},{5,4},{6,7},{7,6},{8,9},{9,8},{10,11... | collective-permute-start | bytes 589832 | tf_op jit(solution)/shard_map/ppermute | solution.py:187
  41.5 15.9 %collective-permute-start.20 = (bf16[128,2048]{1,0:T(8,128)(2,1)S(1)}, bf16[128,2048]{1,0:T(8,128)(2,1)S(1)}, u32[]{:S(2)}, u32[]{:S(2)}) collective-permute-start(bf16[128,2048]{1,0:T(8,128)(2,1)S(1)} %add_share.12), channel_id=1, source_target_pairs={{0,8},{2,10},{4,12},{6,14},{8,16},{9,1},{10,18},{11,3},{12,20},{13... | collective-permute-start | bytes 1572872 | tf_op jit(solution)/shard_map/ppermute | solution.py:50
  45.3 16.7 %collective-permute-start.19 = (bf16[128,2048]{1,0:T(8,128)(2,1)S(1)}, bf16[128,2048]{1,0:T(8,128)(2,1)S(1)}, u32[]{:S(2)}, u32[]{:S(2)}) collective-permute-start(bf16[128,2048]{1,0:T(8,128)(2,1)S(1)} %add_share.13), channel_id=1, source_target_pairs={{1,9},{3,11},{5,13},{7,15},{8,0},{9,17},{10,2},{11,19},{12,4},{13,... | collective-permute-start | bytes 1572872 | tf_op jit(solution)/shard_map/ppermute | solution.py:50
  47.3 21.3 %collective-permute-start.18 = (bf16[128,2048]{1,0:T(8,128)(2,1)S(1)}, bf16[128,2048]{1,0:T(8,128)(2,1)S(1)}, u32[]{:S(2)}, u32[]{:S(2)}) collective-permute-start(bf16[128,2048]{1,0:T(8,128)(2,1)S(1)} %add_share.14), channel_id=1, source_target_pairs={{0,8},{2,10},{4,12},{6,14},{8,16},{9,1},{10,18},{11,3},{12,20},{13... | collective-permute-start | bytes 1572872 | tf_op jit(solution)/shard_map/ppermute | solution.py:50
  51.3 18.0 %collective-permute-start.17 = (bf16[128,2048]{1,0:T(8,128)(2,1)S(1)}, bf16[128,2048]{1,0:T(8,128)(2,1)S(1)}, u32[]{:S(2)}, u32[]{:S(2)}) collective-permute-start(bf16[128,2048]{1,0:T(8,128)(2,1)S(1)} %add_share.15), channel_id=1, source_target_pairs={{1,9},{3,11},{5,13},{7,15},{8,0},{9,17},{10,2},{11,19},{12,4},{13,... | collective-permute-start | bytes 1572872 | tf_op jit(solution)/shard_map/ppermute | solution.py:50
  62.0 7.4 %collective-permute-start.26 = (bf16[2,64,512]{2,1,0:T(8,128)(2,1)S(1)}, bf16[2,64,512]{2,1,0:T(8,128)(2,1)S(1)}, u32[]{:S(2)}, u32[]{:S(2)}) collective-permute-start(bf16[2,64,512]{2,1,0:T(8,128)(2,1)S(1)} %pad_maximum_fusion.4), channel_id=1, source_target_pairs={{0,4},{1,5},{2,6},{3,7},{4,0},{5,1},{6,2},{7,3},{8,12},{9,13},{10,... | collective-permute-start | bytes 393224 | tf_op jit(solution)/shard_map/ppermute | solution.py:187
  62.1 23.4 %collective-permute-start.23 = (bf16[128,2048]{1,0:T(8,128)(2,1)S(1)}, bf16[128,2048]{1,0:T(8,128)(2,1)S(1)}, u32[]{:S(2)}, u32[]{:S(2)}) collective-permute-start(bf16[128,2048]{1,0:T(8,128)(2,1)S(1)} %add_share.17), channel_id=1, source_target_pairs={{1,9},{3,11},{5,13},{7,15},{8,0},{9,17},{10,2},{11,19},{12,4},{13,... | collective-permute-start | bytes 1572872 | tf_op jit(solution)/shard_map/ppermute | solution.py:50
  63.4 16.9 %collective-permute-start.24 = (bf16[128,2048]{1,0:T(8,128)(2,1)S(1)}, bf16[128,2048]{1,0:T(8,128)(2,1)S(1)}, u32[]{:S(2)}, u32[]{:S(2)}) collective-permute-start(bf16[128,2048]{1,0:T(8,128)(2,1)S(1)} %add_share.16), channel_id=1, source_target_pairs={{0,8},{2,10},{4,12},{6,14},{8,16},{9,1},{10,18},{11,3},{12,20},{13... | collective-permute-start | bytes 1572872 | tf_op jit(solution)/shard_map/ppermute | solution.py:50
  69.4 6.7 %collective-permute-start.27 = (bf16[4,64,512]{2,1,0:T(8,128)(2,1)S(1)}, bf16[4,64,512]{2,1,0:T(8,128)(2,1)S(1)}, u32[]{:S(2)}, u32[]{:S(2)}) collective-permute-start(bf16[4,64,512]{2,1,0:T(8,128)(2,1)S(1)} %pad_maximum_fusion.2), channel_id=1, source_target_pairs={{0,1},{1,0},{2,3},{3,2},{4,5},{5,4},{6,7},{7,6},{8,9},{9,8},{10,11... | collective-permute-start | bytes 786440 | tf_op jit(solution)/shard_map/ppermute | solution.py:187
  69.8 22.4 %collective-permute-start.21 = (bf16[128,2048]{1,0:T(8,128)(2,1)S(1)}, bf16[128,2048]{1,0:T(8,128)(2,1)S(1)}, u32[]{:S(2)}, u32[]{:S(2)}) collective-permute-start(bf16[128,2048]{1,0:T(8,128)(2,1)S(1)} %add_share.19), channel_id=1, source_target_pairs={{1,9},{3,11},{5,13},{7,15},{8,0},{9,17},{10,2},{11,19},{12,4},{13,... | collective-permute-start | bytes 1572872 | tf_op jit(solution)/shard_map/ppermute | solution.py:50
  71.1 20.4 %collective-permute-start.22 = (bf16[128,2048]{1,0:T(8,128)(2,1)S(1)}, bf16[128,2048]{1,0:T(8,128)(2,1)S(1)}, u32[]{:S(2)}, u32[]{:S(2)}) collective-permute-start(bf16[128,2048]{1,0:T(8,128)(2,1)S(1)} %add_share.18), channel_id=1, source_target_pairs={{0,8},{2,10},{4,12},{6,14},{8,16},{9,1},{10,18},{11,3},{12,20},{13... | collective-permute-start | bytes 1572872 | tf_op jit(solution)/shard_map/ppermute | solution.py:50
  81.0 27.9 %collective-permute-start.30 = (bf16[128,2048]{1,0:T(8,128)(2,1)S(1)}, bf16[128,2048]{1,0:T(8,128)(2,1)S(1)}, u32[]{:S(2)}, u32[]{:S(2)}) collective-permute-start(bf16[128,2048]{1,0:T(8,128)(2,1)S(1)} %add_share.20), channel_id=1, source_target_pairs={{0,8},{2,10},{4,12},{6,14},{8,16},{9,1},{10,18},{11,3},{12,20},{13... | collective-permute-start | bytes 1572872 | tf_op jit(solution)/shard_map/ppermute | solution.py:50
  85.5 23.4 %collective-permute-start.31 = (bf16[128,2048]{1,0:T(8,128)(2,1)S(1)}, bf16[128,2048]{1,0:T(8,128)(2,1)S(1)}, u32[]{:S(2)}, u32[]{:S(2)}) collective-permute-start(bf16[128,2048]{1,0:T(8,128)(2,1)S(1)} %add_share.21), channel_id=1, source_target_pairs={{1,9},{3,11},{5,13},{7,15},{8,0},{9,17},{10,2},{11,19},{12,4},{13,... | collective-permute-start | bytes 1572872 | tf_op jit(solution)/shard_map/ppermute | solution.py:50
  92.5 20.0 %collective-permute-start.29 = (bf16[128,2048]{1,0:T(8,128)(2,1)S(1)}, bf16[128,2048]{1,0:T(8,128)(2,1)S(1)}, u32[]{:S(2)}, u32[]{:S(2)}) collective-permute-start(bf16[128,2048]{1,0:T(8,128)(2,1)S(1)} %add_share.23), channel_id=1, source_target_pairs={{1,9},{3,11},{5,13},{7,15},{8,0},{9,17},{10,2},{11,19},{12,4},{13,... | collective-permute-start | bytes 1572872 | tf_op jit(solution)/shard_map/ppermute | solution.py:50
  93.8 19.8 %collective-permute-start.28 = (bf16[128,2048]{1,0:T(8,128)(2,1)S(1)}, bf16[128,2048]{1,0:T(8,128)(2,1)S(1)}, u32[]{:S(2)}, u32[]{:S(2)}) collective-permute-start(bf16[128,2048]{1,0:T(8,128)(2,1)S(1)} %add_share.22), channel_id=1, source_target_pairs={{0,8},{2,10},{4,12},{6,14},{8,16},{9,1},{10,18},{11,3},{12,20},{13... | collective-permute-start | bytes 1572872 | tf_op jit(solution)/shard_map/ppermute | solution.py:50
  (11 other events, 85.4 us)

commit v3 on v2

--- a/solution.py
+++ b/solution.py
@@ -220,10 +220,9 @@
     tall = [across(bits) for bits in range(rows - 1, -1, -1)]
     own, tall = tall[-1], jnp.stack(tall[-2::-1])
     near = [tall, swap(tall, 2), swap(tall, 4), swap(tall, 6)]
-    near[0] = after(near[0], [first[0]])
-    near[1] = after(near[1], [first[1]])
+    near[3] = after(near[3], first)
     far = [swap(block, 1) for block in near]
-    far[3] = after(far[3], [second[0]])
+    far = after(far, second[0])
 
     own = own[None]
 

time: 115 us -> 113 us (0.983)
  waiting for transfers between devices: 35.1 us -> 26.9 us
  starting transfers between devices: 58.2 us -> 64.3 us
    ppermute x16, waiting for transfers between devices: 22.3 us -> 16.2 us  [ring(): return lax.ppermute(value, ('row', 'col'), pairs)]
    ppermute x16, starting transfers between devices: 41.8 us -> 46.9 us  [ring(): return lax.ppermute(value, ('row', 'col'), pairs)]
    ppermute x3, waiting for transfers between devices: 4.58 us -> 0.06 us  [across(): lax.ppermute(piece, 'row', [(at, at ^ bits) for at in range(rows)])]
    ppermute x13, waiting for transfers between devices: 8.22 us -> 10.7 us  [swap(): lax.ppermute(value, 'col', [(at, at ^ bits) for at in range(lax.axis_size...]
  transfers between devices with their start and end apart: 32 -> 32, of which waited for: 14 -> 15; matrix products, arithmetic and copies ran while one was open for 4% -> 4% of each run, Pallas kernels for 12% -> 13%
where the time goes in v3:
time: 113 us
  starting transfers between devices  64.3 us (57%)
  waiting for transfers between devices  26.9 us (24%)
  Pallas kernels  15.2 us (13%)
  other arithmetic  2.83 us (3%)
  between operations  1.34 us (1%)
  matrix products  1.25 us (1%)
    ppermute x16, starting transfers between devices, ring(): return lax.ppermute(value, ('row', 'col'), pairs)  46.9 us
    ppermute x16, waiting for transfers between devices, ring(): return lax.ppermute(value, ('row', 'col'), pairs)  16.2 us
    ppermute x13, starting transfers between devices, swap(): lax.ppermute(value, 'col', [(at, at ^ bits) for at in range(lax.axis_size...  12.9 us
    ppermute x13, waiting for transfers between devices, swap(): lax.ppermute(value, 'col', [(at, at ^ bits) for at in range(lax.axis_size...  10.7 us
    pallas_call x1, Pallas kernels, weight_product(): pl.pallas_call(kernel, out_shape=jax.ShapeDtypeStruct((cot.shape[1], widt...  7.6 us
    pallas_call x12, Pallas kernels, add_share(): pl.pallas_call(kernel, out_shape=jax.ShapeDtypeStruct(got.shape, got.dtyp...  4.89 us
    ppermute x3, starting transfers between devices, across(): lax.ppermute(piece, 'row', [(at, at ^ bits) for at in range(rows)])  4.45 us
    pallas_call x2, Pallas kernels, finish(): pl.pallas_call(kernel, out_shape=[jax.ShapeDtypeStruct(share.shape, jnp.b...  2.46 us
  transfers between devices with their start and end apart: 32, of which 15 were waited for; matrix products, arithmetic and copies ran while one was open for 4% of the time, Pallas kernels for 13%

profile of v3, /device:TPU:0, one launch (start us, length us, event | category | flops | bytes accessed | tf_op | source)
XLA Modules:
  0.0 112.8 jit_solution(13801463592685322885)
XLA Ops:
  1.6 3.0 %collective-permute-start.4 = (bf16[64,512]{1,0:T(8,128)(2,1)S(1)}, bf16[64,512]{1,0:T(8,128)(2,1)S(1)}, u32[]{:S(2)}, u32[]{:S(2)}) collective-permute-start(bf16[64,512]{1,0:T(8,128)(2,1)S(1)} %get-tuple-element.88), channel_id=1, source_target_pairs={{0,2},{1,3},{2,0},{3,1},{4,6},{5,7},{6,4},{7,5},{8,10},{9,11},{10,... | collective-permute-start | bytes 196616 | tf_op jit(solution)/shard_map/ppermute | solution.py:187
  4.6 1.5 %collective-permute-start.5 = (bf16[64,512]{1,0:T(8,128)(2,1)S(1)}, bf16[64,512]{1,0:T(8,128)(2,1)S(1)}, u32[]{:S(2)}, u32[]{:S(2)}) collective-permute-start(bf16[64,512]{1,0:T(8,128)(2,1)S(1)} %get-tuple-element.90), channel_id=1, source_target_pairs={{0,4},{1,5},{2,6},{3,7},{4,0},{5,1},{6,2},{7,3},{8,12},{9,13},{10,... | collective-permute-start | bytes 196616 | tf_op jit(solution)/shard_map/ppermute | solution.py:187
  6.2 2.2 %fusion.14 = (bf16[128,2048]{1,0:T(8,128)(2,1)S(1)}, bf16[128,2048]{1,0:T(8,128)(2,1)S(1)}) fusion(bf16[256,2048]{1,0:T(8,128)(2,1)} %refs_1_, bf16[256,2048]{1,0:T(8,128)(2,1)} %refs_0_), kind=kLoop, calls=%fused_computation.22 | loop fusion | flops 4194304 | bytes 3145728 | tf_op jit(solution)/shard_map/convert_element_type | solution.py:252
  8.9 2.4 %collective-permute-done.6 = bf16[64,512]{1,0:T(8,128)(2,1)S(1)} collective-permute-done((bf16[64,512]{1,0:T(8,128)(2,1)S(1)}, bf16[64,512]{1,0:T(8,128)(2,1)S(1)}, u32[]{:S(2)}, u32[]{:S(2)}) %collective-permute-start.6) | collective-permute-done | bytes 65568 | tf_op jit(solution)/shard_map/ppermute | solution.py:187
  11.4 1.6 %collective-permute-start.7 = (bf16[64,512]{1,0:T(8,128)(2,1)S(1)}, bf16[64,512]{1,0:T(8,128)(2,1)S(1)}, u32[]{:S(2)}, u32[]{:S(2)}) collective-permute-start(bf16[64,512]{1,0:T(8,128)(2,1)S(1)} %get-tuple-element.86), channel_id=1, source_target_pairs={{0,8},{8,0},{16,24},{24,16},{1,9},{9,1},{17,25},{25,17},{2,10},{10... | collective-permute-start | bytes 196616 | tf_op jit(solution)/shard_map/ppermute | solution.py:218
  13.0 2.6 %collective-permute-start.8 = (bf16[64,512]{1,0:T(8,128)(2,1)S(1)}, bf16[64,512]{1,0:T(8,128)(2,1)S(1)}, u32[]{:S(2)}, u32[]{:S(2)}) collective-permute-start(bf16[64,512]{1,0:T(8,128)(2,1)S(1)} %get-tuple-element.85), channel_id=1, source_target_pairs={{0,16},{8,24},{16,0},{24,8},{1,17},{9,25},{17,1},{25,9},{2,18},{10... | collective-permute-start | bytes 196616 | tf_op jit(solution)/shard_map/ppermute | solution.py:218
  17.1 4.6 %collective-permute-start.3 = (bf16[128,2048]{1,0:T(8,128)(2,1)S(1)}, bf16[128,2048]{1,0:T(8,128)(2,1)S(1)}, u32[]{:S(2)}, u32[]{:S(2)}) collective-permute-start(bf16[128,2048]{1,0:T(8,128)(2,1)S(1)} %get-tuple-element.71), channel_id=1, source_target_pairs={{0,8},{2,10},{4,12},{6,14},{8,16},{9,1},{10,18},{11,3},{12,20},{13... | collective-permute-start | bytes 1572872 | tf_op jit(solution)/shard_map/ppermute | solution.py:50
  23.9 1.5 %collective-permute-start.11 = (bf16[3,64,512]{2,1,0:T(8,128)(2,1)S(1)}, bf16[3,64,512]{2,1,0:T(8,128)(2,1)S(1)}, u32[]{:S(2)}, u32[]{:S(2)}) collective-permute-start(bf16[3,64,512]{2,1,0:T(8,128)(2,1)S(1)} %pad_maximum_fusion.3.refs_0_), channel_id=1, source_target_pairs={{0,4},{1,5},{2,6},{3,7},{4,0},{5,1},{6,2},{7,3},{8,12},{9,13},{10,... | collective-permute-start | bytes 589832 | tf_op jit(solution)/shard_map/ppermute | solution.py:187
  25.4 3.4 %collective-permute-done.12.refs_3_ = bf16[3,64,512]{2,1,0:T(8,128)(2,1)S(1)} collective-permute-done((bf16[3,64,512]{2,1,0:T(8,128)(2,1)S(1)}, bf16[3,64,512]{2,1,0:T(8,128)(2,1)S(1)}, u32[]{:S(2)}, u32[]{:S(2)}) %collective-permute-start.12) | collective-permute-done | bytes 196640 | tf_op jit(solution)/shard_map/ppermute | solution.py:187
  28.8 2.3 %collective-permute-start.1 = (bf16[128,2048]{1,0:T(8,128)(2,1)S(1)}, bf16[128,2048]{1,0:T(8,128)(2,1)S(1)}, u32[]{:S(2)}, u32[]{:S(2)}) collective-permute-start(bf16[128,2048]{1,0:T(8,128)(2,1)S(1)} %get-tuple-element.72), channel_id=1, source_target_pairs={{0,8},{2,10},{4,12},{6,14},{8,16},{9,1},{10,18},{11,3},{12,20},{13... | collective-permute-start | bytes 1572872 | tf_op jit(solution)/shard_map/ppermute | solution.py:50
  33.1 2.6 %collective-permute-start.14 = (bf16[3,64,512]{2,1,0:T(8,128)(2,1)S(1)}, bf16[3,64,512]{2,1,0:T(8,128)(2,1)S(1)}, u32[]{:S(2)}, u32[]{:S(2)}) collective-permute-start(bf16[3,64,512]{2,1,0:T(8,128)(2,1)S(1)} %collective-permute-done.10.refs_1_), channel_id=1, source_target_pairs={{0,1},{1,0},{2,3},{3,2},{4,5},{5,4},{6,7},{7,6},{8,9},{9,8},{10,11... | collective-permute-start | bytes 589832 | tf_op jit(solution)/shard_map/ppermute | solution.py:187
  37.1 2.4 %collective-permute-done.1.got_ref.refs_1_ = bf16[128,2048]{1,0:T(8,128)(2,1)S(1)} collective-permute-done((bf16[128,2048]{1,0:T(8,128)(2,1)S(1)}, bf16[128,2048]{1,0:T(8,128)(2,1)S(1)}, u32[]{:S(2)}, u32[]{:S(2)}) %collective-permute-start.1) | collective-permute-done | bytes 524320 | tf_op jit(solution)/shard_map/ppermute | solution.py:50
  40.4 4.1 %collective-permute-start.20 = (bf16[128,2048]{1,0:T(8,128)(2,1)S(1)}, bf16[128,2048]{1,0:T(8,128)(2,1)S(1)}, u32[]{:S(2)}, u32[]{:S(2)}) collective-permute-start(bf16[128,2048]{1,0:T(8,128)(2,1)S(1)} %add_share.12), channel_id=1, source_target_pairs={{0,8},{2,10},{4,12},{6,14},{8,16},{9,1},{10,18},{11,3},{12,20},{13... | collective-permute-start | bytes 1572872 | tf_op jit(solution)/shard_map/ppermute | solution.py:50
  46.6 5.1 %collective-permute-start.18 = (bf16[128,2048]{1,0:T(8,128)(2,1)S(1)}, bf16[128,2048]{1,0:T(8,128)(2,1)S(1)}, u32[]{:S(2)}, u32[]{:S(2)}) collective-permute-start(bf16[128,2048]{1,0:T(8,128)(2,1)S(1)} %add_share.14), channel_id=1, source_target_pairs={{0,8},{2,10},{4,12},{6,14},{8,16},{9,1},{10,18},{11,3},{12,20},{13... | collective-permute-start | bytes 1572872 | tf_op jit(solution)/shard_map/ppermute | solution.py:50
  54.0 3.4 %collective-permute-done.25 = bf16[1,64,512]{2,1,0:T(8,128)(2,1)S(1)} collective-permute-done((bf16[1,64,512]{2,1,0:T(8,128)(2,1)S(1)}, bf16[1,64,512]{2,1,0:T(8,128)(2,1)S(1)}, u32[]{:S(2)}, u32[]{:S(2)}) %collective-permute-start.25) | collective-permute-done | bytes 65568 | tf_op jit(solution)/shard_map/ppermute | solution.py:187
  58.2 1.8 %collective-permute-done.19.got_ref.refs_8_ = bf16[128,2048]{1,0:T(8,128)(2,1)S(1)} collective-permute-done((bf16[128,2048]{1,0:T(8,128)(2,1)S(1)}, bf16[128,2048]{1,0:T(8,128)(2,1)S(1)}, u32[]{:S(2)}, u32[]{:S(2)}) %collective-permute-start.19) | collective-permute-done | bytes 524320 | tf_op jit(solution)/shard_map/ppermute | solution.py:50
  61.9 4.6 %collective-permute-start.24 = (bf16[128,2048]{1,0:T(8,128)(2,1)S(1)}, bf16[128,2048]{1,0:T(8,128)(2,1)S(1)}, u32[]{:S(2)}, u32[]{:S(2)}) collective-permute-start(bf16[128,2048]{1,0:T(8,128)(2,1)S(1)} %add_share.16), channel_id=1, source_target_pairs={{0,8},{2,10},{4,12},{6,14},{8,16},{9,1},{10,18},{11,3},{12,20},{13... | collective-permute-start | bytes 1572872 | tf_op jit(solution)/shard_map/ppermute | solution.py:50
  66.5 1.6 %collective-permute-done.18.got_ref.refs_3_ = bf16[128,2048]{1,0:T(8,128)(2,1)S(1)} collective-permute-done((bf16[128,2048]{1,0:T(8,128)(2,1)S(1)}, bf16[128,2048]{1,0:T(8,128)(2,1)S(1)}, u32[]{:S(2)}, u32[]{:S(2)}) %collective-permute-start.18) | collective-permute-done | bytes 524320 | tf_op jit(solution)/shard_map/ppermute | solution.py:50
  70.4 5.8 %collective-permute-start.22 = (bf16[128,2048]{1,0:T(8,128)(2,1)S(1)}, bf16[128,2048]{1,0:T(8,128)(2,1)S(1)}, u32[]{:S(2)}, u32[]{:S(2)}) collective-permute-start(bf16[128,2048]{1,0:T(8,128)(2,1)S(1)} %add_share.18), channel_id=1, source_target_pairs={{0,8},{2,10},{4,12},{6,14},{8,16},{9,1},{10,18},{11,3},{12,20},{13... | collective-permute-start | bytes 1572872 | tf_op jit(solution)/shard_map/ppermute | solution.py:50
  76.3 3.0 %collective-permute-done.24.got_ref.refs_4_ = bf16[128,2048]{1,0:T(8,128)(2,1)S(1)} collective-permute-done((bf16[128,2048]{1,0:T(8,128)(2,1)S(1)}, bf16[128,2048]{1,0:T(8,128)(2,1)S(1)}, u32[]{:S(2)}, u32[]{:S(2)}) %collective-permute-start.24) | collective-permute-done | bytes 524320 | tf_op jit(solution)/shard_map/ppermute | solution.py:50
  80.0 4.4 %collective-permute-start.30 = (bf16[128,2048]{1,0:T(8,128)(2,1)S(1)}, bf16[128,2048]{1,0:T(8,128)(2,1)S(1)}, u32[]{:S(2)}, u32[]{:S(2)}) collective-permute-start(bf16[128,2048]{1,0:T(8,128)(2,1)S(1)} %add_share.20), channel_id=1, source_target_pairs={{0,8},{2,10},{4,12},{6,14},{8,16},{9,1},{10,18},{11,3},{12,20},{13... | collective-permute-start | bytes 1572872 | tf_op jit(solution)/shard_map/ppermute | solution.py:50
  85.8 4.7 %collective-permute-done.22.got_ref.refs_5_ = bf16[128,2048]{1,0:T(8,128)(2,1)S(1)} collective-permute-done((bf16[128,2048]{1,0:T(8,128)(2,1)S(1)}, bf16[128,2048]{1,0:T(8,128)(2,1)S(1)}, u32[]{:S(2)}, u32[]{:S(2)}) %collective-permute-start.22) | collective-permute-done | bytes 524320 | tf_op jit(solution)/shard_map/ppermute | solution.py:50
  92.8 5.7 %collective-permute-start.28 = (bf16[128,2048]{1,0:T(8,128)(2,1)S(1)}, bf16[128,2048]{1,0:T(8,128)(2,1)S(1)}, u32[]{:S(2)}, u32[]{:S(2)}) collective-permute-start(bf16[128,2048]{1,0:T(8,128)(2,1)S(1)} %add_share.22), channel_id=1, source_target_pairs={{0,8},{2,10},{4,12},{6,14},{8,16},{9,1},{10,18},{11,3},{12,20},{13... | collective-permute-start | bytes 1572872 | tf_op jit(solution)/shard_map/ppermute | solution.py:50
  99.8 7.6 %weight_product.1 = bf16[1024,2048]{1,0:T(8,128)(2,1)} custom-call(bf16[256,1024]{1,0:T(8,128)(2,1)S(1)} %lay_strips.3.own_cot_ref, bf16[768,1024]{1,0:T(8,128)(2,1)S(1)} %lay_strips.2.cot_ref, bf16[256,2048]{1,0:T(8,128)(2,1)S(1)} %pad_maximum_fusion.own_ref, bf16[128,2048]{1,0:T(8,128)(2,1)S(1)} %collective-permute-done.3.got_ref.refs_0_, ...), custom_call_target="tpu_custom_call" | custom-call | flops 4294967296 | bytes 8388608 | tf_op jit(solution)/shard_map/weight_product/pallas_call | solution.py:129
  (75 shorter events, 29.5 us)
Async XLA Ops:
  1.6 6.8 %collective-permute-start.4 = (bf16[64,512]{1,0:T(8,128)(2,1)S(1)}, bf16[64,512]{1,0:T(8,128)(2,1)S(1)}, u32[]{:S(2)}, u32[]{:S(2)}) collective-permute-start(bf16[64,512]{1,0:T(8,128)(2,1)S(1)} %get-tuple-element.88), channel_id=1, source_target_pairs={{0,2},{1,3},{2,0},{3,1},{4,6},{5,7},{6,4},{7,5},{8,10},{9,11},{10,... | collective-permute-start | bytes 196616 | tf_op jit(solution)/shard_map/ppermute | solution.py:187
  11.4 10.3 %collective-permute-start.7 = (bf16[64,512]{1,0:T(8,128)(2,1)S(1)}, bf16[64,512]{1,0:T(8,128)(2,1)S(1)}, u32[]{:S(2)}, u32[]{:S(2)}) collective-permute-start(bf16[64,512]{1,0:T(8,128)(2,1)S(1)} %get-tuple-element.86), channel_id=1, source_target_pairs={{0,8},{8,0},{16,24},{24,16},{1,9},{9,1},{17,25},{25,17},{2,10},{10... | collective-permute-start | bytes 196616 | tf_op jit(solution)/shard_map/ppermute | solution.py:218
  13.0 8.7 %collective-permute-start.8 = (bf16[64,512]{1,0:T(8,128)(2,1)S(1)}, bf16[64,512]{1,0:T(8,128)(2,1)S(1)}, u32[]{:S(2)}, u32[]{:S(2)}) collective-permute-start(bf16[64,512]{1,0:T(8,128)(2,1)S(1)} %get-tuple-element.85), channel_id=1, source_target_pairs={{0,16},{8,24},{16,0},{24,8},{1,17},{9,25},{17,1},{25,9},{2,18},{10... | collective-permute-start | bytes 196616 | tf_op jit(solution)/shard_map/ppermute | solution.py:218
  15.9 17.2 %collective-permute-start.2 = (bf16[128,2048]{1,0:T(8,128)(2,1)S(1)}, bf16[128,2048]{1,0:T(8,128)(2,1)S(1)}, u32[]{:S(2)}, u32[]{:S(2)}) collective-permute-start(bf16[128,2048]{1,0:T(8,128)(2,1)S(1)} %get-tuple-element.71), channel_id=1, source_target_pairs={{1,9},{3,11},{5,13},{7,15},{8,0},{9,17},{10,2},{11,19},{12,4},{13,... | collective-permute-start | bytes 1572872 | tf_op jit(solution)/shard_map/ppermute | solution.py:50
  17.1 18.6 %collective-permute-start.3 = (bf16[128,2048]{1,0:T(8,128)(2,1)S(1)}, bf16[128,2048]{1,0:T(8,128)(2,1)S(1)}, u32[]{:S(2)}, u32[]{:S(2)}) collective-permute-start(bf16[128,2048]{1,0:T(8,128)(2,1)S(1)} %get-tuple-element.71), channel_id=1, source_target_pairs={{0,8},{2,10},{4,12},{6,14},{8,16},{9,1},{10,18},{11,3},{12,20},{13... | collective-permute-start | bytes 1572872 | tf_op jit(solution)/shard_map/ppermute | solution.py:50
  21.8 6.9 %collective-permute-start.12 = (bf16[3,64,512]{2,1,0:T(8,128)(2,1)S(1)}, bf16[3,64,512]{2,1,0:T(8,128)(2,1)S(1)}, u32[]{:S(2)}, u32[]{:S(2)}) collective-permute-start(bf16[3,64,512]{2,1,0:T(8,128)(2,1)S(1)} %pad_maximum_fusion.3.refs_0_), channel_id=1, source_target_pairs={{0,6},{1,7},{2,4},{3,5},{4,2},{5,3},{6,0},{7,1},{8,14},{9,15},{10,... | collective-permute-start | bytes 589832 | tf_op jit(solution)/shard_map/ppermute | solution.py:187
  22.4 8.7 %collective-permute-start.10 = (bf16[3,64,512]{2,1,0:T(8,128)(2,1)S(1)}, bf16[3,64,512]{2,1,0:T(8,128)(2,1)S(1)}, u32[]{:S(2)}, u32[]{:S(2)}) collective-permute-start(bf16[3,64,512]{2,1,0:T(8,128)(2,1)S(1)} %pad_maximum_fusion.3.refs_0_), channel_id=1, source_target_pairs={{0,2},{1,3},{2,0},{3,1},{4,6},{5,7},{6,4},{7,5},{8,10},{9,11},{10,... | collective-permute-start | bytes 589832 | tf_op jit(solution)/shard_map/ppermute | solution.py:187
  23.9 7.3 %collective-permute-start.11 = (bf16[3,64,512]{2,1,0:T(8,128)(2,1)S(1)}, bf16[3,64,512]{2,1,0:T(8,128)(2,1)S(1)}, u32[]{:S(2)}, u32[]{:S(2)}) collective-permute-start(bf16[3,64,512]{2,1,0:T(8,128)(2,1)S(1)} %pad_maximum_fusion.3.refs_0_), channel_id=1, source_target_pairs={{0,4},{1,5},{2,6},{3,7},{4,0},{5,1},{6,2},{7,3},{8,12},{9,13},{10,... | collective-permute-start | bytes 589832 | tf_op jit(solution)/shard_map/ppermute | solution.py:187
  28.8 10.7 %collective-permute-start.1 = (bf16[128,2048]{1,0:T(8,128)(2,1)S(1)}, bf16[128,2048]{1,0:T(8,128)(2,1)S(1)}, u32[]{:S(2)}, u32[]{:S(2)}) collective-permute-start(bf16[128,2048]{1,0:T(8,128)(2,1)S(1)} %get-tuple-element.72), channel_id=1, source_target_pairs={{0,8},{2,10},{4,12},{6,14},{8,16},{9,1},{10,18},{11,3},{12,20},{13... | collective-permute-start | bytes 1572872 | tf_op jit(solution)/shard_map/ppermute | solution.py:50
  31.2 20.5 %collective-permute-start = (bf16[128,2048]{1,0:T(8,128)(2,1)S(1)}, bf16[128,2048]{1,0:T(8,128)(2,1)S(1)}, u32[]{:S(2)}, u32[]{:S(2)}) collective-permute-start(bf16[128,2048]{1,0:T(8,128)(2,1)S(1)} %get-tuple-element.72), channel_id=1, source_target_pairs={{1,9},{3,11},{5,13},{7,15},{8,0},{9,17},{10,2},{11,19},{12,4},{13,... | collective-permute-start | bytes 1572872 | tf_op jit(solution)/shard_map/ppermute | solution.py:50
  40.4 17.0 %collective-permute-start.20 = (bf16[128,2048]{1,0:T(8,128)(2,1)S(1)}, bf16[128,2048]{1,0:T(8,128)(2,1)S(1)}, u32[]{:S(2)}, u32[]{:S(2)}) collective-permute-start(bf16[128,2048]{1,0:T(8,128)(2,1)S(1)} %add_share.12), channel_id=1, source_target_pairs={{0,8},{2,10},{4,12},{6,14},{8,16},{9,1},{10,18},{11,3},{12,20},{13... | collective-permute-start | bytes 1572872 | tf_op jit(solution)/shard_map/ppermute | solution.py:50
  44.6 15.4 %collective-permute-start.19 = (bf16[128,2048]{1,0:T(8,128)(2,1)S(1)}, bf16[128,2048]{1,0:T(8,128)(2,1)S(1)}, u32[]{:S(2)}, u32[]{:S(2)}) collective-permute-start(bf16[128,2048]{1,0:T(8,128)(2,1)S(1)} %add_share.13), channel_id=1, source_target_pairs={{1,9},{3,11},{5,13},{7,15},{8,0},{9,17},{10,2},{11,19},{12,4},{13,... | collective-permute-start | bytes 1572872 | tf_op jit(solution)/shard_map/ppermute | solution.py:50
  46.6 21.4 %collective-permute-start.18 = (bf16[128,2048]{1,0:T(8,128)(2,1)S(1)}, bf16[128,2048]{1,0:T(8,128)(2,1)S(1)}, u32[]{:S(2)}, u32[]{:S(2)}) collective-permute-start(bf16[128,2048]{1,0:T(8,128)(2,1)S(1)} %add_share.14), channel_id=1, source_target_pairs={{0,8},{2,10},{4,12},{6,14},{8,16},{9,1},{10,18},{11,3},{12,20},{13... | collective-permute-start | bytes 1572872 | tf_op jit(solution)/shard_map/ppermute | solution.py:50
  51.8 17.0 %collective-permute-start.17 = (bf16[128,2048]{1,0:T(8,128)(2,1)S(1)}, bf16[128,2048]{1,0:T(8,128)(2,1)S(1)}, u32[]{:S(2)}, u32[]{:S(2)}) collective-permute-start(bf16[128,2048]{1,0:T(8,128)(2,1)S(1)} %add_share.15), channel_id=1, source_target_pairs={{1,9},{3,11},{5,13},{7,15},{8,0},{9,17},{10,2},{11,19},{12,4},{13,... | collective-permute-start | bytes 1572872 | tf_op jit(solution)/shard_map/ppermute | solution.py:50
  60.0 8.9 %collective-permute-start.26 = (bf16[2,64,512]{2,1,0:T(8,128)(2,1)S(1)}, bf16[2,64,512]{2,1,0:T(8,128)(2,1)S(1)}, u32[]{:S(2)}, u32[]{:S(2)}) collective-permute-start(bf16[2,64,512]{2,1,0:T(8,128)(2,1)S(1)} %pad_maximum_fusion.4), channel_id=1, source_target_pairs={{0,4},{1,5},{2,6},{3,7},{4,0},{5,1},{6,2},{7,3},{8,12},{9,13},{10,... | collective-permute-start | bytes 393224 | tf_op jit(solution)/shard_map/ppermute | solution.py:187
  60.6 23.8 %collective-permute-start.23 = (bf16[128,2048]{1,0:T(8,128)(2,1)S(1)}, bf16[128,2048]{1,0:T(8,128)(2,1)S(1)}, u32[]{:S(2)}, u32[]{:S(2)}) collective-permute-start(bf16[128,2048]{1,0:T(8,128)(2,1)S(1)} %add_share.17), channel_id=1, source_target_pairs={{1,9},{3,11},{5,13},{7,15},{8,0},{9,17},{10,2},{11,19},{12,4},{13,... | collective-permute-start | bytes 1572872 | tf_op jit(solution)/shard_map/ppermute | solution.py:50
  61.9 17.4 %collective-permute-start.24 = (bf16[128,2048]{1,0:T(8,128)(2,1)S(1)}, bf16[128,2048]{1,0:T(8,128)(2,1)S(1)}, u32[]{:S(2)}, u32[]{:S(2)}) collective-permute-start(bf16[128,2048]{1,0:T(8,128)(2,1)S(1)} %add_share.16), channel_id=1, source_target_pairs={{0,8},{2,10},{4,12},{6,14},{8,16},{9,1},{10,18},{11,3},{12,20},{13... | collective-permute-start | bytes 1572872 | tf_op jit(solution)/shard_map/ppermute | solution.py:50
  68.9 7.3 %collective-permute-start.27 = (bf16[4,64,512]{2,1,0:T(8,128)(2,1)S(1)}, bf16[4,64,512]{2,1,0:T(8,128)(2,1)S(1)}, u32[]{:S(2)}, u32[]{:S(2)}) collective-permute-start(bf16[4,64,512]{2,1,0:T(8,128)(2,1)S(1)} %pad_maximum_fusion.2), channel_id=1, source_target_pairs={{0,1},{1,0},{2,3},{3,2},{4,5},{5,4},{6,7},{7,6},{8,9},{9,8},{10,11... | collective-permute-start | bytes 786440 | tf_op jit(solution)/shard_map/ppermute | solution.py:187
  69.1 22.2 %collective-permute-start.21 = (bf16[128,2048]{1,0:T(8,128)(2,1)S(1)}, bf16[128,2048]{1,0:T(8,128)(2,1)S(1)}, u32[]{:S(2)}, u32[]{:S(2)}) collective-permute-start(bf16[128,2048]{1,0:T(8,128)(2,1)S(1)} %add_share.19), channel_id=1, source_target_pairs={{1,9},{3,11},{5,13},{7,15},{8,0},{9,17},{10,2},{11,19},{12,4},{13,... | collective-permute-start | bytes 1572872 | tf_op jit(solution)/shard_map/ppermute | solution.py:50
  70.4 20.2 %collective-permute-start.22 = (bf16[128,2048]{1,0:T(8,128)(2,1)S(1)}, bf16[128,2048]{1,0:T(8,128)(2,1)S(1)}, u32[]{:S(2)}, u32[]{:S(2)}) collective-permute-start(bf16[128,2048]{1,0:T(8,128)(2,1)S(1)} %add_share.18), channel_id=1, source_target_pairs={{0,8},{2,10},{4,12},{6,14},{8,16},{9,1},{10,18},{11,3},{12,20},{13... | collective-permute-start | bytes 1572872 | tf_op jit(solution)/shard_map/ppermute | solution.py:50
  80.0 27.9 %collective-permute-start.30 = (bf16[128,2048]{1,0:T(8,128)(2,1)S(1)}, bf16[128,2048]{1,0:T(8,128)(2,1)S(1)}, u32[]{:S(2)}, u32[]{:S(2)}) collective-permute-start(bf16[128,2048]{1,0:T(8,128)(2,1)S(1)} %add_share.20), channel_id=1, source_target_pairs={{0,8},{2,10},{4,12},{6,14},{8,16},{9,1},{10,18},{11,3},{12,20},{13... | collective-permute-start | bytes 1572872 | tf_op jit(solution)/shard_map/ppermute | solution.py:50
  84.5 23.4 %collective-permute-start.31 = (bf16[128,2048]{1,0:T(8,128)(2,1)S(1)}, bf16[128,2048]{1,0:T(8,128)(2,1)S(1)}, u32[]{:S(2)}, u32[]{:S(2)}) collective-permute-start(bf16[128,2048]{1,0:T(8,128)(2,1)S(1)} %add_share.21), channel_id=1, source_target_pairs={{1,9},{3,11},{5,13},{7,15},{8,0},{9,17},{10,2},{11,19},{12,4},{13,... | collective-permute-start | bytes 1572872 | tf_op jit(solution)/shard_map/ppermute | solution.py:50
  91.5 19.0 %collective-permute-start.29 = (bf16[128,2048]{1,0:T(8,128)(2,1)S(1)}, bf16[128,2048]{1,0:T(8,128)(2,1)S(1)}, u32[]{:S(2)}, u32[]{:S(2)}) collective-permute-start(bf16[128,2048]{1,0:T(8,128)(2,1)S(1)} %add_share.23), channel_id=1, source_target_pairs={{1,9},{3,11},{5,13},{7,15},{8,0},{9,17},{10,2},{11,19},{12,4},{13,... | collective-permute-start | bytes 1572872 | tf_op jit(solution)/shard_map/ppermute | solution.py:50
  92.8 18.7 %collective-permute-start.28 = (bf16[128,2048]{1,0:T(8,128)(2,1)S(1)}, bf16[128,2048]{1,0:T(8,128)(2,1)S(1)}, u32[]{:S(2)}, u32[]{:S(2)}) collective-permute-start(bf16[128,2048]{1,0:T(8,128)(2,1)S(1)} %add_share.22), channel_id=1, source_target_pairs={{0,8},{2,10},{4,12},{6,14},{8,16},{9,1},{10,18},{11,3},{12,20},{13... | collective-permute-start | bytes 1572872 | tf_op jit(solution)/shard_map/ppermute | solution.py:50
  (11 other events, 77.1 us)

commit v4 on v1

--- a/solution.py
+++ b/solution.py
@@ -261,7 +261,7 @@
                 got = after(steps[-2][at], turn)
                 turn = add_share(got, cot, down_t, way, step, first, tok_rows)
                 steps[-1].append(ring(turn, way))
-                if (step, at, way) in ((2, 1, 1), (3, 0, 1), (3, 1, 1)):
+                if (step, at, way) in ((3, 0, 0), (3, 1, 0), (4, 0, 0)):
                     own_cot, stage = own_group(stage, own_cot, turn), stage + 1
         late = turn
 

time: 114 us -> 113 us (level)
  waiting for transfers between devices: 28.7 us -> 26.9 us
    ppermute x16, waiting for transfers between devices: 18 us -> 15.3 us  [ring(): return lax.ppermute(value, ('row', 'col'), pairs)]
  transfers between devices with their start and end apart: 32 -> 32, of which waited for: 15 -> 13; matrix products, arithmetic and copies ran while one was open for 3% -> 3% of each run, Pallas kernels for 12% -> 13%
where the time goes in v4:
time: 113 us; the launch traced here: 112 us
  starting transfers between devices  63.9 us (57%)
  waiting for transfers between devices  26.9 us (24%)
  Pallas kernels  15.5 us (14%)
  other arithmetic  2.36 us (2%)
  between operations  1.33 us (1%)
  matrix products  1.25 us (1%)
    ppermute x16, starting transfers between devices, ring(): return lax.ppermute(value, ('row', 'col'), pairs)  46.3 us
    ppermute x16, waiting for transfers between devices, ring(): return lax.ppermute(value, ('row', 'col'), pairs)  15.3 us
    ppermute x13, starting transfers between devices, swap(): lax.ppermute(value, 'col', [(at, at ^ bits) for at in range(lax.axis_size...  13.1 us
    ppermute x13, waiting for transfers between devices, swap(): lax.ppermute(value, 'col', [(at, at ^ bits) for at in range(lax.axis_size...  11.5 us
    pallas_call x1, Pallas kernels, weight_product(): pl.pallas_call(kernel, out_shape=jax.ShapeDtypeStruct((cot.shape[1], widt...  7.6 us
    pallas_call x12, Pallas kernels, add_share(): pl.pallas_call(kernel, out_shape=jax.ShapeDtypeStruct(got.shape, got.dtyp...  4.89 us
    ppermute x3, starting transfers between devices, across(): lax.ppermute(piece, 'row', [(at, at ^ bits) for at in range(rows)])  4.45 us
    pallas_call x2, Pallas kernels, finish(): pl.pallas_call(kernel, out_shape=[jax.ShapeDtypeStruct(gate_pre.shape, jn...  2.77 us
  transfers between devices with their start and end apart: 32, of which 13 were waited for; matrix products, arithmetic and copies ran while one was open for 3% of the time, Pallas kernels for 13%

profile of v4, /device:TPU:0, one launch (start us, length us, event | category | flops | bytes accessed | tf_op | source)
XLA Modules:
  0.0 112.2 jit_solution(9250117283552476483)
XLA Ops:
  1.6 3.0 %collective-permute-start = (bf16[64,512]{1,0:T(8,128)(2,1)S(1)}, bf16[64,512]{1,0:T(8,128)(2,1)S(1)}, u32[]{:S(2)}, u32[]{:S(2)}) collective-permute-start(bf16[64,512]{1,0:T(8,128)(2,1)S(1)} %get-tuple-element.82), channel_id=1, source_target_pairs={{0,2},{1,3},{2,0},{3,1},{4,6},{5,7},{6,4},{7,5},{8,10},{9,11},{10,... | collective-permute-start | bytes 196616 | tf_op jit(solution)/shard_map/ppermute | solution.py:184
  4.6 1.5 %collective-permute-start.1 = (bf16[64,512]{1,0:T(8,128)(2,1)S(1)}, bf16[64,512]{1,0:T(8,128)(2,1)S(1)}, u32[]{:S(2)}, u32[]{:S(2)}) collective-permute-start(bf16[64,512]{1,0:T(8,128)(2,1)S(1)} %get-tuple-element.84), channel_id=1, source_target_pairs={{0,4},{1,5},{2,6},{3,7},{4,0},{5,1},{6,2},{7,3},{8,12},{9,13},{10,... | collective-permute-start | bytes 196616 | tf_op jit(solution)/shard_map/ppermute | solution.py:184
  6.2 2.2 %fusion.8 = (bf16[128,2048]{1,0:T(8,128)(2,1)S(1)}, bf16[128,2048]{1,0:T(8,128)(2,1)S(1)}) fusion(bf16[256,2048]{1,0:T(8,128)(2,1)} %refs_1_.1, bf16[256,2048]{1,0:T(8,128)(2,1)} %refs_0_.1), kind=kLoop, calls=%fused_computation.13 | loop fusion | flops 4194304 | bytes 3145728 | tf_op jit(solution)/shard_map/convert_element_type | solution.py:249
  8.9 2.4 %collective-permute-done.2 = bf16[64,512]{1,0:T(8,128)(2,1)S(1)} collective-permute-done((bf16[64,512]{1,0:T(8,128)(2,1)S(1)}, bf16[64,512]{1,0:T(8,128)(2,1)S(1)}, u32[]{:S(2)}, u32[]{:S(2)}) %collective-permute-start.2) | collective-permute-done | bytes 65568 | tf_op jit(solution)/shard_map/ppermute | solution.py:184
  11.4 1.6 %collective-permute-start.4 = (bf16[64,512]{1,0:T(8,128)(2,1)S(1)}, bf16[64,512]{1,0:T(8,128)(2,1)S(1)}, u32[]{:S(2)}, u32[]{:S(2)}) collective-permute-start(bf16[64,512]{1,0:T(8,128)(2,1)S(1)} %get-tuple-element.77), channel_id=1, source_target_pairs={{0,8},{8,0},{16,24},{24,16},{1,9},{9,1},{17,25},{25,17},{2,10},{10... | collective-permute-start | bytes 196616 | tf_op jit(solution)/shard_map/ppermute | solution.py:215
  13.0 2.6 %collective-permute-start.5 = (bf16[64,512]{1,0:T(8,128)(2,1)S(1)}, bf16[64,512]{1,0:T(8,128)(2,1)S(1)}, u32[]{:S(2)}, u32[]{:S(2)}) collective-permute-start(bf16[64,512]{1,0:T(8,128)(2,1)S(1)} %get-tuple-element.79), channel_id=1, source_target_pairs={{0,16},{8,24},{16,0},{24,8},{1,17},{9,25},{17,1},{25,9},{2,18},{10... | collective-permute-start | bytes 196616 | tf_op jit(solution)/shard_map/ppermute | solution.py:215
  17.1 4.6 %collective-permute-start.3 = (bf16[128,2048]{1,0:T(8,128)(2,1)S(1)}, bf16[128,2048]{1,0:T(8,128)(2,1)S(1)}, u32[]{:S(2)}, u32[]{:S(2)}) collective-permute-start(bf16[128,2048]{1,0:T(8,128)(2,1)S(1)} %get-tuple-element.68), channel_id=1, source_target_pairs={{0,8},{2,10},{4,12},{6,14},{8,16},{9,1},{10,18},{11,3},{12,20},{13... | collective-permute-start | bytes 1572872 | tf_op jit(solution)/shard_map/ppermute | solution.py:50
  22.4 1.5 %collective-permute-start.7 = (bf16[3,64,512]{2,1,0:T(8,128)(2,1)S(1)}, bf16[3,64,512]{2,1,0:T(8,128)(2,1)S(1)}, u32[]{:S(2)}, u32[]{:S(2)}) collective-permute-start(bf16[3,64,512]{2,1,0:T(8,128)(2,1)S(1)} %pad_maximum_fusion.3.refs_0_), channel_id=1, source_target_pairs={{0,2},{1,3},{2,0},{3,1},{4,6},{5,7},{6,4},{7,5},{8,10},{9,11},{10,... | collective-permute-start | bytes 589832 | tf_op jit(solution)/shard_map/ppermute | solution.py:184
  23.9 1.5 %collective-permute-start.8 = (bf16[3,64,512]{2,1,0:T(8,128)(2,1)S(1)}, bf16[3,64,512]{2,1,0:T(8,128)(2,1)S(1)}, u32[]{:S(2)}, u32[]{:S(2)}) collective-permute-start(bf16[3,64,512]{2,1,0:T(8,128)(2,1)S(1)} %pad_maximum_fusion.3.refs_0_), channel_id=1, source_target_pairs={{0,4},{1,5},{2,6},{3,7},{4,0},{5,1},{6,2},{7,3},{8,12},{9,13},{10,... | collective-permute-start | bytes 589832 | tf_op jit(solution)/shard_map/ppermute | solution.py:184
  25.4 3.4 %collective-permute-done.9.refs_3_ = bf16[3,64,512]{2,1,0:T(8,128)(2,1)S(1)} collective-permute-done((bf16[3,64,512]{2,1,0:T(8,128)(2,1)S(1)}, bf16[3,64,512]{2,1,0:T(8,128)(2,1)S(1)}, u32[]{:S(2)}, u32[]{:S(2)}) %collective-permute-start.9) | collective-permute-done | bytes 196640 | tf_op jit(solution)/shard_map/ppermute | solution.py:184
  28.8 2.3 %collective-permute-start.15 = (bf16[128,2048]{1,0:T(8,128)(2,1)S(1)}, bf16[128,2048]{1,0:T(8,128)(2,1)S(1)}, u32[]{:S(2)}, u32[]{:S(2)}) collective-permute-start(bf16[128,2048]{1,0:T(8,128)(2,1)S(1)} %get-tuple-element.67), channel_id=1, source_target_pairs={{0,8},{2,10},{4,12},{6,14},{8,16},{9,1},{10,18},{11,3},{12,20},{13... | collective-permute-start | bytes 1572872 | tf_op jit(solution)/shard_map/ppermute | solution.py:50
  33.1 2.6 %collective-permute-start.12 = (bf16[3,64,512]{2,1,0:T(8,128)(2,1)S(1)}, bf16[3,64,512]{2,1,0:T(8,128)(2,1)S(1)}, u32[]{:S(2)}, u32[]{:S(2)}) collective-permute-start(bf16[3,64,512]{2,1,0:T(8,128)(2,1)S(1)} %collective-permute-done.7.refs_1_), channel_id=1, source_target_pairs={{0,1},{1,0},{2,3},{3,2},{4,5},{5,4},{6,7},{7,6},{8,9},{9,8},{10,11... | collective-permute-start | bytes 589832 | tf_op jit(solution)/shard_map/ppermute | solution.py:184
  37.1 2.4 %collective-permute-done.15.got_ref.refs_1_ = bf16[128,2048]{1,0:T(8,128)(2,1)S(1)} collective-permute-done((bf16[128,2048]{1,0:T(8,128)(2,1)S(1)}, bf16[128,2048]{1,0:T(8,128)(2,1)S(1)}, u32[]{:S(2)}, u32[]{:S(2)}) %collective-permute-start.15) | collective-permute-done | bytes 524320 | tf_op jit(solution)/shard_map/ppermute | solution.py:50
  40.4 4.1 %collective-permute-start.16 = (bf16[128,2048]{1,0:T(8,128)(2,1)S(1)}, bf16[128,2048]{1,0:T(8,128)(2,1)S(1)}, u32[]{:S(2)}, u32[]{:S(2)}) collective-permute-start(bf16[128,2048]{1,0:T(8,128)(2,1)S(1)} %add_share.12), channel_id=1, source_target_pairs={{0,8},{2,10},{4,12},{6,14},{8,16},{9,1},{10,18},{11,3},{12,20},{13... | collective-permute-start | bytes 1572872 | tf_op jit(solution)/shard_map/ppermute | solution.py:50
  46.6 5.1 %collective-permute-start.19 = (bf16[128,2048]{1,0:T(8,128)(2,1)S(1)}, bf16[128,2048]{1,0:T(8,128)(2,1)S(1)}, u32[]{:S(2)}, u32[]{:S(2)}) collective-permute-start(bf16[128,2048]{1,0:T(8,128)(2,1)S(1)} %add_share.14), channel_id=1, source_target_pairs={{0,8},{2,10},{4,12},{6,14},{8,16},{9,1},{10,18},{11,3},{12,20},{13... | collective-permute-start | bytes 1572872 | tf_op jit(solution)/shard_map/ppermute | solution.py:50
  53.1 3.7 %collective-permute-done.16.got_ref.refs_2_ = bf16[128,2048]{1,0:T(8,128)(2,1)S(1)} collective-permute-done((bf16[128,2048]{1,0:T(8,128)(2,1)S(1)}, bf16[128,2048]{1,0:T(8,128)(2,1)S(1)}, u32[]{:S(2)}, u32[]{:S(2)}) %collective-permute-start.16) | collective-permute-done | bytes 524320 | tf_op jit(solution)/shard_map/ppermute | solution.py:50
  57.6 5.2 %collective-permute-start.22 = (bf16[128,2048]{1,0:T(8,128)(2,1)S(1)}, bf16[128,2048]{1,0:T(8,128)(2,1)S(1)}, u32[]{:S(2)}, u32[]{:S(2)}) collective-permute-start(bf16[128,2048]{1,0:T(8,128)(2,1)S(1)} %add_share.16), channel_id=1, source_target_pairs={{0,8},{2,10},{4,12},{6,14},{8,16},{9,1},{10,18},{11,3},{12,20},{13... | collective-permute-start | bytes 1572872 | tf_op jit(solution)/shard_map/ppermute | solution.py:50
  64.1 3.9 %collective-permute-done.19.got_ref.refs_3_ = bf16[128,2048]{1,0:T(8,128)(2,1)S(1)} collective-permute-done((bf16[128,2048]{1,0:T(8,128)(2,1)S(1)}, bf16[128,2048]{1,0:T(8,128)(2,1)S(1)}, u32[]{:S(2)}, u32[]{:S(2)}) %collective-permute-start.19) | collective-permute-done | bytes 524320 | tf_op jit(solution)/shard_map/ppermute | solution.py:50
  69.8 5.0 %collective-permute-start.26 = (bf16[128,2048]{1,0:T(8,128)(2,1)S(1)}, bf16[128,2048]{1,0:T(8,128)(2,1)S(1)}, u32[]{:S(2)}, u32[]{:S(2)}) collective-permute-start(bf16[128,2048]{1,0:T(8,128)(2,1)S(1)} %add_share.18), channel_id=1, source_target_pairs={{0,8},{2,10},{4,12},{6,14},{8,16},{9,1},{10,18},{11,3},{12,20},{13... | collective-permute-start | bytes 1572872 | tf_op jit(solution)/shard_map/ppermute | solution.py:50
  77.0 4.3 %collective-permute-done.21 = bf16[2,64,512]{2,1,0:T(8,128)(2,1)S(1)} collective-permute-done((bf16[2,64,512]{2,1,0:T(8,128)(2,1)S(1)}, bf16[2,64,512]{2,1,0:T(8,128)(2,1)S(1)}, u32[]{:S(2)}, u32[]{:S(2)}) %collective-permute-start.21) | collective-permute-done | bytes 131104 | tf_op jit(solution)/shard_map/ppermute | solution.py:184
  82.1 4.6 %collective-permute-start.30 = (bf16[128,2048]{1,0:T(8,128)(2,1)S(1)}, bf16[128,2048]{1,0:T(8,128)(2,1)S(1)}, u32[]{:S(2)}, u32[]{:S(2)}) collective-permute-start(bf16[128,2048]{1,0:T(8,128)(2,1)S(1)} %add_share.20), channel_id=1, source_target_pairs={{0,8},{2,10},{4,12},{6,14},{8,16},{9,1},{10,18},{11,3},{12,20},{13... | collective-permute-start | bytes 1572872 | tf_op jit(solution)/shard_map/ppermute | solution.py:50
  89.8 5.2 %collective-permute-start.28 = (bf16[128,2048]{1,0:T(8,128)(2,1)S(1)}, bf16[128,2048]{1,0:T(8,128)(2,1)S(1)}, u32[]{:S(2)}, u32[]{:S(2)}) collective-permute-start(bf16[128,2048]{1,0:T(8,128)(2,1)S(1)} %add_share.22), channel_id=1, source_target_pairs={{0,8},{2,10},{4,12},{6,14},{8,16},{9,1},{10,18},{11,3},{12,20},{13... | collective-permute-start | bytes 1572872 | tf_op jit(solution)/shard_map/ppermute | solution.py:50
  97.9 7.6 %weight_product.1 = bf16[1024,2048]{1,0:T(8,128)(2,1)} custom-call(bf16[256,1024]{1,0:T(8,128)(2,1)S(1)} %lay_strips.3.own_cot_ref, bf16[768,1024]{1,0:T(8,128)(2,1)S(1)} %lay_strips.2.cot_ref, bf16[256,2048]{1,0:T(8,128)(2,1)S(1)} %pad_maximum_fusion.own_ref, bf16[128,2048]{1,0:T(8,128)(2,1)S(1)} %collective-permute-done.3.got_ref.refs_0_, ...), custom_call_target="tpu_custom_call" | custom-call | flops 4294967296 | bytes 8388608 | tf_op jit(solution)/shard_map/weight_product/pallas_call | solution.py:129
  107.0 3.7 %collective-permute-done.29.refs_4_ = bf16[128,2048]{1,0:T(8,128)(2,1)S(1)} collective-permute-done((bf16[128,2048]{1,0:T(8,128)(2,1)S(1)}, bf16[128,2048]{1,0:T(8,128)(2,1)S(1)}, u32[]{:S(2)}, u32[]{:S(2)}) %collective-permute-start.29) | collective-permute-done | bytes 524320 | tf_op jit(solution)/shard_map/ppermute | solution.py:50
  (74 shorter events, 26.9 us)
Async XLA Ops:
  1.6 6.8 %collective-permute-start = (bf16[64,512]{1,0:T(8,128)(2,1)S(1)}, bf16[64,512]{1,0:T(8,128)(2,1)S(1)}, u32[]{:S(2)}, u32[]{:S(2)}) collective-permute-start(bf16[64,512]{1,0:T(8,128)(2,1)S(1)} %get-tuple-element.82), channel_id=1, source_target_pairs={{0,2},{1,3},{2,0},{3,1},{4,6},{5,7},{6,4},{7,5},{8,10},{9,11},{10,... | collective-permute-start | bytes 196616 | tf_op jit(solution)/shard_map/ppermute | solution.py:184
  11.4 10.3 %collective-permute-start.4 = (bf16[64,512]{1,0:T(8,128)(2,1)S(1)}, bf16[64,512]{1,0:T(8,128)(2,1)S(1)}, u32[]{:S(2)}, u32[]{:S(2)}) collective-permute-start(bf16[64,512]{1,0:T(8,128)(2,1)S(1)} %get-tuple-element.77), channel_id=1, source_target_pairs={{0,8},{8,0},{16,24},{24,16},{1,9},{9,1},{17,25},{25,17},{2,10},{10... | collective-permute-start | bytes 196616 | tf_op jit(solution)/shard_map/ppermute | solution.py:215
  13.0 8.7 %collective-permute-start.5 = (bf16[64,512]{1,0:T(8,128)(2,1)S(1)}, bf16[64,512]{1,0:T(8,128)(2,1)S(1)}, u32[]{:S(2)}, u32[]{:S(2)}) collective-permute-start(bf16[64,512]{1,0:T(8,128)(2,1)S(1)} %get-tuple-element.79), channel_id=1, source_target_pairs={{0,16},{8,24},{16,0},{24,8},{1,17},{9,25},{17,1},{25,9},{2,18},{10... | collective-permute-start | bytes 196616 | tf_op jit(solution)/shard_map/ppermute | solution.py:215
  15.9 17.2 %collective-permute-start.10 = (bf16[128,2048]{1,0:T(8,128)(2,1)S(1)}, bf16[128,2048]{1,0:T(8,128)(2,1)S(1)}, u32[]{:S(2)}, u32[]{:S(2)}) collective-permute-start(bf16[128,2048]{1,0:T(8,128)(2,1)S(1)} %get-tuple-element.68), channel_id=1, source_target_pairs={{1,9},{3,11},{5,13},{7,15},{8,0},{9,17},{10,2},{11,19},{12,4},{13,... | collective-permute-start | bytes 1572872 | tf_op jit(solution)/shard_map/ppermute | solution.py:50
  17.1 18.6 %collective-permute-start.3 = (bf16[128,2048]{1,0:T(8,128)(2,1)S(1)}, bf16[128,2048]{1,0:T(8,128)(2,1)S(1)}, u32[]{:S(2)}, u32[]{:S(2)}) collective-permute-start(bf16[128,2048]{1,0:T(8,128)(2,1)S(1)} %get-tuple-element.68), channel_id=1, source_target_pairs={{0,8},{2,10},{4,12},{6,14},{8,16},{9,1},{10,18},{11,3},{12,20},{13... | collective-permute-start | bytes 1572872 | tf_op jit(solution)/shard_map/ppermute | solution.py:50
  21.8 6.9 %collective-permute-start.9 = (bf16[3,64,512]{2,1,0:T(8,128)(2,1)S(1)}, bf16[3,64,512]{2,1,0:T(8,128)(2,1)S(1)}, u32[]{:S(2)}, u32[]{:S(2)}) collective-permute-start(bf16[3,64,512]{2,1,0:T(8,128)(2,1)S(1)} %pad_maximum_fusion.3.refs_0_), channel_id=1, source_target_pairs={{0,6},{1,7},{2,4},{3,5},{4,2},{5,3},{6,0},{7,1},{8,14},{9,15},{10,... | collective-permute-start | bytes 589832 | tf_op jit(solution)/shard_map/ppermute | solution.py:184
  22.4 8.7 %collective-permute-start.7 = (bf16[3,64,512]{2,1,0:T(8,128)(2,1)S(1)}, bf16[3,64,512]{2,1,0:T(8,128)(2,1)S(1)}, u32[]{:S(2)}, u32[]{:S(2)}) collective-permute-start(bf16[3,64,512]{2,1,0:T(8,128)(2,1)S(1)} %pad_maximum_fusion.3.refs_0_), channel_id=1, source_target_pairs={{0,2},{1,3},{2,0},{3,1},{4,6},{5,7},{6,4},{7,5},{8,10},{9,11},{10,... | collective-permute-start | bytes 589832 | tf_op jit(solution)/shard_map/ppermute | solution.py:184
  23.9 7.3 %collective-permute-start.8 = (bf16[3,64,512]{2,1,0:T(8,128)(2,1)S(1)}, bf16[3,64,512]{2,1,0:T(8,128)(2,1)S(1)}, u32[]{:S(2)}, u32[]{:S(2)}) collective-permute-start(bf16[3,64,512]{2,1,0:T(8,128)(2,1)S(1)} %pad_maximum_fusion.3.refs_0_), channel_id=1, source_target_pairs={{0,4},{1,5},{2,6},{3,7},{4,0},{5,1},{6,2},{7,3},{8,12},{9,13},{10,... | collective-permute-start | bytes 589832 | tf_op jit(solution)/shard_map/ppermute | solution.py:184
  28.8 10.7 %collective-permute-start.15 = (bf16[128,2048]{1,0:T(8,128)(2,1)S(1)}, bf16[128,2048]{1,0:T(8,128)(2,1)S(1)}, u32[]{:S(2)}, u32[]{:S(2)}) collective-permute-start(bf16[128,2048]{1,0:T(8,128)(2,1)S(1)} %get-tuple-element.67), channel_id=1, source_target_pairs={{0,8},{2,10},{4,12},{6,14},{8,16},{9,1},{10,18},{11,3},{12,20},{13... | collective-permute-start | bytes 1572872 | tf_op jit(solution)/shard_map/ppermute | solution.py:50
  31.2 20.5 %collective-permute-start.17 = (bf16[128,2048]{1,0:T(8,128)(2,1)S(1)}, bf16[128,2048]{1,0:T(8,128)(2,1)S(1)}, u32[]{:S(2)}, u32[]{:S(2)}) collective-permute-start(bf16[128,2048]{1,0:T(8,128)(2,1)S(1)} %get-tuple-element.67), channel_id=1, source_target_pairs={{1,9},{3,11},{5,13},{7,15},{8,0},{9,17},{10,2},{11,19},{12,4},{13,... | collective-permute-start | bytes 1572872 | tf_op jit(solution)/shard_map/ppermute | solution.py:50
  40.4 16.4 %collective-permute-start.16 = (bf16[128,2048]{1,0:T(8,128)(2,1)S(1)}, bf16[128,2048]{1,0:T(8,128)(2,1)S(1)}, u32[]{:S(2)}, u32[]{:S(2)}) collective-permute-start(bf16[128,2048]{1,0:T(8,128)(2,1)S(1)} %add_share.12), channel_id=1, source_target_pairs={{0,8},{2,10},{4,12},{6,14},{8,16},{9,1},{10,18},{11,3},{12,20},{13... | collective-permute-start | bytes 1572872 | tf_op jit(solution)/shard_map/ppermute | solution.py:50
  44.6 18.2 %collective-permute-start.20 = (bf16[128,2048]{1,0:T(8,128)(2,1)S(1)}, bf16[128,2048]{1,0:T(8,128)(2,1)S(1)}, u32[]{:S(2)}, u32[]{:S(2)}) collective-permute-start(bf16[128,2048]{1,0:T(8,128)(2,1)S(1)} %add_share.13), channel_id=1, source_target_pairs={{1,9},{3,11},{5,13},{7,15},{8,0},{9,17},{10,2},{11,19},{12,4},{13,... | collective-permute-start | bytes 1572872 | tf_op jit(solution)/shard_map/ppermute | solution.py:50
  46.6 21.4 %collective-permute-start.19 = (bf16[128,2048]{1,0:T(8,128)(2,1)S(1)}, bf16[128,2048]{1,0:T(8,128)(2,1)S(1)}, u32[]{:S(2)}, u32[]{:S(2)}) collective-permute-start(bf16[128,2048]{1,0:T(8,128)(2,1)S(1)} %add_share.14), channel_id=1, source_target_pairs={{0,8},{2,10},{4,12},{6,14},{8,16},{9,1},{10,18},{11,3},{12,20},{13... | collective-permute-start | bytes 1572872 | tf_op jit(solution)/shard_map/ppermute | solution.py:50
  51.8 23.0 %collective-permute-start.23 = (bf16[128,2048]{1,0:T(8,128)(2,1)S(1)}, bf16[128,2048]{1,0:T(8,128)(2,1)S(1)}, u32[]{:S(2)}, u32[]{:S(2)}) collective-permute-start(bf16[128,2048]{1,0:T(8,128)(2,1)S(1)} %add_share.15), channel_id=1, source_target_pairs={{1,9},{3,11},{5,13},{7,15},{8,0},{9,17},{10,2},{11,19},{12,4},{13,... | collective-permute-start | bytes 1572872 | tf_op jit(solution)/shard_map/ppermute | solution.py:50
  57.6 23.7 %collective-permute-start.22 = (bf16[128,2048]{1,0:T(8,128)(2,1)S(1)}, bf16[128,2048]{1,0:T(8,128)(2,1)S(1)}, u32[]{:S(2)}, u32[]{:S(2)}) collective-permute-start(bf16[128,2048]{1,0:T(8,128)(2,1)S(1)} %add_share.16), channel_id=1, source_target_pairs={{0,8},{2,10},{4,12},{6,14},{8,16},{9,1},{10,18},{11,3},{12,20},{13... | collective-permute-start | bytes 1572872 | tf_op jit(solution)/shard_map/ppermute | solution.py:50
  62.8 23.9 %collective-permute-start.27 = (bf16[128,2048]{1,0:T(8,128)(2,1)S(1)}, bf16[128,2048]{1,0:T(8,128)(2,1)S(1)}, u32[]{:S(2)}, u32[]{:S(2)}) collective-permute-start(bf16[128,2048]{1,0:T(8,128)(2,1)S(1)} %add_share.17), channel_id=1, source_target_pairs={{1,9},{3,11},{5,13},{7,15},{8,0},{9,17},{10,2},{11,19},{12,4},{13,... | collective-permute-start | bytes 1572872 | tf_op jit(solution)/shard_map/ppermute | solution.py:50
  68.1 8.1 %collective-permute-start.18 = (bf16[1,64,512]{2,1,0:T(8,128)(2,1)S(1)}, bf16[1,64,512]{2,1,0:T(8,128)(2,1)S(1)}, u32[]{:S(2)}, u32[]{:S(2)}) collective-permute-start(bf16[1,64,512]{2,1,0:T(8,128)(2,1)S(1)} %get-tuple-element.49), channel_id=1, source_target_pairs={{0,2},{1,3},{2,0},{3,1},{4,6},{5,7},{6,4},{7,5},{8,10},{9,11},{10,... | collective-permute-start | bytes 196616 | tf_op jit(solution)/shard_map/ppermute | solution.py:184
  69.8 19.2 %collective-permute-start.26 = (bf16[128,2048]{1,0:T(8,128)(2,1)S(1)}, bf16[128,2048]{1,0:T(8,128)(2,1)S(1)}, u32[]{:S(2)}, u32[]{:S(2)}) collective-permute-start(bf16[128,2048]{1,0:T(8,128)(2,1)S(1)} %add_share.18), channel_id=1, source_target_pairs={{0,8},{2,10},{4,12},{6,14},{8,16},{9,1},{10,18},{11,3},{12,20},{13... | collective-permute-start | bytes 1572872 | tf_op jit(solution)/shard_map/ppermute | solution.py:50
  74.9 20.1 %collective-permute-start.25 = (bf16[128,2048]{1,0:T(8,128)(2,1)S(1)}, bf16[128,2048]{1,0:T(8,128)(2,1)S(1)}, u32[]{:S(2)}, u32[]{:S(2)}) collective-permute-start(bf16[128,2048]{1,0:T(8,128)(2,1)S(1)} %add_share.19), channel_id=1, source_target_pairs={{1,9},{3,11},{5,13},{7,15},{8,0},{9,17},{10,2},{11,19},{12,4},{13,... | collective-permute-start | bytes 1572872 | tf_op jit(solution)/shard_map/ppermute | solution.py:50
  82.1 23.5 %collective-permute-start.30 = (bf16[128,2048]{1,0:T(8,128)(2,1)S(1)}, bf16[128,2048]{1,0:T(8,128)(2,1)S(1)}, u32[]{:S(2)}, u32[]{:S(2)}) collective-permute-start(bf16[128,2048]{1,0:T(8,128)(2,1)S(1)} %add_share.20), channel_id=1, source_target_pairs={{0,8},{2,10},{4,12},{6,14},{8,16},{9,1},{10,18},{11,3},{12,20},{13... | collective-permute-start | bytes 1572872 | tf_op jit(solution)/shard_map/ppermute | solution.py:50
  86.6 9.9 %collective-permute-start.24 = (bf16[4,64,512]{2,1,0:T(8,128)(2,1)S(1)}, bf16[4,64,512]{2,1,0:T(8,128)(2,1)S(1)}, u32[]{:S(2)}, u32[]{:S(2)}) collective-permute-start(bf16[4,64,512]{2,1,0:T(8,128)(2,1)S(1)} %pad_maximum_fusion.2), channel_id=1, source_target_pairs={{0,1},{1,0},{2,3},{3,2},{4,5},{5,4},{6,7},{7,6},{8,9},{9,8},{10,11... | collective-permute-start | bytes 786440 | tf_op jit(solution)/shard_map/ppermute | solution.py:184
  86.8 18.8 %collective-permute-start.31 = (bf16[128,2048]{1,0:T(8,128)(2,1)S(1)}, bf16[128,2048]{1,0:T(8,128)(2,1)S(1)}, u32[]{:S(2)}, u32[]{:S(2)}) collective-permute-start(bf16[128,2048]{1,0:T(8,128)(2,1)S(1)} %add_share.21), channel_id=1, source_target_pairs={{1,9},{3,11},{5,13},{7,15},{8,0},{9,17},{10,2},{11,19},{12,4},{13,... | collective-permute-start | bytes 1572872 | tf_op jit(solution)/shard_map/ppermute | solution.py:50
  89.8 20.9 %collective-permute-start.28 = (bf16[128,2048]{1,0:T(8,128)(2,1)S(1)}, bf16[128,2048]{1,0:T(8,128)(2,1)S(1)}, u32[]{:S(2)}, u32[]{:S(2)}) collective-permute-start(bf16[128,2048]{1,0:T(8,128)(2,1)S(1)} %add_share.22), channel_id=1, source_target_pairs={{0,8},{2,10},{4,12},{6,14},{8,16},{9,1},{10,18},{11,3},{12,20},{13... | collective-permute-start | bytes 1572872 | tf_op jit(solution)/shard_map/ppermute | solution.py:50
  95.2 15.4 %collective-permute-start.29 = (bf16[128,2048]{1,0:T(8,128)(2,1)S(1)}, bf16[128,2048]{1,0:T(8,128)(2,1)S(1)}, u32[]{:S(2)}, u32[]{:S(2)}) collective-permute-start(bf16[128,2048]{1,0:T(8,128)(2,1)S(1)} %add_share.23), channel_id=1, source_target_pairs={{1,9},{3,11},{5,13},{7,15},{8,0},{9,17},{10,2},{11,19},{12,4},{13,... | collective-permute-start | bytes 1572872 | tf_op jit(solution)/shard_map/ppermute | solution.py:50
  (11 other events, 77.8 us)

commit v5 on v1

--- a/solution.py
+++ b/solution.py
@@ -142,7 +142,7 @@
 
 def finish(gate_pre, up_pre, share, fore, back, start, grads):
     span, width = fore.shape
-    tile = 512 if width % 512 == 0 else width
+    tile = 1024 if width % 1024 == 0 else width
     old = () if grads is None else tuple(grads)
 
     def kernel(*refs):

time: 114 us -> 114 us (level)
  no operation moved by 1% of the time
where the time goes in v5:
time: 114 us; the launch traced here: 113 us
  starting transfers between devices  62.9 us (55%)
  waiting for transfers between devices  28.7 us (25%)
  Pallas kernels  15.6 us (14%)
  other arithmetic  2.36 us (2%)
  between operations  1.32 us (1%)
  matrix products  1.25 us (1%)
    ppermute x16, starting transfers between devices, ring(): return lax.ppermute(value, ('row', 'col'), pairs)  45.6 us
    ppermute x16, waiting for transfers between devices, ring(): return lax.ppermute(value, ('row', 'col'), pairs)  17.9 us
    ppermute x13, starting transfers between devices, swap(): lax.ppermute(value, 'col', [(at, at ^ bits) for at in range(lax.axis_size...  12.9 us
    ppermute x13, waiting for transfers between devices, swap(): lax.ppermute(value, 'col', [(at, at ^ bits) for at in range(lax.axis_size...  10.7 us
    pallas_call x1, Pallas kernels, weight_product(): pl.pallas_call(kernel, out_shape=jax.ShapeDtypeStruct((cot.shape[1], widt...  7.6 us
    pallas_call x12, Pallas kernels, add_share(): pl.pallas_call(kernel, out_shape=jax.ShapeDtypeStruct(got.shape, got.dtyp...  4.89 us
    ppermute x3, starting transfers between devices, across(): lax.ppermute(piece, 'row', [(at, at ^ bits) for at in range(rows)])  4.45 us
    pallas_call x2, Pallas kernels, finish(): pl.pallas_call(kernel, out_shape=[jax.ShapeDtypeStruct(gate_pre.shape, jn...  2.84 us
  transfers between devices with their start and end apart: 32, of which 15 were waited for; matrix products, arithmetic and copies ran while one was open for 3% of the time, Pallas kernels for 12%

profile of v5, /device:TPU:0, one launch (start us, length us, event | category | flops | bytes accessed | tf_op | source)
XLA Modules:
  0.0 113.1 jit_solution(11985070798452286051)
XLA Ops:
  1.6 3.0 %collective-permute-start = (bf16[64,512]{1,0:T(8,128)(2,1)S(1)}, bf16[64,512]{1,0:T(8,128)(2,1)S(1)}, u32[]{:S(2)}, u32[]{:S(2)}) collective-permute-start(bf16[64,512]{1,0:T(8,128)(2,1)S(1)} %get-tuple-element.82), channel_id=1, source_target_pairs={{0,2},{1,3},{2,0},{3,1},{4,6},{5,7},{6,4},{7,5},{8,10},{9,11},{10,... | collective-permute-start | bytes 196616 | tf_op jit(solution)/shard_map/ppermute | solution.py:184
  6.2 2.2 %fusion.8 = (bf16[128,2048]{1,0:T(8,128)(2,1)S(1)}, bf16[128,2048]{1,0:T(8,128)(2,1)S(1)}) fusion(bf16[256,2048]{1,0:T(8,128)(2,1)} %refs_1_.1, bf16[256,2048]{1,0:T(8,128)(2,1)} %refs_0_.1), kind=kLoop, calls=%fused_computation.13 | loop fusion | flops 4194304 | bytes 3145728 | tf_op jit(solution)/shard_map/convert_element_type | solution.py:249
  8.9 2.4 %collective-permute-done.2 = bf16[64,512]{1,0:T(8,128)(2,1)S(1)} collective-permute-done((bf16[64,512]{1,0:T(8,128)(2,1)S(1)}, bf16[64,512]{1,0:T(8,128)(2,1)S(1)}, u32[]{:S(2)}, u32[]{:S(2)}) %collective-permute-start.2) | collective-permute-done | bytes 65568 | tf_op jit(solution)/shard_map/ppermute | solution.py:184
  11.4 1.6 %collective-permute-start.7 = (bf16[64,512]{1,0:T(8,128)(2,1)S(1)}, bf16[64,512]{1,0:T(8,128)(2,1)S(1)}, u32[]{:S(2)}, u32[]{:S(2)}) collective-permute-start(bf16[64,512]{1,0:T(8,128)(2,1)S(1)} %get-tuple-element.77), channel_id=1, source_target_pairs={{0,8},{8,0},{16,24},{24,16},{1,9},{9,1},{17,25},{25,17},{2,10},{10... | collective-permute-start | bytes 196616 | tf_op jit(solution)/shard_map/ppermute | solution.py:215
  13.0 2.6 %collective-permute-start.8 = (bf16[64,512]{1,0:T(8,128)(2,1)S(1)}, bf16[64,512]{1,0:T(8,128)(2,1)S(1)}, u32[]{:S(2)}, u32[]{:S(2)}) collective-permute-start(bf16[64,512]{1,0:T(8,128)(2,1)S(1)} %get-tuple-element.79), channel_id=1, source_target_pairs={{0,16},{8,24},{16,0},{24,8},{1,17},{9,25},{17,1},{25,9},{2,18},{10... | collective-permute-start | bytes 196616 | tf_op jit(solution)/shard_map/ppermute | solution.py:215
  17.1 4.6 %collective-permute-start.6 = (bf16[128,2048]{1,0:T(8,128)(2,1)S(1)}, bf16[128,2048]{1,0:T(8,128)(2,1)S(1)}, u32[]{:S(2)}, u32[]{:S(2)}) collective-permute-start(bf16[128,2048]{1,0:T(8,128)(2,1)S(1)} %get-tuple-element.68), channel_id=1, source_target_pairs={{0,8},{2,10},{4,12},{6,14},{8,16},{9,1},{10,18},{11,3},{12,20},{13... | collective-permute-start | bytes 1572872 | tf_op jit(solution)/shard_map/ppermute | solution.py:50
  23.9 1.5 %collective-permute-start.11 = (bf16[3,64,512]{2,1,0:T(8,128)(2,1)S(1)}, bf16[3,64,512]{2,1,0:T(8,128)(2,1)S(1)}, u32[]{:S(2)}, u32[]{:S(2)}) collective-permute-start(bf16[3,64,512]{2,1,0:T(8,128)(2,1)S(1)} %pad_maximum_fusion.3.refs_0_), channel_id=1, source_target_pairs={{0,4},{1,5},{2,6},{3,7},{4,0},{5,1},{6,2},{7,3},{8,12},{9,13},{10,... | collective-permute-start | bytes 589832 | tf_op jit(solution)/shard_map/ppermute | solution.py:184
  25.4 3.4 %collective-permute-done.12.refs_3_ = bf16[3,64,512]{2,1,0:T(8,128)(2,1)S(1)} collective-permute-done((bf16[3,64,512]{2,1,0:T(8,128)(2,1)S(1)}, bf16[3,64,512]{2,1,0:T(8,128)(2,1)S(1)}, u32[]{:S(2)}, u32[]{:S(2)}) %collective-permute-start.12) | collective-permute-done | bytes 196640 | tf_op jit(solution)/shard_map/ppermute | solution.py:184
  28.8 2.3 %collective-permute-start.4 = (bf16[128,2048]{1,0:T(8,128)(2,1)S(1)}, bf16[128,2048]{1,0:T(8,128)(2,1)S(1)}, u32[]{:S(2)}, u32[]{:S(2)}) collective-permute-start(bf16[128,2048]{1,0:T(8,128)(2,1)S(1)} %get-tuple-element.67), channel_id=1, source_target_pairs={{0,8},{2,10},{4,12},{6,14},{8,16},{9,1},{10,18},{11,3},{12,20},{13... | collective-permute-start | bytes 1572872 | tf_op jit(solution)/shard_map/ppermute | solution.py:50
  33.1 2.6 %collective-permute-start.14 = (bf16[3,64,512]{2,1,0:T(8,128)(2,1)S(1)}, bf16[3,64,512]{2,1,0:T(8,128)(2,1)S(1)}, u32[]{:S(2)}, u32[]{:S(2)}) collective-permute-start(bf16[3,64,512]{2,1,0:T(8,128)(2,1)S(1)} %collective-permute-done.10.refs_1_), channel_id=1, source_target_pairs={{0,1},{1,0},{2,3},{3,2},{4,5},{5,4},{6,7},{7,6},{8,9},{9,8},{10,11... | collective-permute-start | bytes 589832 | tf_op jit(solution)/shard_map/ppermute | solution.py:184
  37.1 2.4 %collective-permute-done.4.got_ref.refs_1_ = bf16[128,2048]{1,0:T(8,128)(2,1)S(1)} collective-permute-done((bf16[128,2048]{1,0:T(8,128)(2,1)S(1)}, bf16[128,2048]{1,0:T(8,128)(2,1)S(1)}, u32[]{:S(2)}, u32[]{:S(2)}) %collective-permute-start.4) | collective-permute-done | bytes 524320 | tf_op jit(solution)/shard_map/ppermute | solution.py:50
  40.4 4.1 %collective-permute-start.19 = (bf16[128,2048]{1,0:T(8,128)(2,1)S(1)}, bf16[128,2048]{1,0:T(8,128)(2,1)S(1)}, u32[]{:S(2)}, u32[]{:S(2)}) collective-permute-start(bf16[128,2048]{1,0:T(8,128)(2,1)S(1)} %add_share.12), channel_id=1, source_target_pairs={{0,8},{2,10},{4,12},{6,14},{8,16},{9,1},{10,18},{11,3},{12,20},{13... | collective-permute-start | bytes 1572872 | tf_op jit(solution)/shard_map/ppermute | solution.py:50
  46.6 5.1 %collective-permute-start.22 = (bf16[128,2048]{1,0:T(8,128)(2,1)S(1)}, bf16[128,2048]{1,0:T(8,128)(2,1)S(1)}, u32[]{:S(2)}, u32[]{:S(2)}) collective-permute-start(bf16[128,2048]{1,0:T(8,128)(2,1)S(1)} %add_share.14), channel_id=1, source_target_pairs={{0,8},{2,10},{4,12},{6,14},{8,16},{9,1},{10,18},{11,3},{12,20},{13... | collective-permute-start | bytes 1572872 | tf_op jit(solution)/shard_map/ppermute | solution.py:50
  54.0 3.4 %collective-permute-done.17 = bf16[1,64,512]{2,1,0:T(8,128)(2,1)S(1)} collective-permute-done((bf16[1,64,512]{2,1,0:T(8,128)(2,1)S(1)}, bf16[1,64,512]{2,1,0:T(8,128)(2,1)S(1)}, u32[]{:S(2)}, u32[]{:S(2)}) %collective-permute-start.17) | collective-permute-done | bytes 65568 | tf_op jit(solution)/shard_map/ppermute | solution.py:184
  58.2 1.8 %collective-permute-done.18.got_ref.refs_8_ = bf16[128,2048]{1,0:T(8,128)(2,1)S(1)} collective-permute-done((bf16[128,2048]{1,0:T(8,128)(2,1)S(1)}, bf16[128,2048]{1,0:T(8,128)(2,1)S(1)}, u32[]{:S(2)}, u32[]{:S(2)}) %collective-permute-start.18) | collective-permute-done | bytes 524320 | tf_op jit(solution)/shard_map/ppermute | solution.py:50
  61.9 4.6 %collective-permute-start.27 = (bf16[128,2048]{1,0:T(8,128)(2,1)S(1)}, bf16[128,2048]{1,0:T(8,128)(2,1)S(1)}, u32[]{:S(2)}, u32[]{:S(2)}) collective-permute-start(bf16[128,2048]{1,0:T(8,128)(2,1)S(1)} %add_share.16), channel_id=1, source_target_pairs={{0,8},{2,10},{4,12},{6,14},{8,16},{9,1},{10,18},{11,3},{12,20},{13... | collective-permute-start | bytes 1572872 | tf_op jit(solution)/shard_map/ppermute | solution.py:50
  66.5 1.6 %collective-permute-done.22.got_ref.refs_3_ = bf16[128,2048]{1,0:T(8,128)(2,1)S(1)} collective-permute-done((bf16[128,2048]{1,0:T(8,128)(2,1)S(1)}, bf16[128,2048]{1,0:T(8,128)(2,1)S(1)}, u32[]{:S(2)}, u32[]{:S(2)}) %collective-permute-start.22) | collective-permute-done | bytes 524320 | tf_op jit(solution)/shard_map/ppermute | solution.py:50
  70.4 5.8 %collective-permute-start.25 = (bf16[128,2048]{1,0:T(8,128)(2,1)S(1)}, bf16[128,2048]{1,0:T(8,128)(2,1)S(1)}, u32[]{:S(2)}, u32[]{:S(2)}) collective-permute-start(bf16[128,2048]{1,0:T(8,128)(2,1)S(1)} %add_share.18), channel_id=1, source_target_pairs={{0,8},{2,10},{4,12},{6,14},{8,16},{9,1},{10,18},{11,3},{12,20},{13... | collective-permute-start | bytes 1572872 | tf_op jit(solution)/shard_map/ppermute | solution.py:50
  76.3 3.0 %collective-permute-done.27.got_ref.refs_4_ = bf16[128,2048]{1,0:T(8,128)(2,1)S(1)} collective-permute-done((bf16[128,2048]{1,0:T(8,128)(2,1)S(1)}, bf16[128,2048]{1,0:T(8,128)(2,1)S(1)}, u32[]{:S(2)}, u32[]{:S(2)}) %collective-permute-start.27) | collective-permute-done | bytes 524320 | tf_op jit(solution)/shard_map/ppermute | solution.py:50
  80.0 4.4 %collective-permute-start.30 = (bf16[128,2048]{1,0:T(8,128)(2,1)S(1)}, bf16[128,2048]{1,0:T(8,128)(2,1)S(1)}, u32[]{:S(2)}, u32[]{:S(2)}) collective-permute-start(bf16[128,2048]{1,0:T(8,128)(2,1)S(1)} %add_share.20), channel_id=1, source_target_pairs={{0,8},{2,10},{4,12},{6,14},{8,16},{9,1},{10,18},{11,3},{12,20},{13... | collective-permute-start | bytes 1572872 | tf_op jit(solution)/shard_map/ppermute | solution.py:50
  85.8 4.7 %collective-permute-done.25.got_ref.refs_5_ = bf16[128,2048]{1,0:T(8,128)(2,1)S(1)} collective-permute-done((bf16[128,2048]{1,0:T(8,128)(2,1)S(1)}, bf16[128,2048]{1,0:T(8,128)(2,1)S(1)}, u32[]{:S(2)}, u32[]{:S(2)}) %collective-permute-start.25) | collective-permute-done | bytes 524320 | tf_op jit(solution)/shard_map/ppermute | solution.py:50
  91.3 4.4 %collective-permute-start.28 = (bf16[128,2048]{1,0:T(8,128)(2,1)S(1)}, bf16[128,2048]{1,0:T(8,128)(2,1)S(1)}, u32[]{:S(2)}, u32[]{:S(2)}) collective-permute-start(bf16[128,2048]{1,0:T(8,128)(2,1)S(1)} %add_share.22), channel_id=1, source_target_pairs={{0,8},{2,10},{4,12},{6,14},{8,16},{9,1},{10,18},{11,3},{12,20},{13... | collective-permute-start | bytes 1572872 | tf_op jit(solution)/shard_map/ppermute | solution.py:50
  98.5 7.6 %weight_product.1 = bf16[1024,2048]{1,0:T(8,128)(2,1)} custom-call(bf16[256,1024]{1,0:T(8,128)(2,1)S(1)} %lay_strips.3.own_cot_ref, bf16[768,1024]{1,0:T(8,128)(2,1)S(1)} %lay_strips.2.cot_ref, bf16[256,2048]{1,0:T(8,128)(2,1)S(1)} %pad_maximum_fusion.own_ref, bf16[128,2048]{1,0:T(8,128)(2,1)S(1)} %collective-permute-done.6.got_ref.refs_0_, ...), custom_call_target="tpu_custom_call" | custom-call | flops 4294967296 | bytes 8388608 | tf_op jit(solution)/shard_map/weight_product/pallas_call | solution.py:129
  107.6 3.0 %collective-permute-done.29.refs_4_ = bf16[128,2048]{1,0:T(8,128)(2,1)S(1)} collective-permute-done((bf16[128,2048]{1,0:T(8,128)(2,1)S(1)}, bf16[128,2048]{1,0:T(8,128)(2,1)S(1)}, u32[]{:S(2)}, u32[]{:S(2)}) %collective-permute-start.29) | collective-permute-done | bytes 524320 | tf_op jit(solution)/shard_map/ppermute | solution.py:50
  (74 shorter events, 29.8 us)
Async XLA Ops:
  1.6 6.8 %collective-permute-start = (bf16[64,512]{1,0:T(8,128)(2,1)S(1)}, bf16[64,512]{1,0:T(8,128)(2,1)S(1)}, u32[]{:S(2)}, u32[]{:S(2)}) collective-permute-start(bf16[64,512]{1,0:T(8,128)(2,1)S(1)} %get-tuple-element.82), channel_id=1, source_target_pairs={{0,2},{1,3},{2,0},{3,1},{4,6},{5,7},{6,4},{7,5},{8,10},{9,11},{10,... | collective-permute-start | bytes 196616 | tf_op jit(solution)/shard_map/ppermute | solution.py:184
  11.4 10.3 %collective-permute-start.7 = (bf16[64,512]{1,0:T(8,128)(2,1)S(1)}, bf16[64,512]{1,0:T(8,128)(2,1)S(1)}, u32[]{:S(2)}, u32[]{:S(2)}) collective-permute-start(bf16[64,512]{1,0:T(8,128)(2,1)S(1)} %get-tuple-element.77), channel_id=1, source_target_pairs={{0,8},{8,0},{16,24},{24,16},{1,9},{9,1},{17,25},{25,17},{2,10},{10... | collective-permute-start | bytes 196616 | tf_op jit(solution)/shard_map/ppermute | solution.py:215
  13.0 8.7 %collective-permute-start.8 = (bf16[64,512]{1,0:T(8,128)(2,1)S(1)}, bf16[64,512]{1,0:T(8,128)(2,1)S(1)}, u32[]{:S(2)}, u32[]{:S(2)}) collective-permute-start(bf16[64,512]{1,0:T(8,128)(2,1)S(1)} %get-tuple-element.79), channel_id=1, source_target_pairs={{0,16},{8,24},{16,0},{24,8},{1,17},{9,25},{17,1},{25,9},{2,18},{10... | collective-permute-start | bytes 196616 | tf_op jit(solution)/shard_map/ppermute | solution.py:215
  15.9 17.2 %collective-permute-start.5 = (bf16[128,2048]{1,0:T(8,128)(2,1)S(1)}, bf16[128,2048]{1,0:T(8,128)(2,1)S(1)}, u32[]{:S(2)}, u32[]{:S(2)}) collective-permute-start(bf16[128,2048]{1,0:T(8,128)(2,1)S(1)} %get-tuple-element.68), channel_id=1, source_target_pairs={{1,9},{3,11},{5,13},{7,15},{8,0},{9,17},{10,2},{11,19},{12,4},{13,... | collective-permute-start | bytes 1572872 | tf_op jit(solution)/shard_map/ppermute | solution.py:50
  17.1 18.6 %collective-permute-start.6 = (bf16[128,2048]{1,0:T(8,128)(2,1)S(1)}, bf16[128,2048]{1,0:T(8,128)(2,1)S(1)}, u32[]{:S(2)}, u32[]{:S(2)}) collective-permute-start(bf16[128,2048]{1,0:T(8,128)(2,1)S(1)} %get-tuple-element.68), channel_id=1, source_target_pairs={{0,8},{2,10},{4,12},{6,14},{8,16},{9,1},{10,18},{11,3},{12,20},{13... | collective-permute-start | bytes 1572872 | tf_op jit(solution)/shard_map/ppermute | solution.py:50
  21.8 6.9 %collective-permute-start.12 = (bf16[3,64,512]{2,1,0:T(8,128)(2,1)S(1)}, bf16[3,64,512]{2,1,0:T(8,128)(2,1)S(1)}, u32[]{:S(2)}, u32[]{:S(2)}) collective-permute-start(bf16[3,64,512]{2,1,0:T(8,128)(2,1)S(1)} %pad_maximum_fusion.3.refs_0_), channel_id=1, source_target_pairs={{0,6},{1,7},{2,4},{3,5},{4,2},{5,3},{6,0},{7,1},{8,14},{9,15},{10,... | collective-permute-start | bytes 589832 | tf_op jit(solution)/shard_map/ppermute | solution.py:184
  22.4 8.7 %collective-permute-start.10 = (bf16[3,64,512]{2,1,0:T(8,128)(2,1)S(1)}, bf16[3,64,512]{2,1,0:T(8,128)(2,1)S(1)}, u32[]{:S(2)}, u32[]{:S(2)}) collective-permute-start(bf16[3,64,512]{2,1,0:T(8,128)(2,1)S(1)} %pad_maximum_fusion.3.refs_0_), channel_id=1, source_target_pairs={{0,2},{1,3},{2,0},{3,1},{4,6},{5,7},{6,4},{7,5},{8,10},{9,11},{10,... | collective-permute-start | bytes 589832 | tf_op jit(solution)/shard_map/ppermute | solution.py:184
  23.9 7.3 %collective-permute-start.11 = (bf16[3,64,512]{2,1,0:T(8,128)(2,1)S(1)}, bf16[3,64,512]{2,1,0:T(8,128)(2,1)S(1)}, u32[]{:S(2)}, u32[]{:S(2)}) collective-permute-start(bf16[3,64,512]{2,1,0:T(8,128)(2,1)S(1)} %pad_maximum_fusion.3.refs_0_), channel_id=1, source_target_pairs={{0,4},{1,5},{2,6},{3,7},{4,0},{5,1},{6,2},{7,3},{8,12},{9,13},{10,... | collective-permute-start | bytes 589832 | tf_op jit(solution)/shard_map/ppermute | solution.py:184
  28.8 10.7 %collective-permute-start.4 = (bf16[128,2048]{1,0:T(8,128)(2,1)S(1)}, bf16[128,2048]{1,0:T(8,128)(2,1)S(1)}, u32[]{:S(2)}, u32[]{:S(2)}) collective-permute-start(bf16[128,2048]{1,0:T(8,128)(2,1)S(1)} %get-tuple-element.67), channel_id=1, source_target_pairs={{0,8},{2,10},{4,12},{6,14},{8,16},{9,1},{10,18},{11,3},{12,20},{13... | collective-permute-start | bytes 1572872 | tf_op jit(solution)/shard_map/ppermute | solution.py:50
  31.2 20.5 %collective-permute-start.3 = (bf16[128,2048]{1,0:T(8,128)(2,1)S(1)}, bf16[128,2048]{1,0:T(8,128)(2,1)S(1)}, u32[]{:S(2)}, u32[]{:S(2)}) collective-permute-start(bf16[128,2048]{1,0:T(8,128)(2,1)S(1)} %get-tuple-element.67), channel_id=1, source_target_pairs={{1,9},{3,11},{5,13},{7,15},{8,0},{9,17},{10,2},{11,19},{12,4},{13,... | collective-permute-start | bytes 1572872 | tf_op jit(solution)/shard_map/ppermute | solution.py:50
  40.4 17.0 %collective-permute-start.19 = (bf16[128,2048]{1,0:T(8,128)(2,1)S(1)}, bf16[128,2048]{1,0:T(8,128)(2,1)S(1)}, u32[]{:S(2)}, u32[]{:S(2)}) collective-permute-start(bf16[128,2048]{1,0:T(8,128)(2,1)S(1)} %add_share.12), channel_id=1, source_target_pairs={{0,8},{2,10},{4,12},{6,14},{8,16},{9,1},{10,18},{11,3},{12,20},{13... | collective-permute-start | bytes 1572872 | tf_op jit(solution)/shard_map/ppermute | solution.py:50
  44.6 15.4 %collective-permute-start.18 = (bf16[128,2048]{1,0:T(8,128)(2,1)S(1)}, bf16[128,2048]{1,0:T(8,128)(2,1)S(1)}, u32[]{:S(2)}, u32[]{:S(2)}) collective-permute-start(bf16[128,2048]{1,0:T(8,128)(2,1)S(1)} %add_share.13), channel_id=1, source_target_pairs={{1,9},{3,11},{5,13},{7,15},{8,0},{9,17},{10,2},{11,19},{12,4},{13,... | collective-permute-start | bytes 1572872 | tf_op jit(solution)/shard_map/ppermute | solution.py:50
  46.6 21.4 %collective-permute-start.22 = (bf16[128,2048]{1,0:T(8,128)(2,1)S(1)}, bf16[128,2048]{1,0:T(8,128)(2,1)S(1)}, u32[]{:S(2)}, u32[]{:S(2)}) collective-permute-start(bf16[128,2048]{1,0:T(8,128)(2,1)S(1)} %add_share.14), channel_id=1, source_target_pairs={{0,8},{2,10},{4,12},{6,14},{8,16},{9,1},{10,18},{11,3},{12,20},{13... | collective-permute-start | bytes 1572872 | tf_op jit(solution)/shard_map/ppermute | solution.py:50
  51.8 17.0 %collective-permute-start.21 = (bf16[128,2048]{1,0:T(8,128)(2,1)S(1)}, bf16[128,2048]{1,0:T(8,128)(2,1)S(1)}, u32[]{:S(2)}, u32[]{:S(2)}) collective-permute-start(bf16[128,2048]{1,0:T(8,128)(2,1)S(1)} %add_share.15), channel_id=1, source_target_pairs={{1,9},{3,11},{5,13},{7,15},{8,0},{9,17},{10,2},{11,19},{12,4},{13,... | collective-permute-start | bytes 1572872 | tf_op jit(solution)/shard_map/ppermute | solution.py:50
  60.0 8.9 %collective-permute-start.20 = (bf16[2,64,512]{2,1,0:T(8,128)(2,1)S(1)}, bf16[2,64,512]{2,1,0:T(8,128)(2,1)S(1)}, u32[]{:S(2)}, u32[]{:S(2)}) collective-permute-start(bf16[2,64,512]{2,1,0:T(8,128)(2,1)S(1)} %pad_maximum_fusion.4), channel_id=1, source_target_pairs={{0,4},{1,5},{2,6},{3,7},{4,0},{5,1},{6,2},{7,3},{8,12},{9,13},{10,... | collective-permute-start | bytes 393224 | tf_op jit(solution)/shard_map/ppermute | solution.py:184
  60.6 23.8 %collective-permute-start.26 = (bf16[128,2048]{1,0:T(8,128)(2,1)S(1)}, bf16[128,2048]{1,0:T(8,128)(2,1)S(1)}, u32[]{:S(2)}, u32[]{:S(2)}) collective-permute-start(bf16[128,2048]{1,0:T(8,128)(2,1)S(1)} %add_share.17), channel_id=1, source_target_pairs={{1,9},{3,11},{5,13},{7,15},{8,0},{9,17},{10,2},{11,19},{12,4},{13,... | collective-permute-start | bytes 1572872 | tf_op jit(solution)/shard_map/ppermute | solution.py:50
  61.9 17.4 %collective-permute-start.27 = (bf16[128,2048]{1,0:T(8,128)(2,1)S(1)}, bf16[128,2048]{1,0:T(8,128)(2,1)S(1)}, u32[]{:S(2)}, u32[]{:S(2)}) collective-permute-start(bf16[128,2048]{1,0:T(8,128)(2,1)S(1)} %add_share.16), channel_id=1, source_target_pairs={{0,8},{2,10},{4,12},{6,14},{8,16},{9,1},{10,18},{11,3},{12,20},{13... | collective-permute-start | bytes 1572872 | tf_op jit(solution)/shard_map/ppermute | solution.py:50
  68.9 7.3 %collective-permute-start.23 = (bf16[4,64,512]{2,1,0:T(8,128)(2,1)S(1)}, bf16[4,64,512]{2,1,0:T(8,128)(2,1)S(1)}, u32[]{:S(2)}, u32[]{:S(2)}) collective-permute-start(bf16[4,64,512]{2,1,0:T(8,128)(2,1)S(1)} %pad_maximum_fusion.2), channel_id=1, source_target_pairs={{0,1},{1,0},{2,3},{3,2},{4,5},{5,4},{6,7},{7,6},{8,9},{9,8},{10,11... | collective-permute-start | bytes 786440 | tf_op jit(solution)/shard_map/ppermute | solution.py:184
  69.1 26.6 %collective-permute-start.24 = (bf16[128,2048]{1,0:T(8,128)(2,1)S(1)}, bf16[128,2048]{1,0:T(8,128)(2,1)S(1)}, u32[]{:S(2)}, u32[]{:S(2)}) collective-permute-start(bf16[128,2048]{1,0:T(8,128)(2,1)S(1)} %add_share.19), channel_id=1, source_target_pairs={{1,9},{3,11},{5,13},{7,15},{8,0},{9,17},{10,2},{11,19},{12,4},{13,... | collective-permute-start | bytes 1572872 | tf_op jit(solution)/shard_map/ppermute | solution.py:50
  70.4 20.2 %collective-permute-start.25 = (bf16[128,2048]{1,0:T(8,128)(2,1)S(1)}, bf16[128,2048]{1,0:T(8,128)(2,1)S(1)}, u32[]{:S(2)}, u32[]{:S(2)}) collective-permute-start(bf16[128,2048]{1,0:T(8,128)(2,1)S(1)} %add_share.18), channel_id=1, source_target_pairs={{0,8},{2,10},{4,12},{6,14},{8,16},{9,1},{10,18},{11,3},{12,20},{13... | collective-permute-start | bytes 1572872 | tf_op jit(solution)/shard_map/ppermute | solution.py:50
  80.0 26.1 %collective-permute-start.30 = (bf16[128,2048]{1,0:T(8,128)(2,1)S(1)}, bf16[128,2048]{1,0:T(8,128)(2,1)S(1)}, u32[]{:S(2)}, u32[]{:S(2)}) collective-permute-start(bf16[128,2048]{1,0:T(8,128)(2,1)S(1)} %add_share.20), channel_id=1, source_target_pairs={{0,8},{2,10},{4,12},{6,14},{8,16},{9,1},{10,18},{11,3},{12,20},{13... | collective-permute-start | bytes 1572872 | tf_op jit(solution)/shard_map/ppermute | solution.py:50
  84.5 21.6 %collective-permute-start.31 = (bf16[128,2048]{1,0:T(8,128)(2,1)S(1)}, bf16[128,2048]{1,0:T(8,128)(2,1)S(1)}, u32[]{:S(2)}, u32[]{:S(2)}) collective-permute-start(bf16[128,2048]{1,0:T(8,128)(2,1)S(1)} %add_share.21), channel_id=1, source_target_pairs={{1,9},{3,11},{5,13},{7,15},{8,0},{9,17},{10,2},{11,19},{12,4},{13,... | collective-permute-start | bytes 1572872 | tf_op jit(solution)/shard_map/ppermute | solution.py:50
  91.3 20.3 %collective-permute-start.28 = (bf16[128,2048]{1,0:T(8,128)(2,1)S(1)}, bf16[128,2048]{1,0:T(8,128)(2,1)S(1)}, u32[]{:S(2)}, u32[]{:S(2)}) collective-permute-start(bf16[128,2048]{1,0:T(8,128)(2,1)S(1)} %add_share.22), channel_id=1, source_target_pairs={{0,8},{2,10},{4,12},{6,14},{8,16},{9,1},{10,18},{11,3},{12,20},{13... | collective-permute-start | bytes 1572872 | tf_op jit(solution)/shard_map/ppermute | solution.py:50
  95.9 14.6 %collective-permute-start.29 = (bf16[128,2048]{1,0:T(8,128)(2,1)S(1)}, bf16[128,2048]{1,0:T(8,128)(2,1)S(1)}, u32[]{:S(2)}, u32[]{:S(2)}) collective-permute-start(bf16[128,2048]{1,0:T(8,128)(2,1)S(1)} %add_share.23), channel_id=1, source_target_pairs={{1,9},{3,11},{5,13},{7,15},{8,0},{9,17},{10,2},{11,19},{12,4},{13,... | collective-permute-start | bytes 1572872 | tf_op jit(solution)/shard_map/ppermute | solution.py:50
  (11 other events, 77.1 us)
